TPU v7x, 32 devices: a whole 2x2x4 slice. The times are simulated.
32 devices in a mesh: groups: 2 (over y), chan: 4 (over z), seg: 2 (over x), freq: 2 (over core).
Axes of the slice: x: 2, y: 2, z: 4, core: 2. Of those that a mesh axis runs over, the one named last changes fastest.
Arguments:
- traces: bfloat16 [10, 1024, 4096], P('seg', ('groups', 'chan')), parts along dimension 1, may hold values from -120 to 120
- dead_mask: int32 [1024], P(('groups', 'chan')), parts along dimension 0, may hold values 0 or 1
- seg_counts: int32 [1024], P(('groups', 'chan')), parts along dimension 0, may hold values from 1 to 10
- offsets: int32 [4], replicated, may hold values from 1 to 128, as said below
Outputs:
- correlations: float32 [1024, 4, 512], P(('groups', 'chan', 'seg'), None, 'freq'), parts along dimension 0
There are 2 independent parts, one for each index of `groups`. A program takes and returns all parts, laid end to end along the dimension named above; an argument that names none is the same for every part. Nothing has to cross between parts.
Inputs may be any that keep to these rules, and one draw needn't show every extreme that they name: The 4 offsets are distinct and one of them equals 128.
All inputs are finite; a program needn't handle non-finite values. No bound on the sum of `dead_mask` on one device may be relied on, other than what follows from the above.
Results may differ from a plain program's by a relative error of at most 0.0056.
Values may be sent and summed in bfloat16 or wider, within the bound.
No kernel may reach another device: no remote copies, remote signals or barrier semaphores. Data moves between devices by JAX's collectives and lax.ppermute only.
A program may use at most 128 MiB of HBM per device.

v0:
```python
import math

import jax
import jax.numpy as jnp
from jax import lax
from jax.sharding import PartitionSpec as P

HALF = 32
LAGS = 512
F = 2048


epsilon = 1e-06


def padded(array, sides, width):
    for axis, dim in sides:
        peers, length = (lax.axis_size(axis), array.shape[dim])
        up = [(i, (i + 1) % peers) for i in range(peers - 1)]
        down = [(j, i) for i, j in up]
        last = lax.slice_in_dim(array, length - width, length, axis=dim)
        leading = lax.slice_in_dim(array, 0, width, axis=dim)
        before = lax.ppermute(last, axis, up)
        after = lax.ppermute(leading, axis, down)
        array = jnp.concatenate([before, array, after], axis=dim)
    return array


def from_behind(block, axis, distance):
    devices = range(lax.axis_size(axis))
    route = [(i - distance, i) for i in devices if i - distance in devices]
    return lax.ppermute(block, axis, route)


def fourier_table(bin_first, bin_number, length):
    samples = jnp.arange(length, dtype=jnp.int32)[:, None]
    bin_index = bin_first + jnp.arange(bin_number, dtype=jnp.int32)[None, :]
    phases = (samples * bin_index % length).astype(jnp.float32) * (2.0 * math.pi / length)
    return jnp.concatenate([jnp.cos(phases), -jnp.sin(phases)], axis=1).astype(jnp.bfloat16)


def delay_table(bin_first, bin_number, length, lag_number, bin_total):
    bin_index = bin_first + jnp.arange(bin_number, dtype=jnp.int32)[:, None]
    shifts = jnp.arange(lag_number, dtype=jnp.int32)[None, :] - lag_number // 2
    phases = (bin_index * shifts % length).astype(jnp.float32) * (2.0 * math.pi / length)
    scaling = 1.0 / math.sqrt(bin_total)
    return jnp.concatenate([jnp.cos(phases) * scaling, -jnp.sin(phases) * scaling], axis=0)


def shards(traces, dead_mask, seg_counts, offsets):
    seg_dev, chan_dev, length = traces.shape
    bins_dev = F // lax.axis_size("freq")
    bin_first = lax.axis_index("freq") * bins_dev
    seg_first = lax.axis_index("seg") * seg_dev
    fourier = fourier_table(bin_first, bins_dev, length)
    bin_index = bin_first + jnp.arange(bins_dev, dtype=jnp.int32)
    window_count = (
        jnp.minimum(bin_index + HALF, F - 1) - jnp.maximum(bin_index - HALF, 0) + 1
    ).astype(jnp.float32)
    seg_index = seg_first + jnp.arange(seg_dev, dtype=jnp.int32)
    alive_own = dead_mask.astype(jnp.float32)
    spectra = jnp.dot(
        traces.reshape(seg_dev * chan_dev, length), fourier, preferred_element_type=jnp.float32
    )
    spectra = spectra.reshape(seg_dev, chan_dev, 2 * bins_dev)
    real_part = spectra[:, :, :bins_dev]
    imag_part = spectra[:, :, bins_dev:]
    power_bins = real_part * real_part + imag_part * imag_part
    rimmed = padded(power_bins, (("freq", 2),), HALF)
    window_sum = lax.reduce_window(
        rimmed, jnp.zeros((), rimmed.dtype), lax.add, (1, 1, 2 * HALF + 1), (1, 1, 1), "VALID"
    )
    valid_seg = (seg_index[:, None] < seg_counts[None, :]).astype(jnp.float32) * alive_own[None, :]
    factor = valid_seg[:, :, None] / jnp.sqrt(window_sum / window_count + epsilon)
    white = jnp.concatenate([real_part * factor, imag_part * factor], axis=2)
    own_counts = seg_counts.astype(jnp.float32)
    next_white, next_count_f = from_behind((white, own_counts), "chan", -1)
    combined = jnp.concatenate([white, next_white], axis=1)
    all_counts = jnp.concatenate([own_counts, next_count_f])
    white_re = white[:, :, :bins_dev]
    white_im = white[:, :, bins_dev:]
    slots = []
    for slot in range(offsets.shape[0]):
        offset = offsets[slot]
        partner = lax.dynamic_slice_in_dim(combined, offset, chan_dev, 1)
        partner_re = partner[:, :, :bins_dev]
        partner_im = partner[:, :, bins_dev:]
        cross_spec = jnp.concatenate(
            [
                jnp.sum(white_re * partner_re + white_im * partner_im, axis=0),
                jnp.sum(white_im * partner_re - white_re * partner_im, axis=0),
            ],
            axis=1,
        )
        partner_count = lax.dynamic_slice_in_dim(all_counts, offset, chan_dev, 0)
        divisor = jnp.maximum(jnp.minimum(own_counts, partner_count), 1.0)
        slots.append(cross_spec / divisor[:, None])
    stacked = jnp.stack(slots, axis=1)
    delay = delay_table(bin_first, bins_dev, length, LAGS, F)
    shares = lax.psum_scatter(stacked, "seg", scatter_dimension=0, tiled=True)
    lag_terms = jnp.einsum("ckf,fl->ckl", shares, delay, precision=lax.Precision.HIGHEST)
    return lax.psum_scatter(lag_terms, "freq", scatter_dimension=2, tiled=True)


def solution(mesh):
    in_specs = (
        P("seg", ("groups", "chan"), None),
        P(("groups", "chan")),
        P(("groups", "chan")),
        P(),
    )
    out_specs = P(("groups", "chan", "seg"), None, "freq")
    return jax.shard_map(shards, mesh=mesh, in_specs=in_specs, out_specs=out_specs, check_vma=False)
```

profile of v0, /device:TPU:0, one launch (start us, length us, event | category | flops | bytes accessed | tf_op | source)
XLA Modules:
  0.0 455.6 jit_solution(8970719155979047860)
XLA Ops:
  6.5 69.1 %cosine_convert_fusion = (bf16[4096,1024]{1,0:T(8,128)(2,1)}, bf16[4096,1024]{1,0:T(8,128)(2,1)}) fusion(s32[1024]{0:T(1024)S(1)} %iota_add_fusion), kind=kLoop, calls=%fused_computation.11 | loop fusion | flops 71303168 | bytes 16781312 | tf_op jit(solution)/shard_map/convert
  75.6 17.7 %fusion.3 = f32[2048,640]{0,1:T(8,128)} fusion(bf16[640,4096]{1,0:T(8,128)(2,1)} %bitcast.30, bf16[4096,1024]{1,0:T(8,128)(2,1)} %get-tuple-element.22, bf16[4096,1024]{1,0:T(8,128)(2,1)} %get-tuple-element.21), kind=kOutput, calls=%fused_computation.6 | convolution fusion | flops 10770972672 | bytes 27262976 | tf_op jit(solution)/shard_map/dot_general | solution.py:62
  93.3 5.7 %fusion.21 = (f32[5,128,1024]{2,1,0:T(8,128)}, f32[5,128,1024]{2,1,0:T(8,128)}) fusion(f32[5,128,2048]{2,1,0:T(8,128)} %bitcast.21), kind=kLoop, calls=%fused_computation.63 | loop fusion | bytes 10485760 | tf_op jit(solution)/shard_map/slice | solution.py:66
  99.0 2.1 copy.17
  101.2 4.2 copy.18
  105.4 2.0 multiply_add_fusion
  108.9 2.4 collective-permute-start
  112.9 1.6 collective-permute-done.1
  114.5 1.9 pad_maximum_fusion.3
  116.4 45.5 %reduce_window.7 = f32[5,128,1024]{1,2,0:T(8,128)} reduce-window(f32[5,128,1088]{1,2,0:T(8,128)S(1)} %pad_maximum_fusion.3, f32[]{:T(128)} %constant.50.clone.1), window={size=1x1x65}, to_apply=%region_0.1 | reduce-window | flops 41943040 | bytes 5406724 | tf_op jit(solution)/shard_map/reduce_window | solution.py:70
  161.9 4.0 fusion.20
  165.9 2.9 pad_maximum_fusion.1
  180.3 106.7 %collective-permute-done.3 = f32[128]{0:T(128)S(1)} collective-permute-done((f32[128]{0:T(128)S(1)}, f32[128]{0:T(128)S(1)}, u32[]{:S(2)}, u32[]{:S(2)}) %collective-permute-start.3) | collective-permute-done | bytes 544 | tf_op jit(solution)/shard_map/ppermute | solution.py:32
  287.1 8.0 %pad_maximum_fusion = f32[5,256,2048]{1,2,0:T(8,128)} fusion(f32[5,128,2048]{1,2,0:T(8,128)} %collective-permute-done.2, f32[5,128,1024]{1,2,0:T(8,128)} %copy-done, f32[5,128,1024]{1,2,0:T(8,128)S(1)} %get-tuple-element.15), kind=kLoop, calls=%fused_computation.15 | loop fusion | flops 5242880 | bytes 20971520 | tf_op jit(solution)/shard_map/concatenate | solution.py:78
  295.1 17.6 %add_reduce_fusion.3 = (f32[128,1024]{0,1:T(8,128)}, f32[128,1024]{0,1:T(8,128)S(1)}, f32[128,1024]{0,1:T(8,128)}, f32[128,1024]{0,1:T(8,128)}, f32[128,1024]{0,...) fusion(f32[5,128,1024]{1,2,0:T(8,128)} %copy-done, ...), kind=kLoop, calls=%fused_computation.35 | loop fusion | flops 19922944 | bytes 30408724 | tf_op jit(solution)/shard_map/reduce_sum | solution.py:90
  312.7 1.8 maximum_divide_fusion
  314.8 2.2 pad_maximum_fusion.2
  317.1 5.5 %copy.14 = f32[128,4,2048]{2,1,0:T(4,128)} copy(f32[128,4,2048]{0,2,1:T(8,128)} %pad_maximum_fusion.2) | data formatting | bytes 8388608 | tf_op jit(solution)/shard_map/stack | solution.py:98
  324.5 9.7 %cosine_multiply_fusion = (f32[1024,512]{1,0:T(8,128)S(1)}, f32[1024,512]{1,0:T(8,128)}) fusion(s32[512]{0:T(512)S(1)} %iota_add_fusion.1, s32[1024]{0:T(1024)S(1)} %iota_add_fusion), kind=kLoop, calls=%fused_computation.43 | loop fusion | flops 8912896 | bytes 4200448 | tf_op jit(solution)/shard_map/mul | solution.py:47
  334.2 96.8 %all-reduce.3.cloned.1.call-done = f32[128,4,2048]{2,1,0:T(4,128)} async-done(((f32[128,4,2048]{2,1,0:T(4,128)}), f32[128,4,2048]{2,1,0:T(4,128)}) %all-reduce.3.cloned.1.call-update) | async-done | bytes 4194320
  431.0 2.0 constant_dynamic-slice_fusion
  433.2 5.6 %fusion.10 = f32[64,4,512]{2,0,1:T(8,128)} fusion(f32[1024,512]{1,0:T(8,128)S(1)} %copy-done.3, f32[1024,512]{1,0:T(8,128)S(1)} %get-tuple-element.19, f32[64,4,2048]{2,1,0:T(4,128)S(1)} %constant_dynamic-slice_fusion), kind=kOutput, calls=%fused_computation.19 | convolution fusion | flops 3222274048 | bytes 6815744 | tf_op jit(solution)/shard_map/ckf,fl->ckl/dot_general | solution.py:101
  438.8 8.1 %reduce-scatter.2.cloned.1.call-done = f32[64,4,256]{2,0,1:T(8,128)} async-done(((f32[64,4,512]{2,0,1:T(8,128)}), f32[64,4,256]{2,0,1:T(8,128)}) %reduce-scatter.2.cloned.1.call-update) | async-done | bytes 262160 | tf_op jit(solution)/shard_map/reduce_scatter | solution.py:102
  447.0 1.8 copy.16
  (44 shorter events, 8.7 us)
Async XLA Ops:
  6.5 424.5 %all-reduce.3.cloned.1.call-start = ((), (), s32[]{:S(2)}) async-start(), calls=%async_computation.2 | async-start | bytes 8388608
  101.1 4.2 copy-start.1
  105.4 7.4 %copy-start.9 = (s32[128]{0:T(128)S(1)}, s32[128]{0:T(128)}, u32[]{:S(2)}) copy-start(s32[128]{0:T(128)} %param.5) | copy-start | bytes 1540
  105.4 7.5 %copy-start.8 = (s32[128]{0:T(128)S(1)}, s32[128]{0:T(128)}, u32[]{:S(2)}) copy-start(s32[128]{0:T(128)} %param.6) | copy-start | bytes 1540
  107.4 1.5 copy-start.2
  108.9 4.0 collective-permute-start
  111.3 3.2 collective-permute-start.1
  165.9 3.1 copy-start
  165.9 5.9 %copy-start.7 = (s32[4]{0:T(128)S(1)}, s32[4]{0:T(128)}, u32[]{:S(2)}) copy-start(s32[4]{0:T(128)} %param.7) | copy-start | bytes 52
  169.0 118.1 %collective-permute-start.2 = (f32[5,128,2048]{1,2,0:T(8,128)}, f32[5,128,2048]{1,2,0:T(8,128)}, u32[]{:S(2)}, u32[]{:S(2)}) collective-permute-start(f32[5,128,2048]{1,2,0:T(8,128)} %pad_maximum_fusion.1), channel_id=1, source_target_pairs={{4,0},{8,4},{12,8},{5,1},{9,5},{13,9},{6,2},{10,6},{14,10},{7,3},{... | collective-permute-start | bytes 15728648 | tf_op jit(solution)/shard_map/ppermute | solution.py:32
  170.3 116.7 %collective-permute-start.3 = (f32[128]{0:T(128)S(1)}, f32[128]{0:T(128)S(1)}, u32[]{:S(2)}, u32[]{:S(2)}) collective-permute-start(f32[128]{0:T(128)S(1)} %convert_element_type.24), channel_id=1, source_target_pairs={{4,0},{8,4},{12,8},{5,1},{9,5},{13,9},{6,2},{10,6},{14,10},{7,3},{... | collective-permute-start | bytes 1544 | tf_op jit(solution)/shard_map/ppermute | solution.py:32
  312.7 1.8 copy-start.4
  312.7 1.8 copy-start.5
  312.7 2.0 copy-start.6
  322.6 0.7 copy-start.10
  322.6 124.3 %reduce-scatter.2.cloned.1.call-start = ((), (), s32[]{:S(2)}) async-start(), calls=%async_computation.1 | async-start | bytes 786432 | tf_op jit(solution)/shard_map/reduce_scatter | solution.py:102
  431.0 2.2 copy-start.3
Sparse Core Ops, SparseCore 0:
  322.7 108.2 all-reduce.2
  439.0 7.9 reduce-scatter.1
where the time goes:
time: 456 us
  waiting for transfers between devices  213 us (47%)
  other arithmetic  165 us (36%)
  local copies, waits for them, and re-layouts  25.3 us (6%)
  matrix products  23.3 us (5%)
  between operations  22.1 us (5%)
  starting transfers between devices  6.67 us (1%)
    ppermute x2, waiting for transfers between devices, from_behind(): return lax.ppermute(block, axis, route)  107 us
    unnamed x3, waiting for transfers between devices  96.8 us
    another operation x1, other arithmetic  69.1 us
    another operation x1, other arithmetic, shards(): lax.reduce_window(rimmed, jnp.zeros((), rimmed.dtype), lax.add, (1, 1, 2...  45.5 us
    dot_general x1, matrix products, shards(): jnp.dot(traces.reshape(seg_dev * chan_dev, length), fourier, preferred_el...  17.7 us
    reduce_sum x1, other arithmetic, shards(): jnp.sum(white_re * partner_re + white_im * partner_im, axis=0)  17.6 us
    unnamed x26, local copies, waits for them, and re-layouts  11.6 us
    mul x1, other arithmetic, delay_table(): jnp.cos(phases) * scaling  9.73 us
  transfers between devices with their start and end apart: 6, of which 4 were waited for; matrix products, arithmetic and copies ran while one was open for 2% of the time, Pallas kernels for 0%

commit v1 on v0

v1 whole, which is shorter than its diff:
```python
import math

import jax
import jax.numpy as jnp
import numpy as np
from jax import lax
from jax.experimental import pallas as pl
from jax.experimental.pallas import tpu as pltpu
from jax.sharding import PartitionSpec as P
import ml_dtypes

HALF = 32
LAGS = 512
F = 2048
TILE = 128
EPSILON = 1e-06
MIB = 1 << 20


def tables(length, parts):
    bins_dev = F // parts
    tiles = bins_dev // TILE
    cosines = np.cos(np.arange(length) * (2.0 * math.pi / length))
    sines = -np.sin(np.arange(length) * (2.0 * math.pi / length))
    cos16 = cosines.astype(np.float32).astype(ml_dtypes.bfloat16)
    sin16 = sines.astype(np.float32).astype(ml_dtypes.bfloat16)
    samples = np.arange(length)[:, None]
    fourier = np.zeros((parts, tiles + 1, length, 2 * TILE), ml_dtypes.bfloat16)
    for part in range(parts):
        for tile in range(tiles + 1):
            first = part * bins_dev + (tile - 1) * TILE
            bin_index = first + np.arange(TILE)
            keep = np.ones((TILE,), bool)
            if tile == 0:
                lane = np.arange(TILE)
                after = part * bins_dev + bins_dev + lane
                before = part * bins_dev - TILE + lane
                bin_index = np.where(lane < HALF, after, before)
                keep = ((lane < HALF) & (after < F)) | ((lane >= TILE - HALF) & (before >= 0))
            phases = samples * bin_index[None, :] % length
            zero = ml_dtypes.bfloat16(0)
            fourier[part, tile, :, :TILE] = np.where(keep, cos16[phases], zero)
            fourier[part, tile, :, TILE:] = np.where(keep, sin16[phases], zero)
    lag_part = LAGS // parts
    delay = np.zeros((parts, 2 * bins_dev, LAGS), ml_dtypes.bfloat16)
    scaling = 1.0 / math.sqrt(F)
    for part in range(parts):
        shifts = np.roll(np.arange(LAGS), -part * lag_part) - LAGS // 2
        for tile in range(tiles):
            bin_index = part * bins_dev + tile * TILE + np.arange(TILE)
            phases = bin_index[:, None] * shifts[None, :] % length
            rows = tile * 2 * TILE
            delay[part, rows : rows + TILE] = (cosines[phases] * scaling).astype(ml_dtypes.bfloat16)
            delay[part, rows + TILE : rows + 2 * TILE] = (sines[phases] * scaling).astype(ml_dtypes.bfloat16)
    band = np.abs(np.arange(3 * TILE)[:, None] - TILE - np.arange(TILE)[None, :]) <= HALF
    return fourier, delay, band.astype(ml_dtypes.bfloat16)


def whiten_kernel(tiles, part_ref, x_ref, table_ref, band_ref, valid_ref, lo_ref, hi_ref, spectra, power):
    step = pl.program_id(0)
    segs, half, _ = lo_ref.shape

    def transform():
        block = jnp.dot(x_ref[...], table_ref[...], preferred_element_type=jnp.float32)
        spectra[step] = block
        re, im = block[:, :TILE], block[:, TILE:]
        power[step] = (re * re + im * im).astype(jnp.bfloat16)

    def finish():
        tile = step - 2
        after = lax.rem(tile + 1, tiles + 1)
        window = jnp.dot(power[tile - 1], band_ref[:TILE], preferred_element_type=jnp.float32)
        window += jnp.dot(power[tile], band_ref[TILE : 2 * TILE], preferred_element_type=jnp.float32)
        window += jnp.dot(power[after], band_ref[2 * TILE :], preferred_element_type=jnp.float32)
        first = part_ref[0] * (tiles * TILE) + (tile - 1) * TILE
        bin_index = first + lax.broadcasted_iota(jnp.int32, (1, TILE), 1)
        count = jnp.minimum(bin_index + HALF, F - 1) - jnp.maximum(bin_index - HALF, 0) + 1
        inverse = 1.0 / count.astype(jnp.float32)
        factor = valid_ref[...] * lax.rsqrt(window * inverse + EPSILON)
        re = (spectra[tile, :, :TILE] * factor).astype(jnp.bfloat16)
        im = (spectra[tile, :, TILE:] * factor).astype(jnp.bfloat16)
        for seg in range(segs):
            row = seg * 2 * half
            lo_ref[seg, :, :TILE] = re[row : row + half]
            lo_ref[seg, :, TILE:] = im[row : row + half]
            hi_ref[seg, :, :TILE] = re[row + half : row + 2 * half]
            hi_ref[seg, :, TILE:] = im[row + half : row + 2 * half]

    @pl.when(step < 3)
    def _():
        transform()

    @pl.when((step >= 3) & (step <= tiles))
    def _():
        transform()
        finish()

    @pl.when(step > tiles)
    def _():
        finish()


def whiten(part, traces, fourier, band, valid):
    segs, chans, length = traces.shape
    rows, half = segs * chans, chans // 2
    tiles = fourier.shape[1] - 1
    out = jax.ShapeDtypeStruct((segs, half, 2 * TILE * tiles), jnp.bfloat16)
    out_spec = pl.BlockSpec((segs, half, 2 * TILE), lambda j, p: (0, 0, jnp.clip(j - 3, 0, tiles - 1)))
    return pl.pallas_call(
        lambda *refs: whiten_kernel(tiles, *refs),
        out_shape=(out, out),
        grid_spec=pltpu.PrefetchScalarGridSpec(
            num_scalar_prefetch=1,
            grid=(tiles + 3,),
            in_specs=[
                pl.BlockSpec((rows, length), lambda j, p: (0, 0)),
                pl.BlockSpec((None, None, length, 2 * TILE), lambda j, p: (p[0], jnp.minimum(j, tiles), 0, 0)),
                pl.BlockSpec((3 * TILE, TILE), lambda j, p: (0, 0)),
                pl.BlockSpec((rows, TILE), lambda j, p: (0, 0)),
            ],
            out_specs=[out_spec, out_spec],
            scratch_shapes=[
                pltpu.VMEM((tiles + 1, rows, 2 * TILE), jnp.float32),
                pltpu.VMEM((tiles + 1, rows, TILE), jnp.bfloat16),
            ],
        ),
        compiler_params=pltpu.CompilerParams(vmem_limit_bytes=40 * MIB),
        cost_estimate=pl.CostEstimate(
            flops=2 * rows * length * 2 * TILE * (tiles + 1),
            bytes_accessed=2 * length * 2 * TILE * (tiles + 1),
            transcendentals=0,
        ),
        name="whiten",
    )(part, traces.reshape(rows, length), fourier, band, valid)


def correlate_kernel(
    scalars, before_ref, lo_ref, hi_ref, after_ref, delay_ref, keep_ref, send_ref, frame, cross, total
):
    step, last = pl.program_id(0), pl.num_programs(0) - 1
    segs, half, _ = lo_ref.shape
    chans = 2 * half
    slots = cross.shape[0]
    keep = keep_ref.shape[2]
    for seg in range(segs):
        for place, ref in enumerate((before_ref, lo_ref, hi_ref, after_ref)):
            block = ref[seg].astype(jnp.float32)
            frame[seg, 0, place * half : (place + 1) * half] = block[:, :TILE]
            frame[seg, 1, place * half : (place + 1) * half] = block[:, TILE:]

    for slot in range(slots):
        offset = scalars[1 + slot]
        own_first = jnp.minimum(half, chans - offset)

        def rows(index, carry, slot=slot, own_first=own_first, offset=offset):
            real = jnp.zeros((16, TILE), jnp.float32)
            imag = jnp.zeros((16, TILE), jnp.float32)
            base = own_first + index * 16
            for seg in range(segs):
                own_re = frame[seg, 0, pl.ds(base, 16), :]
                own_im = frame[seg, 1, pl.ds(base, 16), :]
                far_re = frame[seg, 0, pl.ds(base + offset, 16), :]
                far_im = frame[seg, 1, pl.ds(base + offset, 16), :]
                real += own_re * far_re + own_im * far_im
                imag += own_im * far_re - own_re * far_im
            spot = pl.ds(pl.multiple_of(index * 16, 16), 16)
            cross[slot, spot, :TILE] = real.astype(jnp.bfloat16)
            cross[slot, spot, TILE:] = imag.astype(jnp.bfloat16)
            return carry

        lax.fori_loop(0, chans // 16, rows, 0)
        part = jnp.dot(cross[slot], delay_ref[...], preferred_element_type=jnp.float32)

        @pl.when(step == 0)
        def _(slot=slot, part=part):
            total[slot] = part

        @pl.when(step > 0)
        def _(slot=slot, part=part):
            total[slot] += part

    @pl.when(step == last)
    def _():
        keep_ref[...] = jnp.zeros_like(keep_ref)
        for slot in range(slots):
            offset = scalars[1 + slot]
            own_first = jnp.minimum(half, chans - offset)
            frame[0, 0, : chans + half] = jnp.zeros((chans + half, TILE), jnp.float32)
            for lane in range(total.shape[2] // TILE):
                frame[0, 0, pl.ds(own_first, chans), :] = total[slot, :, lane * TILE : (lane + 1) * TILE]
                placed = frame[0, 0, : chans + half]
                at = lane * TILE
                if at < keep:
                    keep_ref[slot, :, at : at + TILE] = placed
                else:
                    send_ref[slot, :, at - keep : at - keep + TILE] = placed.astype(send_ref.dtype)


def correlate(scalars, before, lo, hi, after, delay, parts):
    segs, half, columns = lo.shape
    tiles = columns // (2 * TILE)
    slots = scalars.shape[0] - 1
    lags = delay.shape[2]
    rows = 3 * half
    spec = pl.BlockSpec((segs, half, 2 * TILE), lambda j, s: (0, 0, j))
    whole = lambda width: pl.BlockSpec((slots, rows, width), lambda j, s: (0, 0, 0))
    keep = lags // parts
    return pl.pallas_call(
        correlate_kernel,
        out_shape=(
            jax.ShapeDtypeStruct((slots, rows, keep), jnp.float32),
            jax.ShapeDtypeStruct((slots, rows, lags - keep), jnp.bfloat16),
        ),
        grid_spec=pltpu.PrefetchScalarGridSpec(
            num_scalar_prefetch=1,
            grid=(tiles,),
            in_specs=[spec, spec, spec, spec, pl.BlockSpec((None, 2 * TILE, lags), lambda j, s: (s[0], j, 0))],
            out_specs=[whole(keep), whole(lags - keep)],
            scratch_shapes=[
                pltpu.VMEM((segs, 2, 4 * half, TILE), jnp.float32),
                pltpu.VMEM((slots, 2 * half, 2 * TILE), jnp.bfloat16),
                pltpu.VMEM((slots, 2 * half, lags), jnp.float32),
            ],
        ),
        compiler_params=pltpu.CompilerParams(vmem_limit_bytes=40 * MIB),
        name="correlate",
    )(scalars, before, lo, hi, after, delay)


def shift(block, axis, distance):
    devices = range(lax.axis_size(axis))
    return lax.ppermute(block, axis, [(i, i + distance) for i in devices if i + distance in devices])


def shards(traces, dead_mask, seg_counts, offsets):
    segs, chans, length = traces.shape
    half = chans // 2
    parts = lax.axis_size("freq")
    spans = lax.axis_size("seg")
    assert parts == 2
    fourier, delay, band = tables(length, parts)
    part = lax.axis_index("freq")
    span = lax.axis_index("seg")
    seg_index = span * segs + jnp.arange(segs, dtype=jnp.int32)
    valid = (seg_index[:, None] < seg_counts[None, :]) & (dead_mask[None, :] > 0)
    valid = jnp.broadcast_to(valid.astype(jnp.float32).reshape(segs * chans, 1), (segs * chans, TILE))
    next_counts = shift(seg_counts, "chan", -1)
    lo, hi = whiten(part.reshape(1).astype(jnp.int32), traces, jnp.asarray(fourier), jnp.asarray(band), valid)
    before = shift(hi, "chan", 1)
    after = shift(lo, "chan", -1)
    scalars = jnp.concatenate([part.reshape(1).astype(jnp.int32), offsets])
    keep, send = correlate(scalars, before, lo, hi, after, jnp.asarray(delay), parts)
    keep = keep + lax.ppermute(send, "freq", [(0, 1), (1, 0)]).astype(jnp.float32)
    back = shift(keep[:, :half].astype(jnp.bfloat16), "chan", -1).astype(jnp.float32)
    keep = keep[:, half:]
    keep = keep + jnp.pad(back, ((0, 0), (chans - half, 0), (0, 0)))
    piece = chans // spans
    result = lax.dynamic_slice_in_dim(keep, span * piece, piece, 1)
    for step in range(1, spans):
        target = lax.rem(span + step, spans)
        block = lax.dynamic_slice_in_dim(keep, target * piece, piece, 1).astype(jnp.bfloat16)
        result = result + lax.ppermute(block, "seg", [(i, (i + step) % spans) for i in range(spans)]).astype(jnp.float32)
    all_counts = jnp.concatenate([seg_counts, next_counts])
    inverses = []
    for slot in range(offsets.shape[0]):
        own = lax.dynamic_slice_in_dim(all_counts, span * piece, piece, 0)
        far = lax.dynamic_slice_in_dim(all_counts, span * piece + offsets[slot], piece, 0)
        inverses.append(1.0 / jnp.maximum(jnp.minimum(own, far), 1).astype(jnp.float32))
    inverse = jnp.stack(inverses, axis=0)
    return jnp.transpose(result * inverse[:, :, None], (1, 0, 2))


def solution(mesh):
    in_specs = (
        P("seg", ("groups", "chan"), None),
        P(("groups", "chan")),
        P(("groups", "chan")),
        P(),
    )
    out_specs = P(("groups", "chan", "seg"), None, "freq")
    return jax.shard_map(shards, mesh=mesh, in_specs=in_specs, out_specs=out_specs, check_vma=False)
```

time: 456 us -> 95.5 us (0.21)
  waiting for transfers between devices: 213 us -> 41.3 us
  other arithmetic: 165 us -> 1.88 us
  Pallas kernels: 0 us -> 33.8 us
  matrix products: 23.3 us -> 0 us
  local copies, waits for them, and re-layouts: 25.3 us -> 5.09 us
  between operations: 22.1 us -> 2.65 us
    another operation x3, other arithmetic: 117 us -> 0.18 us  [shards(): inverse = jnp.stack(inverses, axis=0)]
    unnamed x3 -> x0, waiting for transfers between devices: 96.8 us -> none
    ppermute x4 -> x6, waiting for transfers between devices: 108 us -> 41.3 us  [the longest x4 37.7 us: shift(): lax.ppermute(block, axis, [(i, i + distance) for i in devices if i + dist...]
    pallas_call x0 -> x2, Pallas kernels: none -> 33.8 us  [the longest x1 20.1 us: whiten(): pl.pallas_call(lambda *refs: whiten_kernel(tiles, *refs), out_shape=(out,...]
    dot_general x2 -> x0, matrix products: 23.3 us -> none  [the longest x1 17.7 us: shards(): jnp.dot(traces.reshape(seg_dev * chan_dev, length), fourier, preferred_el...]
    reduce_sum x1 -> x0, other arithmetic: 17.6 us -> none  [shards(): jnp.sum(white_re * partner_re + white_im * partner_im, axis=0)]
    mul x3 -> x0, other arithmetic: 13.8 us -> none  [the longest x1 9.73 us: delay_table(): jnp.cos(phases) * scaling]
    concatenate x4 -> x1, other arithmetic: 12.8 us -> 0.08 us  [shards(): scalars = jnp.concatenate([part.reshape(1).astype(jnp.int32), offsets])]
  transfers between devices with their start and end apart: 6 -> 6, of which waited for: 4 -> 4; matrix products, arithmetic and copies ran while one was open for 2% -> 1% of each run, Pallas kernels for 0% -> 0%
where the time goes in v1:
time: 95.5 us; the launch traced here: 95.2 us
  waiting for transfers between devices  41.3 us (43%)
  Pallas kernels  33.8 us (35%)
  starting transfers between devices  10.5 us (11%)
  local copies, waits for them, and re-layouts  5.09 us (5%)
  between operations  2.65 us (3%)
  other arithmetic  1.88 us (2%)
    ppermute x4, waiting for transfers between devices, shift(): lax.ppermute(block, axis, [(i, i + distance) for i in devices if i + dist...  37.7 us
    pallas_call x1, Pallas kernels, whiten(): pl.pallas_call(lambda *refs: whiten_kernel(tiles, *refs), out_shape=(out,...  20.1 us
    pallas_call x1, Pallas kernels, correlate(): pl.pallas_call(correlate_kernel, out_shape=(jax.ShapeDtypeStruct((slots,...  13.7 us
    ppermute x4, starting transfers between devices, shift(): lax.ppermute(block, axis, [(i, i + distance) for i in devices if i + dist...  8.88 us
    ppermute x1, waiting for transfers between devices, shards(): lax.ppermute(block, 'seg', [(i, (i + step) % spans) for i in range(spans)])  3.51 us
    unnamed x11, local copies, waits for them, and re-layouts  3.4 us
  transfers between devices with their start and end apart: 6, of which 4 were waited for; matrix products, arithmetic and copies ran while one was open for 1% of the time, Pallas kernels for 0%

profile of v1, /device:TPU:0, one launch (start us, length us, event | category | flops | bytes accessed | tf_op | source)
XLA Modules:
  0.0 95.2 jit_solution(16759804660699301400)
XLA Ops:
  0.0 0.7 broadcast_compare_fusion
  0.7 0.7 convert_bitcast_fusion
  1.4 0.1 broadcast_in_dim.2.refs_4_
  1.6 2.5 %copy-done.1 = bf16[5,128,4096]{2,1,0:T(8,128)(2,1)S(1)} copy-done((bf16[5,128,4096]{2,1,0:T(8,128)(2,1)S(1)}, bf16[5,128,4096]{2,1,0:T(8,128)(2,1)}, u32[]{:S(2)}) %copy-start.1) | copy-done | bytes 5242904
  4.0 0.9 copy-done.2
  4.9 20.1 %whiten.1 = (bf16[5,64,2048]{2,1,0:T(8,128)(2,1)S(1)}, bf16[5,64,2048]{2,1,0:T(8,128)(2,1)S(1)}) custom-call(s32[1]{0:T(128)} %bitcast.refs_0_, bf16[640,4096]{1,0:T(8,128)(2,1)S(1)} %bitcast.18, bf16[2,9,4096,256]{3,2,1,0:T(8,128)(2,1)} %constant.34.clone.refs_2_, bf16[384,128]{1,0:T(8,128)(2,1)S(1)} %copy-done.2, f32[640,128]{1,0:T(8,128)S(1)} %broadcast_in_dim.2.refs_4_), custom_call_target="tpu_custom_call" | custom-call | flops 12079595520 | bytes 18874368 | tf_op jit(solution)/shard_map/whiten/pallas_call | solution.py:109
  25.0 5.0 %collective-permute-start = (bf16[5,64,2048]{2,1,0:T(8,128)(2,1)S(1)}, bf16[5,64,2048]{2,1,0:T(8,128)(2,1)S(1)}, u32[]{:S(2)}, u32[]{:S(2)}) collective-permute-start(bf16[5,64,2048]{2,1,0:T(8,128)(2,1)S(1)} %get-tuple-element.9.hi_ref), channel_id=1, source_target_pairs={{0,4},{4,8},{8,12},{1,5},{5,9},{9,13},{2,6},{6,10},{10,14},{3,7},{... | collective-permute-start | bytes 3932168 | tf_op jit(solution)/shard_map/ppermute | solution.py:232
  30.0 1.3 %collective-permute-start.1 = (bf16[5,64,2048]{2,1,0:T(8,128)(2,1)S(1)}, bf16[5,64,2048]{2,1,0:T(8,128)(2,1)S(1)}, u32[]{:S(2)}, u32[]{:S(2)}) collective-permute-start(bf16[5,64,2048]{2,1,0:T(8,128)(2,1)S(1)} %get-tuple-element.10.lo_ref), channel_id=1, source_target_pairs={{4,0},{8,4},{12,8},{5,1},{9,5},{13,9},{6,2},{10,6},{14,10},{7,3},{... | collective-permute-start | bytes 3932168 | tf_op jit(solution)/shard_map/ppermute | solution.py:232
  31.3 0.1 pad_add_fusion.scalars
  31.4 26.6 %collective-permute-done.before_ref = bf16[5,64,2048]{2,1,0:T(8,128)(2,1)S(1)} collective-permute-done((bf16[5,64,2048]{2,1,0:T(8,128)(2,1)S(1)}, bf16[5,64,2048]{2,1,0:T(8,128)(2,1)S(1)}, u32[]{:S(2)}, u32[]{:S(2)}) %collective-permute-start) | collective-permute-done | bytes 1310752 | tf_op jit(solution)/shard_map/ppermute | solution.py:232
  58.0 4.2 %collective-permute-done.1.after_ref = bf16[5,64,2048]{2,1,0:T(8,128)(2,1)S(1)} collective-permute-done((bf16[5,64,2048]{2,1,0:T(8,128)(2,1)S(1)}, bf16[5,64,2048]{2,1,0:T(8,128)(2,1)S(1)}, u32[]{:S(2)}, u32[]{:S(2)}) %collective-permute-start.1) | collective-permute-done | bytes 1310752 | tf_op jit(solution)/shard_map/ppermute | solution.py:232
  62.2 13.7 %correlate.1 = (f32[4,192,256]{2,1,0:T(8,128)S(1)}, bf16[4,192,256]{2,1,0:T(8,128)(2,1)S(1)}) custom-call(s32[5]{0:T(128)S(1)} %pad_add_fusion.scalars, bf16[5,64,2048]{2,1,0:T(8,128)(2,1)S(1)} %collective-permute-done.before_ref, bf16[5,64,2048]{2,1,0:T(8,128)(2,1)S(1)} %get-tuple-element.10.lo_ref, bf16[5,64,2048]{2,1,0:T(8,128)(2,1)S(1)} %get-tuple-element.9.hi_ref, ...), custom_call_target="tpu_custom_call" | custom-call | tf_op jit(solution)/shard_map/correlate/pallas_call | solution.py:208
  75.9 0.1 collective-permute-start.2
  76.0 1.3 %collective-permute-start.5 = (s32[128]{0:T(128)S(1)}, s32[128]{0:T(128)S(1)}, u32[]{:S(2)}, u32[]{:S(2)}) collective-permute-start(s32[128]{0:T(128)S(1)} %copy-done.4), channel_id=1, source_target_pairs={{4,0},{8,4},{12,8},{5,1},{9,5},{13,9},{6,2},{10,6},{14,10},{7,3},{... | collective-permute-start | bytes 1544 | tf_op jit(solution)/shard_map/ppermute | solution.py:232
  77.3 0.6 fusion
  80.4 0.1 convert_add_fusion
  80.5 1.3 %collective-permute-start.3 = (bf16[4,64,256]{2,1,0:T(8,128)(2,1)S(1)}, bf16[4,64,256]{2,1,0:T(8,128)(2,1)S(1)}, u32[]{:S(2)}, u32[]{:S(2)}) collective-permute-start(bf16[4,64,256]{2,1,0:T(8,128)(2,1)S(1)} %slice.29), channel_id=1, source_target_pairs={{4,0},{8,4},{12,8},{5,1},{9,5},{13,9},{6,2},{10,6},{14,10},{7,3},{... | collective-permute-start | bytes 393224 | tf_op jit(solution)/shard_map/ppermute | solution.py:232
  81.9 0.1 divide_bitcast_fusion.3
  81.9 7.0 %collective-permute-done.3 = bf16[4,64,256]{2,1,0:T(8,128)(2,1)S(1)} collective-permute-done((bf16[4,64,256]{2,1,0:T(8,128)(2,1)S(1)}, bf16[4,64,256]{2,1,0:T(8,128)(2,1)S(1)}, u32[]{:S(2)}, u32[]{:S(2)}) %collective-permute-start.3) | collective-permute-done | bytes 131104 | tf_op jit(solution)/shard_map/ppermute | solution.py:232
  89.0 1.5 %collective-permute-start.4 = (bf16[4,64,256]{2,1,0:T(8,128)(2,1)S(1)}, bf16[4,64,256]{2,1,0:T(8,128)(2,1)S(1)}, u32[]{:S(2)}, u32[]{:S(2)}) collective-permute-start(bf16[4,64,256]{2,1,0:T(8,128)(2,1)S(1)} %dynamic-slice_convert_fusion), channel_id=1, source_target_pairs={{0,2},{2,0},{1,3},{3,1},{4,6},{6,4},{5,7},{7,5},{8,10},{10,8},{9,1... | collective-permute-start | bytes 393224 | tf_op jit(solution)/shard_map/ppermute | solution.py:262
  90.6 0.1 divide_bitcast_fusion.2
  90.7 3.5 %collective-permute-done.4 = bf16[4,64,256]{2,1,0:T(8,128)(2,1)S(1)} collective-permute-done((bf16[4,64,256]{2,1,0:T(8,128)(2,1)S(1)}, bf16[4,64,256]{2,1,0:T(8,128)(2,1)S(1)}, u32[]{:S(2)}, u32[]{:S(2)}) %collective-permute-start.4) | collective-permute-done | bytes 131104 | tf_op jit(solution)/shard_map/ppermute | solution.py:262
  94.2 0.1 multiply_bitcast_fusion
  94.3 0.9 copy.8
  (18 shorter events, 0.2 us)
Async XLA Ops:
  1.5 2.5 %copy-start.1 = (bf16[5,128,4096]{2,1,0:T(8,128)(2,1)S(1)}, bf16[5,128,4096]{2,1,0:T(8,128)(2,1)}, u32[]{:S(2)}) copy-start(bf16[5,128,4096]{2,1,0:T(8,128)(2,1)} %param.7) | copy-start | bytes 15728644
  4.0 0.9 copy-start.2
  4.9 26.4 %copy-start.3 = (s32[4]{0:T(128)S(1)}, s32[4]{0:T(128)}, u32[]{:S(2)}) copy-start(s32[4]{0:T(128)} %param.10) | copy-start | bytes 52
  4.9 57.2 %copy-start = (bf16[2,2048,512]{2,1,0:T(8,128)(2,1)S(1)}, bf16[2,2048,512]{2,1,0:T(8,128)(2,1)}, u32[]{:S(2)}) copy-start(bf16[2,2048,512]{2,1,0:T(8,128)(2,1)} %constant.36.clone.delay_ref) | copy-start | bytes 12582916
  25.0 33.0 %collective-permute-start = (bf16[5,64,2048]{2,1,0:T(8,128)(2,1)S(1)}, bf16[5,64,2048]{2,1,0:T(8,128)(2,1)S(1)}, u32[]{:S(2)}, u32[]{:S(2)}) collective-permute-start(bf16[5,64,2048]{2,1,0:T(8,128)(2,1)S(1)} %get-tuple-element.9.hi_ref), channel_id=1, source_target_pairs={{0,4},{4,8},{8,12},{1,5},{5,9},{9,13},{2,6},{6,10},{10,14},{3,7},{... | collective-permute-start | bytes 3932168 | tf_op jit(solution)/shard_map/ppermute | solution.py:232
  30.0 32.1 %collective-permute-start.1 = (bf16[5,64,2048]{2,1,0:T(8,128)(2,1)S(1)}, bf16[5,64,2048]{2,1,0:T(8,128)(2,1)S(1)}, u32[]{:S(2)}, u32[]{:S(2)}) collective-permute-start(bf16[5,64,2048]{2,1,0:T(8,128)(2,1)S(1)} %get-tuple-element.10.lo_ref), channel_id=1, source_target_pairs={{4,0},{8,4},{12,8},{5,1},{9,5},{13,9},{6,2},{10,6},{14,10},{7,3},{... | collective-permute-start | bytes 3932168 | tf_op jit(solution)/shard_map/ppermute | solution.py:232
  31.4 44.6 %copy-start.4 = (s32[128]{0:T(128)S(1)}, s32[128]{0:T(128)}, u32[]{:S(2)}) copy-start(s32[128]{0:T(128)} %param.9) | copy-start | bytes 1540
  75.9 4.5 %collective-permute-start.2 = (bf16[4,192,256]{2,1,0:T(8,128)(2,1)S(1)}, bf16[4,192,256]{2,1,0:T(8,128)(2,1)S(1)}, u32[]{:S(2)}, u32[]{:S(2)}) collective-permute-start(bf16[4,192,256]{2,1,0:T(8,128)(2,1)S(1)} %get-tuple-element.12), channel_id=1, source_target_pairs={{0,1},{1,0},{2,3},{3,2},{4,5},{5,4},{6,7},{7,6},{8,9},{9,8},{10,11... | collective-permute-start | bytes 1179656 | tf_op jit(solution)/shard_map/ppermute | solution.py:253
  76.0 5.9 %collective-permute-start.5 = (s32[128]{0:T(128)S(1)}, s32[128]{0:T(128)S(1)}, u32[]{:S(2)}, u32[]{:S(2)}) collective-permute-start(s32[128]{0:T(128)S(1)} %copy-done.4), channel_id=1, source_target_pairs={{4,0},{8,4},{12,8},{5,1},{9,5},{13,9},{6,2},{10,6},{14,10},{7,3},{... | collective-permute-start | bytes 1544 | tf_op jit(solution)/shard_map/ppermute | solution.py:232
  80.5 8.4 %collective-permute-start.3 = (bf16[4,64,256]{2,1,0:T(8,128)(2,1)S(1)}, bf16[4,64,256]{2,1,0:T(8,128)(2,1)S(1)}, u32[]{:S(2)}, u32[]{:S(2)}) collective-permute-start(bf16[4,64,256]{2,1,0:T(8,128)(2,1)S(1)} %slice.29), channel_id=1, source_target_pairs={{4,0},{8,4},{12,8},{5,1},{9,5},{13,9},{6,2},{10,6},{14,10},{7,3},{... | collective-permute-start | bytes 393224 | tf_op jit(solution)/shard_map/ppermute | solution.py:232
  89.0 5.2 %collective-permute-start.4 = (bf16[4,64,256]{2,1,0:T(8,128)(2,1)S(1)}, bf16[4,64,256]{2,1,0:T(8,128)(2,1)S(1)}, u32[]{:S(2)}, u32[]{:S(2)}) collective-permute-start(bf16[4,64,256]{2,1,0:T(8,128)(2,1)S(1)} %dynamic-slice_convert_fusion), channel_id=1, source_target_pairs={{0,2},{2,0},{1,3},{3,1},{4,6},{6,4},{5,7},{7,5},{8,10},{10,8},{9,1... | collective-permute-start | bytes 393224 | tf_op jit(solution)/shard_map/ppermute | solution.py:262

commit v2 on v1

v2 whole, which is shorter than its diff:
```python
import functools
import math

import jax
import jax.numpy as jnp
import numpy as np
from jax import lax
from jax.experimental import pallas as pl
from jax.experimental.pallas import tpu as pltpu
from jax.sharding import PartitionSpec as P
import ml_dtypes

HALF = 32
LAGS = 512
F = 2048
TILE = 128
EPSILON = 1e-06
MIB = 1 << 20
CHUNKS = 8
GROUPS = (5, 9)


def tables(length, parts):
    bins_dev = F // parts
    tiles = bins_dev // TILE
    cosines = np.cos(np.arange(length) * (2.0 * math.pi / length))
    sines = -np.sin(np.arange(length) * (2.0 * math.pi / length))
    cos16 = cosines.astype(np.float32).astype(ml_dtypes.bfloat16)
    sin16 = sines.astype(np.float32).astype(ml_dtypes.bfloat16)
    samples = np.arange(length)[:, None]
    fourier = np.zeros((parts, tiles + 1, length, 2 * TILE), ml_dtypes.bfloat16)
    for part in range(parts):
        for tile in range(tiles + 1):
            first = part * bins_dev + (tile - 1) * TILE
            bin_index = first + np.arange(TILE)
            keep = np.ones((TILE,), bool)
            if tile == 0:
                lane = np.arange(TILE)
                after = part * bins_dev + bins_dev + lane
                before = part * bins_dev - TILE + lane
                bin_index = np.where(lane < HALF, after, before)
                keep = ((lane < HALF) & (after < F)) | ((lane >= TILE - HALF) & (before >= 0))
            phases = samples * bin_index[None, :] % length
            zero = ml_dtypes.bfloat16(0)
            fourier[part, tile, :, :TILE] = np.where(keep, cos16[phases], zero)
            fourier[part, tile, :, TILE:] = np.where(keep, sin16[phases], zero)
    lag_part = LAGS // parts
    delay = np.zeros((parts, 2 * bins_dev, LAGS), ml_dtypes.bfloat16)
    scaling = 1.0 / math.sqrt(F)
    for part in range(parts):
        shifts = np.roll(np.arange(LAGS), -part * lag_part) - LAGS // 2
        for tile in range(tiles):
            bin_index = part * bins_dev + tile * TILE + np.arange(TILE)
            phases = bin_index[:, None] * shifts[None, :] % length
            rows = tile * 2 * TILE
            delay[part, rows : rows + TILE] = (cosines[phases] * scaling).astype(ml_dtypes.bfloat16)
            delay[part, rows + TILE : rows + 2 * TILE] = (sines[phases] * scaling).astype(ml_dtypes.bfloat16)
    band = np.abs(np.arange(3 * TILE)[:, None] - TILE - np.arange(TILE)[None, :]) <= HALF
    return fourier, delay, band.astype(ml_dtypes.bfloat16)


def whiten_kernel(plan, scalars, x_hbm, table_ref, band_ref, counts_ref, alive_ref, *refs):
    (first, stop), _, tiles = plan
    refs = list(refs)
    carried = (refs.pop(0), refs.pop(0)) if first else None
    lo_ref, hi_ref = refs.pop(0), refs.pop(0)
    handed = (refs.pop(0), refs.pop(0)) if stop <= tiles else None
    x, sems, eff, spectra, power = refs
    step = pl.program_id(0)
    made = stop - first
    segs, half, _ = lo_ref.shape
    chans = 2 * half
    chunk = x.shape[1] // CHUNKS
    edge = 0 if first else 3
    lag = 1 if first else 3

    def fetch(index):
        part = pl.ds(index * chunk, chunk)
        return pltpu.make_async_copy(x_hbm.at[:, part], x.at[:, part], sems.at[index])

    def store(block):
        slot = step + 1
        spectra[slot] = block
        re, im = block[:, :TILE], block[:, TILE:]
        power[slot + 2] = (re * re + im * im).astype(jnp.bfloat16)

    def finish():
        tile = first + step - 2
        slot = step - 1
        before, after = slot + 1, jnp.where(tile == tiles, edge, slot + 3)
        window = jnp.dot(power[before], band_ref[:TILE], preferred_element_type=jnp.float32)
        window += jnp.dot(power[slot + 2], band_ref[TILE : 2 * TILE], preferred_element_type=jnp.float32)
        window += jnp.dot(power[after], band_ref[2 * TILE :], preferred_element_type=jnp.float32)
        bin_index = scalars[0] * (tiles * TILE) + (tile - 1) * TILE + lax.broadcasted_iota(jnp.int32, (1, TILE), 1)
        count = jnp.minimum(bin_index + HALF, F - 1) - jnp.maximum(bin_index - HALF, 0) + 1
        inverse = 1.0 / count.astype(jnp.float32)
        for seg in range(segs):
            row = seg * chans
            scale = lax.rsqrt(window[row : row + chans] * inverse + EPSILON)
            number = (scalars[1] + seg).astype(jnp.float32)
            scale = jnp.where(number < eff[...], scale, 0.0)
            re = (spectra[slot, row : row + chans, :TILE] * scale).astype(jnp.bfloat16)
            im = (spectra[slot, row : row + chans, TILE:] * scale).astype(jnp.bfloat16)
            lo_ref[seg, :, :TILE] = re[:half]
            lo_ref[seg, :, TILE:] = im[:half]
            hi_ref[seg, :, :TILE] = re[half:]
            hi_ref[seg, :, TILE:] = im[half:]

    @pl.when(step == 0)
    def _():
        for index in range(CHUNKS):
            fetch(index).start()
        row = jnp.where(alive_ref[...] > 0, counts_ref[...], 0).astype(jnp.float32)
        eff[...] = jnp.transpose(jnp.broadcast_to(row, (chans, chans)))
        if carried:
            spectra[0] = carried[0][...]
            power[0:3] = carried[1][...]
        block = None
        for index in range(CHUNKS):
            fetch(index).wait()
            part = slice(index * chunk, (index + 1) * chunk)
            term = jnp.dot(x[:, part], table_ref[part], preferred_element_type=jnp.float32)
            block = term if block is None else block + term
        store(block)

    if lag > 1:

        @pl.when((step >= 1) & (step < lag))
        def _():
            store(jnp.dot(x[...], table_ref[...], preferred_element_type=jnp.float32))

    @pl.when((step >= lag) & (step < made))
    def _():
        finish()
        store(jnp.dot(x[...], table_ref[...], preferred_element_type=jnp.float32))

    @pl.when(step >= made)
    def _():
        finish()

    if handed:

        @pl.when(step == made)
        def _():
            handed[0][...] = spectra[made]
            handed[1][0] = power[edge]
            handed[1][1] = power[made + 1]
            handed[1][2] = power[made + 2]


def whiten(plan, scalars, rows, fourier, band, counts, alive, carried, segs):
    (first, stop), (done_first, done_stop), tiles = plan
    made, done = stop - first, done_stop - done_first
    total, length = rows.shape
    half = total // segs // 2
    lag = 1 if first else 3
    steps = done + lag
    out = jax.ShapeDtypeStruct((segs, half, 2 * TILE * done), jnp.bfloat16)
    out_spec = pl.BlockSpec((segs, half, 2 * TILE), lambda j, p: (0, 0, jnp.clip(j - lag, 0, done - 1)))
    out_shape, out_specs = [out, out], [out_spec, out_spec]
    carry_spec = [
        pl.BlockSpec((total, 2 * TILE), lambda j, p: (0, 0)),
        pl.BlockSpec((3, total, TILE), lambda j, p: (0, 0, 0)),
    ]
    if stop <= tiles:
        out_shape += [
            jax.ShapeDtypeStruct((total, 2 * TILE), jnp.float32),
            jax.ShapeDtypeStruct((3, total, TILE), jnp.bfloat16),
        ]
        out_specs += carry_spec
    vector = pl.BlockSpec((1, 2 * half), lambda j, p: (0, 0))
    return pl.pallas_call(
        functools.partial(whiten_kernel, plan),
        out_shape=out_shape,
        grid_spec=pltpu.PrefetchScalarGridSpec(
            num_scalar_prefetch=1,
            grid=(steps,),
            in_specs=[
                pl.BlockSpec(memory_space=pl.ANY),
                pl.BlockSpec(
                    (None, None, length, 2 * TILE), lambda j, p: (p[0], jnp.minimum(first + j, stop - 1), 0, 0)
                ),
                pl.BlockSpec((3 * TILE, TILE), lambda j, p: (0, 0)),
                vector,
                vector,
            ]
            + (carry_spec if first else []),
            out_specs=out_specs,
            scratch_shapes=[
                pltpu.VMEM((total, length), jnp.bfloat16),
                pltpu.SemaphoreType.DMA((CHUNKS,)),
                pltpu.VMEM((2 * half, 2 * half), jnp.float32),
                pltpu.VMEM((made + 1, total, 2 * TILE), jnp.float32),
                pltpu.VMEM((made + 3, total, TILE), jnp.bfloat16),
            ],
        ),
        compiler_params=pltpu.CompilerParams(vmem_limit_bytes=48 * MIB),
        cost_estimate=pl.CostEstimate(
            flops=2 * total * length * 2 * TILE * made,
            bytes_accessed=2 * length * 2 * TILE * made + 2 * total * length,
            transcendentals=0,
        ),
        name="whiten",
    )(scalars, rows, fourier, band, counts, alive, *carried)


def window_start(offset, chans):
    return jnp.minimum(chans // 2, chans - offset) // 16 * 16


def correlate_kernel(plan, scalars, before_ref, lo_ref, hi_ref, after_ref, delay_ref, *refs):
    tile_first, is_first, is_last = plan
    refs = list(refs)
    if is_first:
        own_counts, next_counts = refs.pop(0), refs.pop(0)
    else:
        sum_ref = refs.pop(0)
    if is_last:
        keep_ref, send_ref = refs.pop(0), refs.pop(0)
    else:
        total = refs.pop(0)
    if is_first:
        inverse_ref = refs.pop(0)
    if is_last:
        total = refs.pop(0)
    select, frame, far, cross = refs
    step, last = pl.program_id(0), pl.num_programs(0) - 1
    segs, half, _ = lo_ref.shape
    chans = 2 * half
    slots = cross.shape[0] // chans

    @pl.when(step == 0)
    def _():
        total[...] = jnp.zeros_like(total) if is_first else sum_ref[...]
        row = lax.broadcasted_iota(jnp.int32, (chans, 2 * chans), 0)
        column = lax.broadcasted_iota(jnp.int32, (chans, 2 * chans), 1)
        for slot in range(slots):
            offset = scalars[1 + slot]
            match = column == row + window_start(offset, chans) + offset
            select[slot * chans : (slot + 1) * chans] = match.astype(jnp.float32).astype(jnp.bfloat16)
        if is_first:
            row = lax.broadcasted_iota(jnp.int32, (chans, chans), 0)
            column = lax.broadcasted_iota(jnp.int32, (chans, chans), 1)
            own, following = own_counts[...].astype(jnp.float32), next_counts[...].astype(jnp.float32)
            mine = jnp.sum(jnp.where(row == column, own, 0.0), axis=1, keepdims=True)
            for slot in range(slots):
                target = row + scalars[1 + slot]
                partner = jnp.where(column == target, own, 0.0) + jnp.where(column + chans == target, following, 0.0)
                partner = jnp.sum(partner, axis=1, keepdims=True)
                divisor = jnp.maximum(jnp.minimum(mine, partner), 1.0)
                inverse_ref[slot] = jnp.broadcast_to(1.0 / divisor, (chans, TILE))

    for seg in range(segs):
        for place, ref in enumerate((before_ref, lo_ref, hi_ref, after_ref)):
            frame[seg, place * half : (place + 1) * half] = ref[seg]
    for seg in range(segs):
        far[seg] = jnp.dot(select[...], frame[seg], preferred_element_type=jnp.float32)
    for slot in range(slots):
        start = window_start(scalars[1 + slot], chans)

        def rows(index, carry, slot=slot, start=start):
            real = jnp.zeros((16, TILE), jnp.float32)
            imag = jnp.zeros((16, TILE), jnp.float32)
            base = pl.multiple_of(start + index * 16, 16)
            spot = pl.multiple_of(slot * chans + index * 16, 16)
            for seg in range(segs):
                own = frame[seg, pl.ds(base, 16), :].astype(jnp.float32)
                own_re, own_im = own[:, :TILE], own[:, TILE:]
                far_re, far_im = far[seg, pl.ds(spot, 16), :TILE], far[seg, pl.ds(spot, 16), TILE:]
                real += own_re * far_re + own_im * far_im
                imag += own_im * far_re - own_re * far_im
            cross[pl.ds(spot, 16), :TILE] = real.astype(jnp.bfloat16)
            cross[pl.ds(spot, 16), TILE:] = imag.astype(jnp.bfloat16)
            return carry

        lax.fori_loop(0, chans // 16, rows, 0, unroll=True)
    total[...] += jnp.dot(cross[...], delay_ref[...], preferred_element_type=jnp.float32)

    if is_last:

        @pl.when(step == last)
        def _():
            keep = keep_ref.shape[2]
            keep_ref[...] = jnp.zeros_like(keep_ref)
            send_ref[...] = jnp.zeros_like(send_ref)
            for slot in range(slots):
                start = pl.multiple_of(window_start(scalars[1 + slot], chans), 16)
                block = total[slot * chans : (slot + 1) * chans]
                keep_ref[slot, pl.ds(start, chans), :] = block[:, :keep]
                send_ref[slot, pl.ds(start, chans), :] = block[:, keep:].astype(send_ref.dtype)


def correlate(plan, scalars, before, lo, hi, after, delay, extra, parts):
    tile_first, is_first, is_last = plan
    segs, half, columns = lo.shape
    chans = 2 * half
    tiles = columns // (2 * TILE)
    slots = scalars.shape[0] - 1
    lags = delay.shape[2]
    keep = lags // parts
    spec = pl.BlockSpec((segs, half, 2 * TILE), lambda j, s: (0, 0, j))
    flat = pl.BlockSpec((slots * chans, lags), lambda j, s: (0, 0))
    vector = pl.BlockSpec((1, chans), lambda j, s: (0, 0))
    frame = lambda width: pl.BlockSpec((slots, 3 * half, width), lambda j, s: (0, 0, 0))
    scratch = [
        pltpu.VMEM((slots * chans, 2 * chans), jnp.bfloat16),
        pltpu.VMEM((segs, 2 * chans, 2 * TILE), jnp.bfloat16),
        pltpu.VMEM((segs, slots * chans, 2 * TILE), jnp.float32),
        pltpu.VMEM((slots * chans, 2 * TILE), jnp.bfloat16),
    ]
    out_shape, out_specs = [], []
    if is_last:
        out_shape += [
            jax.ShapeDtypeStruct((slots, 3 * half, keep), jnp.float32),
            jax.ShapeDtypeStruct((slots, 3 * half, lags - keep), jnp.bfloat16),
        ]
        out_specs += [frame(keep), frame(lags - keep)]
        scratch = [pltpu.VMEM((slots * chans, lags), jnp.float32)] + scratch
    else:
        out_shape += [jax.ShapeDtypeStruct((slots * chans, lags), jnp.float32)]
        out_specs += [flat]
    if is_first:
        out_shape += [jax.ShapeDtypeStruct((slots, chans, TILE), jnp.float32)]
        out_specs += [pl.BlockSpec((slots, chans, TILE), lambda j, s: (0, 0, 0))]
    return pl.pallas_call(
        functools.partial(correlate_kernel, plan),
        out_shape=out_shape,
        grid_spec=pltpu.PrefetchScalarGridSpec(
            num_scalar_prefetch=1,
            grid=(tiles,),
            in_specs=[spec, spec, spec, spec]
            + [pl.BlockSpec((None, 2 * TILE, lags), lambda j, s: (s[0], tile_first + j, 0))]
            + ([vector, vector] if is_first else [flat]),
            out_specs=out_specs,
            scratch_shapes=scratch,
        ),
        compiler_params=pltpu.CompilerParams(vmem_limit_bytes=32 * MIB),
        cost_estimate=pl.CostEstimate(
            flops=tiles * 2 * slots * chans * 2 * TILE * (segs * 2 * chans + lags),
            bytes_accessed=tiles * (4 * segs * half * 2 * TILE * 2),
            transcendentals=0,
        ),
        name="correlate",
    )(scalars, before, lo, hi, after, delay, *extra)


def gather_kernel(scalars, keep_ref, got_ref, mine_ref, other_ref, back_ref):
    _, rows, _ = mine_ref.shape
    half = back_ref.shape[1]
    back_ref[...] = (keep_ref[:, :half] + got_ref[:, :half].astype(jnp.float32)).astype(back_ref.dtype)
    mine = pl.ds(pl.multiple_of(half + scalars[0] * rows, rows), rows)
    other = pl.ds(pl.multiple_of(half + (1 - scalars[0]) * rows, rows), rows)
    mine_ref[...] = keep_ref[:, mine, :] + got_ref[:, mine, :].astype(jnp.float32)
    other_ref[...] = (keep_ref[:, other, :] + got_ref[:, other, :].astype(jnp.float32)).astype(other_ref.dtype)


def gather(span, keep, got):
    slots, rows, lags = keep.shape
    half = rows // 3
    spec = lambda r: pl.BlockSpec((slots, r, lags), lambda j, s: (0, 0, 0))
    return pl.pallas_call(
        gather_kernel,
        out_shape=[
            jax.ShapeDtypeStruct((slots, half, lags), jnp.float32),
            jax.ShapeDtypeStruct((slots, half, lags), jnp.bfloat16),
            jax.ShapeDtypeStruct((slots, half, lags), jnp.bfloat16),
        ],
        grid_spec=pltpu.PrefetchScalarGridSpec(
            num_scalar_prefetch=1, grid=(1,), in_specs=[spec(rows)] * 2, out_specs=[spec(half)] * 3
        ),
        name="gather",
    )(span, keep, got)


def finish_kernel(scalars, mine_ref, other_ref, near_ref, far_ref, inverse_ref, out_ref):
    slots, rows, lags = mine_ref.shape
    mine = pl.ds(pl.multiple_of(scalars[0] * rows, rows), rows)
    for slot in range(slots):
        scale = inverse_ref[slot, mine, :]
        scale = jnp.concatenate([scale] * (lags // TILE), axis=1)
        block = mine_ref[slot] + other_ref[slot].astype(jnp.float32)
        block += near_ref[slot].astype(jnp.float32) + far_ref[slot].astype(jnp.float32)
        out_ref[slot] = block * scale


def finish(span, mine, other, near, far, inverse):
    slots, rows, lags = mine.shape
    spec = pl.BlockSpec((slots, rows, lags), lambda j, s: (0, 0, 0))
    return pl.pallas_call(
        finish_kernel,
        out_shape=jax.ShapeDtypeStruct((slots, rows, lags), jnp.float32),
        grid_spec=pltpu.PrefetchScalarGridSpec(
            num_scalar_prefetch=1,
            grid=(1,),
            in_specs=[spec] * 4 + [pl.BlockSpec(inverse.shape, lambda j, s: (0, 0, 0))],
            out_specs=spec,
        ),
        name="finish",
    )(span, mine, other, near, far, inverse)


def shift(block, axis, distance):
    devices = range(lax.axis_size(axis))
    return lax.ppermute(block, axis, [(i, i + distance) for i in devices if i + distance in devices])


def reduced(span, keep, got, chans):
    spans = lax.axis_size("seg")
    half = chans // 2
    keep = keep + got.astype(jnp.float32)
    back = shift(keep[:, :half].astype(jnp.bfloat16), "chan", -1).astype(jnp.float32)
    keep = keep[:, half:] + jnp.pad(back, ((0, 0), (chans - half, 0), (0, 0)))
    piece = chans // spans
    result = lax.dynamic_slice_in_dim(keep, span * piece, piece, 1)
    for step in range(1, spans):
        target = lax.rem(span + step, spans)
        block = lax.dynamic_slice_in_dim(keep, target * piece, piece, 1).astype(jnp.bfloat16)
        block = lax.ppermute(block, "seg", [(i, (i + step) % spans) for i in range(spans)])
        result = result + block.astype(jnp.float32)
    return result


def shards(traces, dead_mask, seg_counts, offsets):
    segs, chans, length = traces.shape
    parts, spans, blocks = lax.axis_size("freq"), lax.axis_size("seg"), lax.axis_size("chan")
    assert parts == 2
    fourier, delay, band = (jnp.asarray(table) for table in tables(length, parts))
    tiles = fourier.shape[1] - 1
    part = lax.axis_index("freq").astype(jnp.int32)
    span = lax.axis_index("seg").astype(jnp.int32)
    counts, alive = seg_counts.reshape(1, chans), dead_mask.reshape(1, chans)
    next_counts = shift(seg_counts, "chan", -1).reshape(1, chans)
    rows = traces.reshape(segs * chans, length)
    place = jnp.stack([part, span * segs])
    scalars = jnp.concatenate([part.reshape(1), offsets])

    blocks_out, carried = [], []
    made = 0
    for index, stop in enumerate(GROUPS):
        plan = ((made, stop), (max(made - 1, 1), stop - 1 if stop <= tiles else tiles + 1), tiles)
        lo, hi, *carried = whiten(plan, place, rows, fourier, band, counts, alive, carried, segs)
        up, down = hi, lo
        if blocks_out:
            up, down, *earlier = lax.optimization_barrier((up, down, blocks_out[-1][0], blocks_out[-1][3]))
            blocks_out[-1] = (earlier[0], *blocks_out[-1][1:3], earlier[1])
        blocks_out.append((shift(up, "chan", 1), lo, hi, shift(down, "chan", -1)))
        made = stop
    extra, tile_first = [counts, next_counts], 0
    for index, group in enumerate(blocks_out):
        plan = (tile_first, index == 0, index == len(blocks_out) - 1)
        results = list(correlate(plan, scalars, *group, delay, extra, parts))
        if index == 0:
            inverse = results.pop()
        extra = results
        tile_first += group[1].shape[2] // (2 * TILE)
    keep, send = results
    got = lax.ppermute(send, "freq", [(0, 1), (1, 0)])
    if spans == 2:
        position = span.reshape(1)
        mine, other, back = gather(position, keep, got)
        other = lax.ppermute(other, "seg", [(0, 1), (1, 0)])
        near = lax.ppermute(back, ("chan", "seg"), [(2 * i + 3, 2 * i + 1) for i in range(blocks - 1)])
        far = lax.ppermute(back, ("chan", "seg"), [(2 * i + 2, 2 * i + 1) for i in range(blocks - 1)])
        result = finish(position, mine, other, near, far, inverse)
    else:
        piece = chans // spans
        result = reduced(span, keep, got, chans)
        result = result * lax.dynamic_slice_in_dim(inverse, span * piece, piece, 1)[:, :, :1]
    return jnp.transpose(result, (1, 0, 2))


def solution(mesh):
    in_specs = (
        P("seg", ("groups", "chan"), None),
        P(("groups", "chan")),
        P(("groups", "chan")),
        P(),
    )
    out_specs = P(("groups", "chan", "seg"), None, "freq")
    return jax.shard_map(shards, mesh=mesh, in_specs=in_specs, out_specs=out_specs, check_vma=False)
```

time: 95.5 us -> 89.1 us (0.933)
  the two profiles are of different devices: /device:TPU:0 before, /device:TPU:2 now
where the time goes in v2:
time: 89.1 us; the launch traced here: 88.7 us
  Pallas kernels  40.1 us (45%)
  waiting for transfers between devices  26.2 us (29%)
  starting transfers between devices  15.1 us (17%)
  local copies, waits for them, and re-layouts  7.03 us (8%)
    pallas_call x2, Pallas kernels, whiten(): pl.pallas_call(functools.partial(whiten_kernel, plan), out_shape=out_shap...  27.2 us
    ppermute x5, waiting for transfers between devices, shift(): lax.ppermute(block, axis, [(i, i + distance) for i in devices if i + dist...  18.4 us
    ppermute x5, starting transfers between devices, shift(): lax.ppermute(block, axis, [(i, i + distance) for i in devices if i + dist...  12 us
    pallas_call x2, Pallas kernels, correlate(): pl.pallas_call(functools.partial(correlate_kernel, plan), out_shape=out_s...  8.85 us
    unnamed x22, local copies, waits for them, and re-layouts  5.21 us
    ppermute x1, waiting for transfers between devices, shards(): lax.ppermute(back, ('chan', 'seg'), [(2 * i + 2, 2 * i + 1) for i in rang...  3.03 us
    ppermute x1, waiting for transfers between devices, shards(): other = lax.ppermute(other, 'seg', [(0, 1), (1, 0)])  2.62 us
    pallas_call x1, Pallas kernels, gather(): pl.pallas_call(gather_kernel, out_shape=[jax.ShapeDtypeStruct((slots, hal...  2.05 us
  transfers between devices with their start and end apart: 9, of which 5 were waited for; matrix products, arithmetic and copies ran while one was open for 0% of the time, Pallas kernels for 19%

profile of v2, /device:TPU:2, one launch (start us, length us, event | category | flops | bytes accessed | tf_op | source)
XLA Modules:
  0.0 88.7 jit_solution(1627853472904854120)
XLA Ops:
  0.1 0.9 %copy-done.2 = bf16[384,128]{1,0:T(8,128)(2,1)S(1)} copy-done((bf16[384,128]{1,0:T(8,128)(2,1)S(1)}, bf16[384,128]{1,0:T(8,128)(2,1)}, u32[]{:S(2)}) %copy-start.2) | copy-done | bytes 98328
  1.0 0.7 copy-done.4
  1.6 0.7 copy-done.5
  2.3 14.0 %whiten.2 = (bf16[5,64,768]{2,1,0:T(8,128)(2,1)S(1)}, bf16[5,64,768]{2,1,0:T(8,128)(2,1)S(1)}, f32[640,256]{1,0:T(8,128)S(1)}, bf16[3,640,128]{2,1,0:T(8,128)(2,1)S(1)}) custom-call(s32[2]{0:T(128)S(1)} %pad_add_fusion.1.scalars, bf16[640,4096]{1,0:T(8,128)(2,1)} %bitcast.14, bf16[2,9,4096,256]{3,2,1,0:T(8,128)(2,1)} %constant.14.clone.table_ref, ...), custom_call_target="tpu_custom_call" | custom-call | flops 6710886400 | bytes 15728640 | tf_op jit(solution)/shard_map/whiten/pallas_call | solution.py:172
  16.3 3.5 %collective-permute-start = (bf16[5,64,768]{2,1,0:T(8,128)(2,1)S(1)}, bf16[5,64,768]{2,1,0:T(8,128)(2,1)S(1)}, u32[]{:S(2)}, u32[]{:S(2)}) collective-permute-start(bf16[5,64,768]{2,1,0:T(8,128)(2,1)S(1)} %get-tuple-element.26.hi_ref), channel_id=1, source_target_pairs={{0,4},{4,8},{8,12},{1,5},{5,9},{9,13},{2,6},{6,10},{10,14},{3,7},{... | collective-permute-start | bytes 1474568 | tf_op jit(solution)/shard_map/ppermute | solution.py:404
  19.8 1.3 %collective-permute-start.1 = (bf16[5,64,768]{2,1,0:T(8,128)(2,1)S(1)}, bf16[5,64,768]{2,1,0:T(8,128)(2,1)S(1)}, u32[]{:S(2)}, u32[]{:S(2)}) collective-permute-start(bf16[5,64,768]{2,1,0:T(8,128)(2,1)S(1)} %get-tuple-element.27.lo_ref), channel_id=1, source_target_pairs={{4,0},{8,4},{12,8},{5,1},{9,5},{13,9},{6,2},{10,6},{14,10},{7,3},{... | collective-permute-start | bytes 1474568 | tf_op jit(solution)/shard_map/ppermute | solution.py:404
  21.1 13.2 %whiten.3 = (bf16[5,64,1280]{2,1,0:T(8,128)(2,1)S(1)}, bf16[5,64,1280]{2,1,0:T(8,128)(2,1)S(1)}) custom-call(s32[2]{0:T(128)S(1)} %pad_add_fusion.1.scalars, bf16[640,4096]{1,0:T(8,128)(2,1)} %bitcast.15, bf16[2,9,4096,256]{3,2,1,0:T(8,128)(2,1)} %constant.14.clone.table_ref, bf16[384,128]{1,0:T(8,128)(2,1)S(1)} %copy-done.2, s32[1,128]{1,0:T(1,128)S(1)} %bitcast.9, ...), custom_call_target="tpu_custom_call" | custom-call | flops 5368709120 | bytes 13631488 | tf_op jit(solution)/shard_map/whiten/pallas_call | solution.py:172
  34.4 4.6 %collective-permute-start.2 = (bf16[5,64,1280]{2,1,0:T(8,128)(2,1)S(1)}, bf16[5,64,1280]{2,1,0:T(8,128)(2,1)S(1)}, u32[]{:S(2)}, u32[]{:S(2)}) collective-permute-start(bf16[5,64,1280]{2,1,0:T(8,128)(2,1)S(1)} %get-tuple-element.28.hi_ref), channel_id=1, source_target_pairs={{0,4},{4,8},{8,12},{1,5},{5,9},{9,13},{2,6},{6,10},{10,14},{3,7},{... | collective-permute-start | bytes 2457608 | tf_op jit(solution)/shard_map/ppermute | solution.py:404
  39.0 1.3 %collective-permute-start.3 = (bf16[5,64,1280]{2,1,0:T(8,128)(2,1)S(1)}, bf16[5,64,1280]{2,1,0:T(8,128)(2,1)S(1)}, u32[]{:S(2)}, u32[]{:S(2)}) collective-permute-start(bf16[5,64,1280]{2,1,0:T(8,128)(2,1)S(1)} %get-tuple-element.29.lo_ref), channel_id=1, source_target_pairs={{4,0},{8,4},{12,8},{5,1},{9,5},{13,9},{6,2},{10,6},{14,10},{7,3},{... | collective-permute-start | bytes 2457608 | tf_op jit(solution)/shard_map/ppermute | solution.py:404
  40.3 1.3 %collective-permute-start.4 = (s32[128]{0:T(128)S(1)}, s32[128]{0:T(128)S(1)}, u32[]{:S(2)}, u32[]{:S(2)}) collective-permute-start(s32[128]{0:T(128)S(1)} %copy-done.4), channel_id=1, source_target_pairs={{4,0},{8,4},{12,8},{5,1},{9,5},{13,9},{6,2},{10,6},{14,10},{7,3},{... | collective-permute-start | bytes 1544 | tf_op jit(solution)/shard_map/ppermute | solution.py:404
  41.6 18.4 %collective-permute-done.4 = s32[128]{0:T(128)S(1)} collective-permute-done((s32[128]{0:T(128)S(1)}, s32[128]{0:T(128)S(1)}, u32[]{:S(2)}, u32[]{:S(2)}) %collective-permute-start.4) | collective-permute-done | bytes 544 | tf_op jit(solution)/shard_map/ppermute | solution.py:404
  60.1 3.5 %correlate.2 = (f32[512,512]{1,0:T(8,128)S(1)}, f32[4,128,128]{2,1,0:T(8,128)S(1)}) custom-call(s32[5]{0:T(128)S(1)} %pad_add_fusion.scalars, bf16[5,64,768]{2,1,0:T(8,128)(2,1)S(1)} %collective-permute-done.before_ref, bf16[5,64,768]{2,1,0:T(8,128)(2,1)S(1)} %get-tuple-element.27.lo_ref, bf16[5,64,768]{2,1,0:T(8,128)(2,1)S(1)} %get-tuple-element.26.hi_ref, ...), custom_call_target="tpu_custom_call" | custom-call | flops 1409286144 | bytes 1966080 | tf_op jit(solution)/shard_map/correlate/pallas_call | solution.py:325
  63.6 0.7 copy-done.3
  64.3 5.3 %correlate.3 = (f32[4,192,256]{2,1,0:T(8,128)S(1)}, bf16[4,192,256]{2,1,0:T(8,128)(2,1)S(1)}) custom-call(s32[5]{0:T(128)S(1)} %pad_add_fusion.scalars, bf16[5,64,1280]{2,1,0:T(8,128)(2,1)S(1)} %collective-permute-done.2.before_ref, bf16[5,64,1280]{2,1,0:T(8,128)(2,1)S(1)} %get-tuple-element.29.lo_ref, bf16[5,64,1280]{2,1,0:T(8,128)(2,1)S(1)} %get-tuple-element.28.hi_ref, ...), custom_call_target="tpu_custom_call" | custom-call | flops 2348810240 | bytes 3276800 | tf_op jit(solution)/shard_map/correlate/pallas_call | solution.py:325
  69.6 0.9 copy-done.1
  70.5 1.7 %collective-permute-done.5.got_ref = bf16[4,192,256]{2,1,0:T(8,128)(2,1)S(1)} collective-permute-done((bf16[4,192,256]{2,1,0:T(8,128)(2,1)S(1)}, bf16[4,192,256]{2,1,0:T(8,128)(2,1)S(1)}, u32[]{:S(2)}, u32[]{:S(2)}) %collective-permute-start.5) | collective-permute-done | bytes 393248 | tf_op jit(solution)/shard_map/ppermute | solution.py:457
  72.2 0.8 copy-done.6
  73.0 2.0 %gather.1 = (f32[4,64,256]{2,1,0:T(8,128)}, bf16[4,64,256]{2,1,0:T(8,128)(2,1)}, bf16[4,64,256]{2,1,0:T(8,128)(2,1)}) custom-call(s32[1]{0:T(128)} %bitcast.scalars, f32[4,192,256]{2,1,0:T(8,128)} %copy-done.1, bf16[4,192,256]{2,1,0:T(8,128)(2,1)} %copy-done.6), custom_call_target="tpu_custom_call" | custom-call | tf_op jit(solution)/shard_map/gather/pallas_call | solution.py:361
  75.6 1.3 %collective-permute-start.8 = (bf16[4,64,256]{2,1,0:T(8,128)(2,1)}, bf16[4,64,256]{2,1,0:T(8,128)(2,1)S(1)}, u32[]{:S(2)}, u32[]{:S(2)}) collective-permute-start(bf16[4,64,256]{2,1,0:T(8,128)(2,1)} %get-tuple-element.37), channel_id=1, source_target_pairs={{4,2},{8,6},{12,10},{5,3},{9,7},{13,11},{20,18},{24,22},{28,26},{2... | collective-permute-start | bytes 393224 | tf_op jit(solution)/shard_map/ppermute | solution.py:463
  76.9 1.3 %collective-permute-start.7 = (bf16[4,64,256]{2,1,0:T(8,128)(2,1)}, bf16[4,64,256]{2,1,0:T(8,128)(2,1)S(1)}, u32[]{:S(2)}, u32[]{:S(2)}) collective-permute-start(bf16[4,64,256]{2,1,0:T(8,128)(2,1)} %get-tuple-element.37), channel_id=1, source_target_pairs={{6,2},{10,6},{14,10},{7,3},{11,7},{15,11},{22,18},{26,22},{30,26},... | collective-permute-start | bytes 393224 | tf_op jit(solution)/shard_map/ppermute | solution.py:462
  78.2 2.6 %collective-permute-done.6.other_ref = bf16[4,64,256]{2,1,0:T(8,128)(2,1)S(1)} collective-permute-done((bf16[4,64,256]{2,1,0:T(8,128)(2,1)}, bf16[4,64,256]{2,1,0:T(8,128)(2,1)S(1)}, u32[]{:S(2)}, u32[]{:S(2)}) %collective-permute-start.6) | collective-permute-done | bytes 131104 | tf_op jit(solution)/shard_map/ppermute | solution.py:461
  80.8 3.0 %collective-permute-done.8.far_ref = bf16[4,64,256]{2,1,0:T(8,128)(2,1)S(1)} collective-permute-done((bf16[4,64,256]{2,1,0:T(8,128)(2,1)}, bf16[4,64,256]{2,1,0:T(8,128)(2,1)S(1)}, u32[]{:S(2)}, u32[]{:S(2)}) %collective-permute-start.8) | collective-permute-done | bytes 131104 | tf_op jit(solution)/shard_map/ppermute | solution.py:463
  84.9 2.0 %finish.1 = f32[4,64,256]{2,1,0:T(8,128)} custom-call(s32[1]{0:T(128)} %bitcast.scalars, f32[4,64,256]{2,1,0:T(8,128)} %get-tuple-element.35.mine_ref, bf16[4,64,256]{2,1,0:T(8,128)(2,1)} %copy-done.7, bf16[4,64,256]{2,1,0:T(8,128)(2,1)} %copy-done.9, bf16[4,64,256]{2,1,0:T(8,128)(2,1)} %copy-done.8, f32[4,128,128]{2,1,0:T(8,128)} %copy-done.3), custom_call_target="tpu_custom_call" | custom-call | tf_op jit(solution)/shard_map/finish/pallas_call | solution.py:389
  86.9 1.8 %copy.8 = f32[64,4,256]{2,1,0:T(4,128)} copy(f32[64,4,256]{2,0,1:T(8,128)} %bitcast.16) | data formatting | bytes 524288 | tf_op jit(solution)/shard_map/transpose | solution.py:469
  (25 shorter events, 1.8 us)
Async XLA Ops:
  0.1 0.9 %copy-start.2 = (bf16[384,128]{1,0:T(8,128)(2,1)S(1)}, bf16[384,128]{1,0:T(8,128)(2,1)}, u32[]{:S(2)}) copy-start(bf16[384,128]{1,0:T(8,128)(2,1)} %constant.16.clone.band_ref) | copy-start | bytes 294916
  1.0 0.7 copy-start.4
  1.6 0.7 copy-start.5
  16.3 18.1 %collective-permute-start = (bf16[5,64,768]{2,1,0:T(8,128)(2,1)S(1)}, bf16[5,64,768]{2,1,0:T(8,128)(2,1)S(1)}, u32[]{:S(2)}, u32[]{:S(2)}) collective-permute-start(bf16[5,64,768]{2,1,0:T(8,128)(2,1)S(1)} %get-tuple-element.26.hi_ref), channel_id=1, source_target_pairs={{0,4},{4,8},{8,12},{1,5},{5,9},{9,13},{2,6},{6,10},{10,14},{3,7},{... | collective-permute-start | bytes 1474568 | tf_op jit(solution)/shard_map/ppermute | solution.py:404
  19.8 14.6 %collective-permute-start.1 = (bf16[5,64,768]{2,1,0:T(8,128)(2,1)S(1)}, bf16[5,64,768]{2,1,0:T(8,128)(2,1)S(1)}, u32[]{:S(2)}, u32[]{:S(2)}) collective-permute-start(bf16[5,64,768]{2,1,0:T(8,128)(2,1)S(1)} %get-tuple-element.27.lo_ref), channel_id=1, source_target_pairs={{4,0},{8,4},{12,8},{5,1},{9,5},{13,9},{6,2},{10,6},{14,10},{7,3},{... | collective-permute-start | bytes 1474568 | tf_op jit(solution)/shard_map/ppermute | solution.py:404
  21.1 20.5 %copy-start.10 = (s32[4]{0:T(128)S(1)}, s32[4]{0:T(128)}, u32[]{:S(2)}) copy-start(s32[4]{0:T(128)} %param.10) | copy-start | bytes 52
  21.1 38.9 %copy-start = (bf16[2,2048,512]{2,1,0:T(8,128)(2,1)S(1)}, bf16[2,2048,512]{2,1,0:T(8,128)(2,1)}, u32[]{:S(2)}) copy-start(bf16[2,2048,512]{2,1,0:T(8,128)(2,1)} %constant.15.clone.delay_ref) | copy-start | bytes 12582916
  34.4 29.9 %collective-permute-start.2 = (bf16[5,64,1280]{2,1,0:T(8,128)(2,1)S(1)}, bf16[5,64,1280]{2,1,0:T(8,128)(2,1)S(1)}, u32[]{:S(2)}, u32[]{:S(2)}) collective-permute-start(bf16[5,64,1280]{2,1,0:T(8,128)(2,1)S(1)} %get-tuple-element.28.hi_ref), channel_id=1, source_target_pairs={{0,4},{4,8},{8,12},{1,5},{5,9},{9,13},{2,6},{6,10},{10,14},{3,7},{... | collective-permute-start | bytes 2457608 | tf_op jit(solution)/shard_map/ppermute | solution.py:404
  39.0 25.3 %collective-permute-start.3 = (bf16[5,64,1280]{2,1,0:T(8,128)(2,1)S(1)}, bf16[5,64,1280]{2,1,0:T(8,128)(2,1)S(1)}, u32[]{:S(2)}, u32[]{:S(2)}) collective-permute-start(bf16[5,64,1280]{2,1,0:T(8,128)(2,1)S(1)} %get-tuple-element.29.lo_ref), channel_id=1, source_target_pairs={{4,0},{8,4},{12,8},{5,1},{9,5},{13,9},{6,2},{10,6},{14,10},{7,3},{... | collective-permute-start | bytes 2457608 | tf_op jit(solution)/shard_map/ppermute | solution.py:404
  40.3 19.8 %collective-permute-start.4 = (s32[128]{0:T(128)S(1)}, s32[128]{0:T(128)S(1)}, u32[]{:S(2)}, u32[]{:S(2)}) collective-permute-start(s32[128]{0:T(128)S(1)} %copy-done.4), channel_id=1, source_target_pairs={{4,0},{8,4},{12,8},{5,1},{9,5},{13,9},{6,2},{10,6},{14,10},{7,3},{... | collective-permute-start | bytes 1544 | tf_op jit(solution)/shard_map/ppermute | solution.py:404
  63.6 0.7 copy-start.3
  69.6 0.9 copy-start.1
  70.5 1.7 %collective-permute-start.5 = (bf16[4,192,256]{2,1,0:T(8,128)(2,1)S(1)}, bf16[4,192,256]{2,1,0:T(8,128)(2,1)S(1)}, u32[]{:S(2)}, u32[]{:S(2)}) collective-permute-start(bf16[4,192,256]{2,1,0:T(8,128)(2,1)S(1)} %get-tuple-element.34), channel_id=1, source_target_pairs={{0,1},{1,0},{2,3},{3,2},{4,5},{5,4},{6,7},{7,6},{8,9},{9,8},{10,11... | collective-permute-start | bytes 1179656 | tf_op jit(solution)/shard_map/ppermute | solution.py:457
  72.2 0.8 copy-start.6
  75.1 5.7 %collective-permute-start.6 = (bf16[4,64,256]{2,1,0:T(8,128)(2,1)}, bf16[4,64,256]{2,1,0:T(8,128)(2,1)S(1)}, u32[]{:S(2)}, u32[]{:S(2)}) collective-permute-start(bf16[4,64,256]{2,1,0:T(8,128)(2,1)} %get-tuple-element.36), channel_id=1, source_target_pairs={{0,2},{2,0},{1,3},{3,1},{4,6},{6,4},{5,7},{7,5},{8,10},{10,8},{9,1... | collective-permute-start | bytes 393224 | tf_op jit(solution)/shard_map/ppermute | solution.py:461
  75.6 8.2 %collective-permute-start.8 = (bf16[4,64,256]{2,1,0:T(8,128)(2,1)}, bf16[4,64,256]{2,1,0:T(8,128)(2,1)S(1)}, u32[]{:S(2)}, u32[]{:S(2)}) collective-permute-start(bf16[4,64,256]{2,1,0:T(8,128)(2,1)} %get-tuple-element.37), channel_id=1, source_target_pairs={{4,2},{8,6},{12,10},{5,3},{9,7},{13,11},{20,18},{24,22},{28,26},{2... | collective-permute-start | bytes 393224 | tf_op jit(solution)/shard_map/ppermute | solution.py:463
  76.9 7.4 %collective-permute-start.7 = (bf16[4,64,256]{2,1,0:T(8,128)(2,1)}, bf16[4,64,256]{2,1,0:T(8,128)(2,1)S(1)}, u32[]{:S(2)}, u32[]{:S(2)}) collective-permute-start(bf16[4,64,256]{2,1,0:T(8,128)(2,1)} %get-tuple-element.37), channel_id=1, source_target_pairs={{6,2},{10,6},{14,10},{7,3},{11,7},{15,11},{22,18},{26,22},{30,26},... | collective-permute-start | bytes 393224 | tf_op jit(solution)/shard_map/ppermute | solution.py:462
  80.8 3.4 %copy-start.7 = (bf16[4,64,256]{2,1,0:T(8,128)(2,1)}, bf16[4,64,256]{2,1,0:T(8,128)(2,1)S(1)}, u32[]{:S(2)}) copy-start(bf16[4,64,256]{2,1,0:T(8,128)(2,1)S(1)} %collective-permute-done.6.other_ref) | copy-start | bytes 393220
  83.8 0.7 copy-start.8
  84.2 0.7 copy-start.9

commit v3 on v2

v3 whole, which is shorter than its diff:
```python
import functools
import math

import jax
import jax.numpy as jnp
import numpy as np
from jax import lax
from jax.experimental import pallas as pl
from jax.experimental.pallas import tpu as pltpu
from jax.sharding import PartitionSpec as P
import ml_dtypes

HALF = 32
LAGS = 512
F = 2048
TILE = 128
EPSILON = 1e-06
MIB = 1 << 20
GROUPS = (5, 9)


def tables(length, parts):
    bins_dev = F // parts
    tiles = bins_dev // TILE
    cosines = np.cos(np.arange(length) * (2.0 * math.pi / length))
    sines = -np.sin(np.arange(length) * (2.0 * math.pi / length))
    cos16 = cosines.astype(np.float32).astype(ml_dtypes.bfloat16)
    sin16 = sines.astype(np.float32).astype(ml_dtypes.bfloat16)
    samples = np.arange(length)[:, None]
    fourier = np.zeros((parts, tiles + 1, length, 2 * TILE), ml_dtypes.bfloat16)
    for part in range(parts):
        for tile in range(tiles + 1):
            first = part * bins_dev + (tile - 1) * TILE
            bin_index = first + np.arange(TILE)
            keep = np.ones((TILE,), bool)
            if tile == 0:
                lane = np.arange(TILE)
                after = part * bins_dev + bins_dev + lane
                before = part * bins_dev - TILE + lane
                bin_index = np.where(lane < HALF, after, before)
                keep = ((lane < HALF) & (after < F)) | ((lane >= TILE - HALF) & (before >= 0))
            phases = samples * bin_index[None, :] % length
            zero = ml_dtypes.bfloat16(0)
            fourier[part, tile, :, :TILE] = np.where(keep, cos16[phases], zero)
            fourier[part, tile, :, TILE:] = np.where(keep, sin16[phases], zero)
    lag_part = LAGS // parts
    delay = np.zeros((parts, 2 * bins_dev, LAGS), ml_dtypes.bfloat16)
    scaling = 1.0 / math.sqrt(F)
    for part in range(parts):
        shifts = np.roll(np.arange(LAGS), -part * lag_part) - LAGS // 2
        for tile in range(tiles):
            bin_index = part * bins_dev + tile * TILE + np.arange(TILE)
            phases = bin_index[:, None] * shifts[None, :] % length
            rows = tile * 2 * TILE
            delay[part, rows : rows + TILE] = (cosines[phases] * scaling).astype(ml_dtypes.bfloat16)
            delay[part, rows + TILE : rows + 2 * TILE] = (sines[phases] * scaling).astype(ml_dtypes.bfloat16)
    return fourier, delay


def whiten_kernel(plan, scalars, table_ref, *refs):
    (first, stop), _, tiles = plan
    refs = list(refs)
    x, limits = refs.pop(0), refs.pop(0)
    if first:
        carried_spectrum, carried_power = refs.pop(0), refs.pop(0)
    one_ref, two_ref = refs.pop(0), refs.pop(0)
    handed = stop <= tiles
    if handed:
        handed_spectrum, handed_power = refs.pop(0), refs.pop(0)
    spectra, power, band, eff = refs
    step = pl.program_id(0)
    made = stop - first
    segs, half, _ = one_ref.shape
    chans = 2 * half
    edge = 0 if first else 3
    lag = 1 if first else 3
    even = scalars[2] == 0

    def store():
        block = jnp.dot(x[...], table_ref[...], preferred_element_type=jnp.float32)
        slot = step + 1
        spectra[slot] = block
        re, im = block[:, :TILE], block[:, TILE:]
        power[slot + 2] = (re * re + im * im).astype(jnp.bfloat16)

    def finish():
        tile = first + step - 2
        slot = step - 1
        before, after = slot + 1, jnp.where(tile == tiles, edge, slot + 3)
        window = jnp.dot(power[before], band[:TILE], preferred_element_type=jnp.float32)
        window += jnp.dot(power[slot + 2], band[TILE : 2 * TILE], preferred_element_type=jnp.float32)
        window += jnp.dot(power[after], band[2 * TILE :], preferred_element_type=jnp.float32)
        bin_index = scalars[0] * (tiles * TILE) + (tile - 1) * TILE + lax.broadcasted_iota(jnp.int32, (1, TILE), 1)
        count = jnp.minimum(bin_index + HALF, F - 1) - jnp.maximum(bin_index - HALF, 0) + 1
        inverse = 1.0 / count.astype(jnp.float32)
        for seg in range(segs):
            row = seg * chans
            scale = lax.rsqrt(window[row : row + chans] * inverse + EPSILON)
            number = (scalars[1] + seg).astype(jnp.float32)
            scale = jnp.where(number < eff[...], scale, 0.0)
            for lanes in (slice(0, TILE), slice(TILE, 2 * TILE)):
                white = spectra[slot, row : row + chans, lanes] * scale
                lo, hi = white[:half], white[half:]
                one_ref[seg, :, lanes] = jnp.where(even, hi, lo).astype(jnp.bfloat16)
                two_ref[seg, :, lanes] = jnp.where(even, lo, hi).astype(jnp.bfloat16)

    @pl.when(step == 0)
    def _():
        row = lax.broadcasted_iota(jnp.int32, (3 * TILE, TILE), 0)
        column = lax.broadcasted_iota(jnp.int32, (3 * TILE, TILE), 1)
        near = jnp.abs(row - TILE - column) <= HALF
        band[...] = near.astype(jnp.float32).astype(jnp.bfloat16)
        eff[...] = jnp.transpose(jnp.broadcast_to(limits[...], (chans, chans)))
        if first:
            spectra[0] = carried_spectrum[...]
            power[0:3] = carried_power[...]

    @pl.when(step < lag)
    def _():
        store()

    @pl.when((step >= lag) & (step < made))
    def _():
        finish()
        store()

    @pl.when(step >= made)
    def _():
        finish()

    if handed:

        @pl.when(step == made)
        def _():
            handed_spectrum[...] = spectra[made]
            handed_power[0] = power[edge]
            handed_power[1] = power[made + 1]
            handed_power[2] = power[made + 2]


def whiten(plan, scalars, operands, fourier, segs, chans):
    (first, stop), (done_first, done_stop), tiles = plan
    made, done = stop - first, done_stop - done_first
    half, total, length = chans // 2, segs * chans, fourier.shape[2]
    lag = 1 if first else 3
    out = jax.ShapeDtypeStruct((segs, half, 2 * TILE * done), jnp.bfloat16)
    out_spec = pl.BlockSpec((segs, half, 2 * TILE), lambda j, p: (0, 0, jnp.clip(j - lag, 0, done - 1)))
    out_shape, out_specs = [out, out], [out_spec, out_spec]
    scratch = [
        pltpu.VMEM((made + 1, total, 2 * TILE), jnp.float32),
        pltpu.VMEM((made + 3, total, TILE), jnp.bfloat16),
        pltpu.VMEM((3 * TILE, TILE), jnp.bfloat16),
        pltpu.VMEM((chans, chans), jnp.float32),
    ]
    here = pl.BlockSpec(memory_space=pltpu.VMEM)
    if stop <= tiles:
        out_shape += [
            jax.ShapeDtypeStruct((total, 2 * TILE), jnp.float32),
            jax.ShapeDtypeStruct((3, total, TILE), jnp.bfloat16),
        ]
        out_specs += [here, here]
    return pl.pallas_call(
        functools.partial(whiten_kernel, plan),
        out_shape=out_shape,
        grid_spec=pltpu.PrefetchScalarGridSpec(
            num_scalar_prefetch=1,
            grid=(done + lag,),
            in_specs=[
                pl.BlockSpec(
                    (None, None, length, 2 * TILE), lambda j, p: (p[0], jnp.minimum(first + j, stop - 1), 0, 0)
                ),
            ]
            + [here] * len(operands),
            out_specs=out_specs,
            scratch_shapes=scratch,
        ),
        compiler_params=pltpu.CompilerParams(vmem_limit_bytes=36 * MIB),
        cost_estimate=pl.CostEstimate(
            flops=2 * total * length * 2 * TILE * made,
            bytes_accessed=2 * length * 2 * TILE * made + 2 * total * length,
            transcendentals=0,
        ),
        name="whiten",
    )(scalars, fourier, *operands)


def window_start(offset, chans):
    return jnp.minimum(chans // 2, chans - offset) // 16 * 16


def correlate_kernel(plan, scalars, one_ref, two_ref, got_one_ref, got_two_ref, delay_ref, *refs):
    tile_first, is_first, is_last = plan
    refs = list(refs)
    if is_first:
        own_counts, next_counts = refs.pop(0), refs.pop(0)
    else:
        sum_ref = refs.pop(0)
    if is_last:
        keep_ref, send_ref = refs.pop(0), refs.pop(0)
    else:
        total = refs.pop(0)
    if is_first:
        inverse_ref = refs.pop(0)
    if is_last:
        total = refs.pop(0)
    select, frame, far, cross = refs
    step, last = pl.program_id(0), pl.num_programs(0) - 1
    segs, half, _ = one_ref.shape
    chans = 2 * half
    slots = cross.shape[0] // chans
    even, known = scalars[1] == 0, scalars[2]

    @pl.when(step == 0)
    def _():
        total[...] = jnp.zeros_like(total) if is_first else sum_ref[...]
        row = lax.broadcasted_iota(jnp.int32, (chans, 2 * chans), 0)
        column = lax.broadcasted_iota(jnp.int32, (chans, 2 * chans), 1)
        for slot in range(slots):
            offset = scalars[3 + slot]
            match = (column == row + window_start(offset, chans) + offset) & (column < known)
            select[slot * chans : (slot + 1) * chans] = match.astype(jnp.float32).astype(jnp.bfloat16)
        if is_first:
            row = lax.broadcasted_iota(jnp.int32, (chans, chans), 0)
            column = lax.broadcasted_iota(jnp.int32, (chans, chans), 1)
            own, following = own_counts[...].astype(jnp.float32), next_counts[...].astype(jnp.float32)
            mine = jnp.sum(jnp.where(row == column, own, 0.0), axis=1, keepdims=True)
            for slot in range(slots):
                target = row + scalars[3 + slot]
                partner = jnp.where(column == target, own, 0.0) + jnp.where(column + chans == target, following, 0.0)
                partner = jnp.sum(partner, axis=1, keepdims=True)
                divisor = jnp.maximum(jnp.minimum(mine, partner), 1.0)
                inverse_ref[slot] = jnp.broadcast_to(1.0 / divisor, inverse_ref.shape[1:])

    order = ((one_ref, 2, 1), (two_ref, 1, 2), (got_one_ref, 3, 0), (got_two_ref, 0, 3))
    for ref, if_even, if_odd in order:
        spot = pl.ds(pl.multiple_of(jnp.where(even, if_even * half, if_odd * half), half), half)
        for seg in range(segs):
            frame[seg, spot, :] = ref[seg]
    for seg in range(segs):
        far[seg] = jnp.dot(select[...], frame[seg], preferred_element_type=jnp.float32)
    for slot in range(slots):
        start = window_start(scalars[3 + slot], chans)

        def rows(index, carry, slot=slot, start=start):
            real = jnp.zeros((16, TILE), jnp.float32)
            imag = jnp.zeros((16, TILE), jnp.float32)
            base = pl.multiple_of(start + index * 16, 16)
            spot = pl.multiple_of(slot * chans + index * 16, 16)
            for seg in range(segs):
                own = frame[seg, pl.ds(base, 16), :].astype(jnp.float32)
                own_re, own_im = own[:, :TILE], own[:, TILE:]
                far_re, far_im = far[seg, pl.ds(spot, 16), :TILE], far[seg, pl.ds(spot, 16), TILE:]
                real += own_re * far_re + own_im * far_im
                imag += own_im * far_re - own_re * far_im
            cross[pl.ds(spot, 16), :TILE] = real.astype(jnp.bfloat16)
            cross[pl.ds(spot, 16), TILE:] = imag.astype(jnp.bfloat16)
            return carry

        lax.fori_loop(0, chans // 16, rows, 0, unroll=True)
    total[...] += jnp.dot(cross[...], delay_ref[...], preferred_element_type=jnp.float32)

    if is_last:

        @pl.when(step == last)
        def _():
            keep = keep_ref.shape[2]
            keep_ref[...] = jnp.zeros_like(keep_ref)
            send_ref[...] = jnp.zeros_like(send_ref)
            for slot in range(slots):
                start = pl.multiple_of(window_start(scalars[3 + slot], chans), 16)
                block = total[slot * chans : (slot + 1) * chans]
                keep_ref[slot, pl.ds(start, chans), :] = block[:, :keep]
                send_ref[slot, pl.ds(start, chans), :] = block[:, keep:].astype(send_ref.dtype)


def correlate(plan, scalars, one, two, got_one, got_two, delay, extra, parts):
    tile_first, is_first, is_last = plan
    segs, half, columns = one.shape
    chans = 2 * half
    tiles = columns // (2 * TILE)
    slots = scalars.shape[0] - 3
    lags = delay.shape[2]
    keep = lags // parts
    spec = pl.BlockSpec((segs, half, 2 * TILE), lambda j, s: (0, 0, j))
    flat = pl.BlockSpec(memory_space=pltpu.VMEM)
    vector = pl.BlockSpec((1, chans), lambda j, s: (0, 0))
    frame = lambda width: pl.BlockSpec((slots, 3 * half, width), lambda j, s: (0, 0, 0))
    scratch = [
        pltpu.VMEM((slots * chans, 2 * chans), jnp.bfloat16),
        pltpu.VMEM((segs, 2 * chans, 2 * TILE), jnp.bfloat16),
        pltpu.VMEM((segs, slots * chans, 2 * TILE), jnp.float32),
        pltpu.VMEM((slots * chans, 2 * TILE), jnp.bfloat16),
    ]
    out_shape, out_specs = [], []
    if is_last:
        out_shape += [
            jax.ShapeDtypeStruct((slots, 3 * half, keep), jnp.float32),
            jax.ShapeDtypeStruct((slots, 3 * half, lags - keep), jnp.bfloat16),
        ]
        out_specs += [frame(keep), frame(lags - keep)]
        scratch = [pltpu.VMEM((slots * chans, lags), jnp.float32)] + scratch
    else:
        out_shape += [jax.ShapeDtypeStruct((slots * chans, lags), jnp.float32)]
        out_specs += [flat]
    if is_first:
        out_shape += [jax.ShapeDtypeStruct((slots, chans, keep), jnp.float32)]
        out_specs += [flat]
    return pl.pallas_call(
        functools.partial(correlate_kernel, plan),
        out_shape=out_shape,
        grid_spec=pltpu.PrefetchScalarGridSpec(
            num_scalar_prefetch=1,
            grid=(tiles,),
            in_specs=[spec, spec, spec, spec]
            + [pl.BlockSpec((None, 2 * TILE, lags), lambda j, s: (s[0], tile_first + j, 0))]
            + ([vector, vector] if is_first else [flat]),
            out_specs=out_specs,
            scratch_shapes=scratch,
        ),
        compiler_params=pltpu.CompilerParams(vmem_limit_bytes=32 * MIB),
        cost_estimate=pl.CostEstimate(
            flops=tiles * 2 * slots * chans * 2 * TILE * (segs * 2 * chans + lags),
            bytes_accessed=tiles * (4 * segs * half * 2 * TILE * 2),
            transcendentals=0,
        ),
        name="correlate",
    )(scalars, one, two, got_one, got_two, delay, *extra)


def neighbours(devices, first):
    route = list(range(devices))
    for i in range(first, devices - 1, 2):
        route[i], route[i + 1] = i + 1, i
    return list(enumerate(route))


def reduced(span, keep, chans, has_next):
    spans, blocks = lax.axis_size("seg"), lax.axis_size("chan")
    half = chans // 2
    back = lax.ppermute(keep[:, :half].astype(jnp.bfloat16), "chan", [(i, (i - 1) % blocks) for i in range(blocks)])
    back = jnp.where(has_next, back.astype(jnp.float32), 0.0)
    keep = keep[:, half:] + jnp.pad(back, ((0, 0), (chans - half, 0), (0, 0)))
    piece = chans // spans
    result = lax.dynamic_slice_in_dim(keep, span * piece, piece, 1)
    for step in range(1, spans):
        target = lax.rem(span + step, spans)
        block = lax.dynamic_slice_in_dim(keep, target * piece, piece, 1).astype(jnp.bfloat16)
        block = lax.ppermute(block, "seg", [(i, (i + step) % spans) for i in range(spans)])
        result = result + block.astype(jnp.float32)
    return result


def shards(traces, dead_mask, seg_counts, offsets):
    segs, chans, length = traces.shape
    half = chans // 2
    parts, spans, blocks = lax.axis_size("freq"), lax.axis_size("seg"), lax.axis_size("chan")
    assert parts == 2
    fourier, delay = (jnp.asarray(table) for table in tables(length, parts))
    tiles = fourier.shape[1] - 1
    part = lax.axis_index("freq").astype(jnp.int32)
    span = lax.axis_index("seg").astype(jnp.int32)
    place = lax.axis_index("chan").astype(jnp.int32)
    has_next = place < blocks - 1
    counts = seg_counts.reshape(1, chans)
    limits = jnp.where(dead_mask > 0, seg_counts, 0).astype(jnp.float32).reshape(1, chans)
    next_counts = lax.ppermute(seg_counts, "chan", [(i, (i - 1) % blocks) for i in range(blocks)]).reshape(1, chans)
    parity = place & 1
    scalars = jnp.stack([part, span * segs, parity])
    known = jnp.where(has_next, 4 * half, 3 * half)
    settings = jnp.concatenate([jnp.stack([part, parity, known]), offsets])

    groups, operands, made = [], [traces.reshape(segs * chans, length), limits], 0
    for stop in GROUPS:
        plan = ((made, stop), (max(made - 1, 1), stop - 1 if stop <= tiles else tiles + 1), tiles)
        one, two, *passed = whiten(plan, scalars, operands, fourier, segs, chans)
        operands = operands[:2] + passed
        send_one, send_two = one, two
        if groups:
            send_one, send_two, *earlier = lax.optimization_barrier((one, two, *groups[-1][2:]))
            groups[-1] = (*groups[-1][:2], *earlier)
        got_one = lax.ppermute(send_one, "chan", neighbours(blocks, 0))
        got_two = lax.ppermute(send_two, "chan", neighbours(blocks, 1))
        groups.append((one, two, got_one, got_two))
        made = stop
    extra, tile_first = [counts, next_counts], 0
    for index, group in enumerate(groups):
        plan = (tile_first, index == 0, index == len(groups) - 1)
        results = list(correlate(plan, settings, *group, delay, extra, parts))
        if index == 0:
            inverse = results.pop()
        extra = results
        tile_first += group[0].shape[2] // (2 * TILE)
    keep, send = results
    keep = keep + lax.ppermute(send, "freq", [(0, 1), (1, 0)]).astype(jnp.float32)
    if spans == 2:
        lower, upper = keep[:, half:chans], keep[:, chans:]
        mine = jnp.where(span == 0, lower, upper)
        other = jnp.where(span == 0, upper, lower).astype(jnp.bfloat16)
        back = keep[:, :half].astype(jnp.bfloat16)
        other = lax.ppermute(other, "seg", [(0, 1), (1, 0)])
        route = [(2 * i + 1, 2 * ((i - 1) % blocks) + 1) for i in range(blocks)]
        near = lax.ppermute(back, ("chan", "seg"), route + [(2 * i, 2 * i) for i in range(blocks)])
        route = [(2 * i, 2 * ((i - 1) % blocks) + 1) for i in range(blocks)]
        far = lax.ppermute(back, ("chan", "seg"), route + [(2 * i + 1, 2 * i) for i in range(blocks)])
        returned = jnp.where(has_next & (span == 1), near.astype(jnp.float32) + far.astype(jnp.float32), 0.0)
        result = mine + other.astype(jnp.float32) + returned
        result = result * jnp.where(span == 0, inverse[:, :half], inverse[:, half:])
    else:
        piece = chans // spans
        result = reduced(span, keep, chans, has_next)
        result = result * lax.dynamic_slice_in_dim(inverse, span * piece, piece, 1)
    return jnp.transpose(result, (1, 0, 2))


def solution(mesh):
    in_specs = (
        P("seg", ("groups", "chan"), None),
        P(("groups", "chan")),
        P(("groups", "chan")),
        P(),
    )
    out_specs = P(("groups", "chan", "seg"), None, "freq")
    return jax.shard_map(shards, mesh=mesh, in_specs=in_specs, out_specs=out_specs, check_vma=False)
```

time: 89.1 us -> 78.5 us (0.88)
  the two profiles are of different devices: /device:TPU:2 before, /device:TPU:0 now
where the time goes in v3:
time: 78.5 us; the launch traced here: 77.7 us
  Pallas kernels  32.3 us (41%)
  starting transfers between devices  26.3 us (34%)
  waiting for transfers between devices  12.3 us (16%)
  local copies, waits for them, and re-layouts  5.57 us (7%)
  other arithmetic  1.05 us (1%)
    pallas_call x2, Pallas kernels, whiten(): pl.pallas_call(functools.partial(whiten_kernel, plan), out_shape=out_shap...  22 us
    pallas_call x2, Pallas kernels, correlate(): pl.pallas_call(functools.partial(correlate_kernel, plan), out_shape=out_s...  10.3 us
    ppermute x2, starting transfers between devices, shards(): got_two = lax.ppermute(send_two, 'chan', neighbours(blocks, 1))  8.59 us
    ppermute x2, starting transfers between devices, shards(): got_one = lax.ppermute(send_one, 'chan', neighbours(blocks, 0))  7.52 us
    ppermute x1, waiting for transfers between devices, shards(): lax.ppermute(seg_counts, 'chan', [(i, (i - 1) % blocks) for i in range(bl...  7.5 us
    ppermute x1, starting transfers between devices, shards(): lax.ppermute(back, ('chan', 'seg'), route + [(2 * i + 1, 2 * i) for i in...  5.36 us
    unnamed x10, local copies, waits for them, and re-layouts  4.69 us
    ppermute x1, waiting for transfers between devices, shards(): lax.ppermute(back, ('chan', 'seg'), route + [(2 * i + 1, 2 * i) for i in...  3.1 us
  transfers between devices with their start and end apart: 9, of which 3 were waited for; matrix products, arithmetic and copies ran while one was open for 0% of the time, Pallas kernels for 19%

profile of v3, /device:TPU:0, one launch (start us, length us, event | category | flops | bytes accessed | tf_op | source)
XLA Modules:
  0.0 77.7 jit_solution(14023889689455138118)
XLA Ops:
  0.0 0.7 fusion.1.refs_1_
  0.7 0.1 pad_add_fusion.1.scalars
  0.8 2.5 %copy-done = bf16[5,128,4096]{2,1,0:T(8,128)(2,1)S(1)} copy-done((bf16[5,128,4096]{2,1,0:T(8,128)(2,1)S(1)}, bf16[5,128,4096]{2,1,0:T(8,128)(2,1)}, u32[]{:S(2)}) %copy-start) | copy-done | bytes 5242904
  3.2 11.1 %whiten.2 = (bf16[5,64,768]{2,1,0:T(8,128)(2,1)S(1)}, bf16[5,64,768]{2,1,0:T(8,128)(2,1)S(1)}, f32[640,256]{1,0:T(8,128)S(1)}, bf16[3,640,128]{2,1,0:T(8,128)(2,1)S(1)}) custom-call(s32[3]{0:T(128)S(1)} %pad_add_fusion.1.scalars, bf16[2,9,4096,256]{3,2,1,0:T(8,128)(2,1)} %constant.30.clone.table_ref, bf16[640,4096]{1,0:T(8,128)(2,1)S(1)} %bitcast.11, ...), custom_call_target="tpu_custom_call" | custom-call | flops 6710886400 | bytes 15728640 | tf_op jit(solution)/shard_map/whiten/pallas_call | solution.py:162
  14.3 3.1 %collective-permute-start = (bf16[5,64,768]{2,1,0:T(8,128)(2,1)S(1)}, bf16[5,64,768]{2,1,0:T(8,128)(2,1)S(1)}, u32[]{:S(2)}, u32[]{:S(2)}) collective-permute-start(bf16[5,64,768]{2,1,0:T(8,128)(2,1)S(1)} %get-tuple-element.23.one_ref), channel_id=1, source_target_pairs={{0,4},{4,0},{8,12},{12,8},{1,5},{5,1},{9,13},{13,9},{2,6},{6,2},{1... | collective-permute-start | bytes 1474568 | tf_op jit(solution)/shard_map/ppermute | solution.py:381
  17.4 0.7 collective-permute-start.1
  18.1 11.0 %whiten.3 = (bf16[5,64,1280]{2,1,0:T(8,128)(2,1)}, bf16[5,64,1280]{2,1,0:T(8,128)(2,1)}) custom-call(s32[3]{0:T(128)S(1)} %pad_add_fusion.1.scalars, bf16[2,9,4096,256]{3,2,1,0:T(8,128)(2,1)} %constant.30.clone.table_ref, bf16[640,4096]{1,0:T(8,128)(2,1)S(1)} %bitcast.12, f32[1,128]{1,0:T(1,128)S(1)} %fusion.1.refs_1_, ...), custom_call_target="tpu_custom_call" | custom-call | flops 5368709120 | bytes 13631488 | tf_op jit(solution)/shard_map/whiten/pallas_call | solution.py:162
  29.1 4.4 %collective-permute-start.2 = (bf16[5,64,1280]{2,1,0:T(8,128)(2,1)}, bf16[5,64,1280]{2,1,0:T(8,128)(2,1)}, u32[]{:S(2)}, u32[]{:S(2)}) collective-permute-start(bf16[5,64,1280]{2,1,0:T(8,128)(2,1)} %get-tuple-element.25.one_ref), channel_id=1, source_target_pairs={{0,4},{4,0},{8,12},{12,8},{1,5},{5,1},{9,13},{13,9},{2,6},{6,2},{1... | collective-permute-start | bytes 2457608 | tf_op jit(solution)/shard_map/ppermute | solution.py:381
  33.5 7.9 %collective-permute-start.3 = (bf16[5,64,1280]{2,1,0:T(8,128)(2,1)}, bf16[5,64,1280]{2,1,0:T(8,128)(2,1)}, u32[]{:S(2)}, u32[]{:S(2)}) collective-permute-start(bf16[5,64,1280]{2,1,0:T(8,128)(2,1)} %get-tuple-element.26.two_ref), channel_id=1, source_target_pairs={{0,0},{4,8},{8,4},{12,12},{1,1},{5,9},{9,5},{13,13},{2,2},{6,10},{... | collective-permute-start | bytes 2457608 | tf_op jit(solution)/shard_map/ppermute | solution.py:382
  41.4 2.5 %collective-permute-start.4 = (s32[128]{0:T(128)S(1)}, s32[128]{0:T(128)S(1)}, u32[]{:S(2)}, u32[]{:S(2)}) collective-permute-start(s32[128]{0:T(128)S(1)} %copy-done.3), channel_id=1, source_target_pairs={{0,12},{4,0},{8,4},{12,8},{1,13},{5,1},{9,5},{13,9},{2,14},{6,2},{... | collective-permute-start | bytes 1544 | tf_op jit(solution)/shard_map/ppermute | solution.py:366
  43.9 0.1 pad_add_fusion.scalars
  44.0 7.5 %collective-permute-done.4 = s32[128]{0:T(128)S(1)} collective-permute-done((s32[128]{0:T(128)S(1)}, s32[128]{0:T(128)S(1)}, u32[]{:S(2)}, u32[]{:S(2)}) %collective-permute-start.4) | collective-permute-done | bytes 544 | tf_op jit(solution)/shard_map/ppermute | solution.py:366
  51.5 2.2 %copy-done.1 = bf16[2,2048,512]{2,1,0:T(8,128)(2,1)S(1)} copy-done((bf16[2,2048,512]{2,1,0:T(8,128)(2,1)S(1)}, bf16[2,2048,512]{2,1,0:T(8,128)(2,1)}, u32[]{:S(2)}) %copy-start.1) | copy-done | bytes 4194328
  53.7 3.5 %correlate.2 = (f32[512,512]{1,0:T(8,128)S(1)}, f32[4,128,256]{2,1,0:T(8,128)S(1)}) custom-call(s32[7]{0:T(128)S(1)} %pad_add_fusion.scalars, bf16[5,64,768]{2,1,0:T(8,128)(2,1)S(1)} %get-tuple-element.23.one_ref, bf16[5,64,768]{2,1,0:T(8,128)(2,1)S(1)} %get-tuple-element.24.two_ref, bf16[5,64,768]{2,1,0:T(8,128)(2,1)S(1)} %collective-permute-done.got_one_ref, ...), custom_call_target="tpu_custom_call" | custom-call | flops 1409286144 | bytes 1966080 | tf_op jit(solution)/shard_map/correlate/pallas_call | solution.py:308
  57.3 6.8 %correlate.3 = (f32[4,192,256]{2,1,0:T(8,128)S(1)}, bf16[4,192,256]{2,1,0:T(8,128)(2,1)S(1)}) custom-call(s32[7]{0:T(128)S(1)} %pad_add_fusion.scalars, bf16[5,64,1280]{2,1,0:T(8,128)(2,1)} %get-tuple-element.25.one_ref, bf16[5,64,1280]{2,1,0:T(8,128)(2,1)} %get-tuple-element.26.two_ref, bf16[5,64,1280]{2,1,0:T(8,128)(2,1)} %collective-permute-done.2.got_one_ref, ...), custom_call_target="tpu_custom_call" | custom-call | flops 2348810240 | bytes 3276800 | tf_op jit(solution)/shard_map/correlate/pallas_call | solution.py:308
  64.1 0.1 collective-permute-start.5
  64.2 1.7 %collective-permute-done.5 = bf16[4,192,256]{2,1,0:T(8,128)(2,1)S(1)} collective-permute-done((bf16[4,192,256]{2,1,0:T(8,128)(2,1)S(1)}, bf16[4,192,256]{2,1,0:T(8,128)(2,1)S(1)}, u32[]{:S(2)}, u32[]{:S(2)}) %collective-permute-start.5) | collective-permute-done | bytes 393248 | tf_op jit(solution)/shard_map/ppermute | solution.py:394
  65.9 0.1 convert_add_fusion
  66.0 1.6 %collective-permute-start.6 = (bf16[4,64,256]{2,1,0:T(8,128)(2,1)S(1)}, bf16[4,64,256]{2,1,0:T(8,128)(2,1)S(1)}, u32[]{:S(2)}, u32[]{:S(2)}) collective-permute-start(bf16[4,64,256]{2,1,0:T(8,128)(2,1)S(1)} %get-tuple-element.33), channel_id=1, source_target_pairs={{0,2},{2,0},{1,3},{3,1},{4,6},{6,4},{5,7},{7,5},{8,10},{10,8},{9,1... | collective-permute-start | bytes 393224 | tf_op jit(solution)/shard_map/ppermute | solution.py:400
  67.6 0.7 collective-permute-start.7
  68.2 5.4 %collective-permute-start.8 = (bf16[4,64,256]{2,1,0:T(8,128)(2,1)S(1)}, bf16[4,64,256]{2,1,0:T(8,128)(2,1)S(1)}, u32[]{:S(2)}, u32[]{:S(2)}) collective-permute-start(bf16[4,64,256]{2,1,0:T(8,128)(2,1)S(1)} %get-tuple-element.34), channel_id=1, source_target_pairs={{0,14},{4,2},{8,6},{12,10},{2,0},{6,4},{10,8},{14,12},{1,15},{5,3}... | collective-permute-start | bytes 393224 | tf_op jit(solution)/shard_map/ppermute | solution.py:404
  73.6 3.1 %collective-permute-done.8 = bf16[4,64,256]{2,1,0:T(8,128)(2,1)S(1)} collective-permute-done((bf16[4,64,256]{2,1,0:T(8,128)(2,1)S(1)}, bf16[4,64,256]{2,1,0:T(8,128)(2,1)S(1)}, u32[]{:S(2)}, u32[]{:S(2)}) %collective-permute-start.8) | collective-permute-done | bytes 131104 | tf_op jit(solution)/shard_map/ppermute | solution.py:404
  76.7 0.1 multiply_bitcast_fusion
  76.8 0.9 %copy.7 = f32[64,4,256]{2,1,0:T(4,128)} copy(f32[64,4,256]{2,0,1:T(8,128)S(1)} %multiply_bitcast_fusion) | data formatting | bytes 524288 | tf_op jit(solution)/shard_map/transpose | solution.py:412
  (15 shorter events, 0.1 us)
Async XLA Ops:
  0.8 2.5 %copy-start = (bf16[5,128,4096]{2,1,0:T(8,128)(2,1)S(1)}, bf16[5,128,4096]{2,1,0:T(8,128)(2,1)}, u32[]{:S(2)}) copy-start(bf16[5,128,4096]{2,1,0:T(8,128)(2,1)} %param.6) | copy-start | bytes 15728644
  14.3 14.8 %collective-permute-start = (bf16[5,64,768]{2,1,0:T(8,128)(2,1)S(1)}, bf16[5,64,768]{2,1,0:T(8,128)(2,1)S(1)}, u32[]{:S(2)}, u32[]{:S(2)}) collective-permute-start(bf16[5,64,768]{2,1,0:T(8,128)(2,1)S(1)} %get-tuple-element.23.one_ref), channel_id=1, source_target_pairs={{0,4},{4,0},{8,12},{12,8},{1,5},{5,1},{9,13},{13,9},{2,6},{6,2},{1... | collective-permute-start | bytes 1474568 | tf_op jit(solution)/shard_map/ppermute | solution.py:381
  17.4 11.7 %collective-permute-start.1 = (bf16[5,64,768]{2,1,0:T(8,128)(2,1)S(1)}, bf16[5,64,768]{2,1,0:T(8,128)(2,1)S(1)}, u32[]{:S(2)}, u32[]{:S(2)}) collective-permute-start(bf16[5,64,768]{2,1,0:T(8,128)(2,1)S(1)} %get-tuple-element.24.two_ref), channel_id=1, source_target_pairs={{0,0},{4,8},{8,4},{12,12},{1,1},{5,9},{9,5},{13,13},{2,2},{6,10},{... | collective-permute-start | bytes 1474568 | tf_op jit(solution)/shard_map/ppermute | solution.py:382
  18.1 23.3 %copy-start.3 = (s32[128]{0:T(128)S(1)}, s32[128]{0:T(128)}, u32[]{:S(2)}) copy-start(s32[128]{0:T(128)} %param.8) | copy-start | bytes 1540
  18.1 25.8 %copy-start.4 = (s32[4]{0:T(128)S(1)}, s32[4]{0:T(128)}, u32[]{:S(2)}) copy-start(s32[4]{0:T(128)} %param.9) | copy-start | bytes 52
  29.1 28.2 %collective-permute-start.2 = (bf16[5,64,1280]{2,1,0:T(8,128)(2,1)}, bf16[5,64,1280]{2,1,0:T(8,128)(2,1)}, u32[]{:S(2)}, u32[]{:S(2)}) collective-permute-start(bf16[5,64,1280]{2,1,0:T(8,128)(2,1)} %get-tuple-element.25.one_ref), channel_id=1, source_target_pairs={{0,4},{4,0},{8,12},{12,8},{1,5},{5,1},{9,13},{13,9},{2,6},{6,2},{1... | collective-permute-start | bytes 2457608 | tf_op jit(solution)/shard_map/ppermute | solution.py:381
  33.5 23.8 %collective-permute-start.3 = (bf16[5,64,1280]{2,1,0:T(8,128)(2,1)}, bf16[5,64,1280]{2,1,0:T(8,128)(2,1)}, u32[]{:S(2)}, u32[]{:S(2)}) collective-permute-start(bf16[5,64,1280]{2,1,0:T(8,128)(2,1)} %get-tuple-element.26.two_ref), channel_id=1, source_target_pairs={{0,0},{4,8},{8,4},{12,12},{1,1},{5,9},{9,5},{13,13},{2,2},{6,10},{... | collective-permute-start | bytes 2457608 | tf_op jit(solution)/shard_map/ppermute | solution.py:382
  41.4 10.1 %collective-permute-start.4 = (s32[128]{0:T(128)S(1)}, s32[128]{0:T(128)S(1)}, u32[]{:S(2)}, u32[]{:S(2)}) collective-permute-start(s32[128]{0:T(128)S(1)} %copy-done.3), channel_id=1, source_target_pairs={{0,12},{4,0},{8,4},{12,8},{1,13},{5,1},{9,5},{13,9},{2,14},{6,2},{... | collective-permute-start | bytes 1544 | tf_op jit(solution)/shard_map/ppermute | solution.py:366
  51.5 2.2 %copy-start.1 = (bf16[2,2048,512]{2,1,0:T(8,128)(2,1)S(1)}, bf16[2,2048,512]{2,1,0:T(8,128)(2,1)}, u32[]{:S(2)}) copy-start(bf16[2,2048,512]{2,1,0:T(8,128)(2,1)} %constant.31.clone.delay_ref) | copy-start | bytes 12582916
  53.7 3.6 %copy-start.2 = (bf16[2,2048,512]{2,1,0:T(8,128)(2,1)S(1)}, bf16[2,2048,512]{2,1,0:T(8,128)(2,1)}, u32[]{:S(2)}) copy-start(bf16[2,2048,512]{2,1,0:T(8,128)(2,1)} %constant.31.clone.delay_ref) | copy-start | bytes 12582916
  64.1 1.8 %collective-permute-start.5 = (bf16[4,192,256]{2,1,0:T(8,128)(2,1)S(1)}, bf16[4,192,256]{2,1,0:T(8,128)(2,1)S(1)}, u32[]{:S(2)}, u32[]{:S(2)}) collective-permute-start(bf16[4,192,256]{2,1,0:T(8,128)(2,1)S(1)} %get-tuple-element.31), channel_id=1, source_target_pairs={{0,1},{1,0},{2,3},{3,2},{4,5},{5,4},{6,7},{7,6},{8,9},{9,8},{10,11... | collective-permute-start | bytes 1179656 | tf_op jit(solution)/shard_map/ppermute | solution.py:394
  66.0 7.6 %collective-permute-start.6 = (bf16[4,64,256]{2,1,0:T(8,128)(2,1)S(1)}, bf16[4,64,256]{2,1,0:T(8,128)(2,1)S(1)}, u32[]{:S(2)}, u32[]{:S(2)}) collective-permute-start(bf16[4,64,256]{2,1,0:T(8,128)(2,1)S(1)} %get-tuple-element.33), channel_id=1, source_target_pairs={{0,2},{2,0},{1,3},{3,1},{4,6},{6,4},{5,7},{7,5},{8,10},{10,8},{9,1... | collective-permute-start | bytes 393224 | tf_op jit(solution)/shard_map/ppermute | solution.py:400
  67.6 6.0 %collective-permute-start.7 = (bf16[4,64,256]{2,1,0:T(8,128)(2,1)S(1)}, bf16[4,64,256]{2,1,0:T(8,128)(2,1)S(1)}, u32[]{:S(2)}, u32[]{:S(2)}) collective-permute-start(bf16[4,64,256]{2,1,0:T(8,128)(2,1)S(1)} %get-tuple-element.34), channel_id=1, source_target_pairs={{2,14},{6,2},{10,6},{14,10},{0,0},{4,4},{8,8},{12,12},{3,15},{7,3}... | collective-permute-start | bytes 393224 | tf_op jit(solution)/shard_map/ppermute | solution.py:402
  68.2 8.5 %collective-permute-start.8 = (bf16[4,64,256]{2,1,0:T(8,128)(2,1)S(1)}, bf16[4,64,256]{2,1,0:T(8,128)(2,1)S(1)}, u32[]{:S(2)}, u32[]{:S(2)}) collective-permute-start(bf16[4,64,256]{2,1,0:T(8,128)(2,1)S(1)} %get-tuple-element.34), channel_id=1, source_target_pairs={{0,14},{4,2},{8,6},{12,10},{2,0},{6,4},{10,8},{14,12},{1,15},{5,3}... | collective-permute-start | bytes 393224 | tf_op jit(solution)/shard_map/ppermute | solution.py:404

commit v4 on v3

--- a/solution.py
+++ b/solution.py
@@ -16,7 +16,7 @@
 TILE = 128
 EPSILON = 1e-06
 MIB = 1 << 20
-GROUPS = (5, 9)
+GROUPS = (6, 9)
 
 
 def tables(length, parts):
@@ -327,11 +327,35 @@
     )(scalars, one, two, got_one, got_two, delay, *extra)
 
 
-def neighbours(devices, first):
-    route = list(range(devices))
-    for i in range(first, devices - 1, 2):
-        route[i], route[i + 1] = i + 1, i
-    return list(enumerate(route))
+def swap(block, first):
+    blocks, parts = lax.axis_size("chan"), lax.axis_size("freq")
+    route = []
+    for i in range(blocks):
+        partner = i + 1 if (i - first) % 2 == 0 else i - 1
+        alone = not 0 <= partner < blocks
+        for part in range(parts):
+            target = i * parts + (part + 1) % parts if alone else partner * parts + part
+            route.append((i * parts + part, target))
+    return lax.ppermute(block, ("chan", "freq"), route)
+
+
+def returns(blocks, parts):
+    near, far = {}, {}
+    last = blocks - 1
+    for i in range(blocks):
+        near[i, 1] = (i - 1, 1) if i else (0, 0)
+        near[i, 0] = (i + 1, 0) if i < last else (last, 1)
+        far[i, 0] = (i - 1, 1) if i else (0, 0)
+        far[i, 1] = (i + 1, 0) if i < last else (last, 1)
+    routes = []
+    for steps in (near, far):
+        route = []
+        for source, target in steps.items():
+            for part in range(parts):
+                end = (part + 1) % parts if source == target else part
+                route.append(((2 * source[0] + source[1]) * parts + part, (2 * target[0] + target[1]) * parts + end))
+        routes.append(route)
+    return routes
 
 
 def reduced(span, keep, chans, has_next):
@@ -374,12 +398,12 @@
         plan = ((made, stop), (max(made - 1, 1), stop - 1 if stop <= tiles else tiles + 1), tiles)
         one, two, *passed = whiten(plan, scalars, operands, fourier, segs, chans)
         operands = operands[:2] + passed
-        send_one, send_two = one, two
         if groups:
             send_one, send_two, *earlier = lax.optimization_barrier((one, two, *groups[-1][2:]))
             groups[-1] = (*groups[-1][:2], *earlier)
-        got_one = lax.ppermute(send_one, "chan", neighbours(blocks, 0))
-        got_two = lax.ppermute(send_two, "chan", neighbours(blocks, 1))
+        else:
+            send_one, send_two, next_counts = lax.optimization_barrier((one, two, next_counts))
+        got_one, got_two = swap(send_one, 0), swap(send_two, 1)
         groups.append((one, two, got_one, got_two))
         made = stop
     extra, tile_first = [counts, next_counts], 0
@@ -398,10 +422,9 @@
         other = jnp.where(span == 0, upper, lower).astype(jnp.bfloat16)
         back = keep[:, :half].astype(jnp.bfloat16)
         other = lax.ppermute(other, "seg", [(0, 1), (1, 0)])
-        route = [(2 * i + 1, 2 * ((i - 1) % blocks) + 1) for i in range(blocks)]
-        near = lax.ppermute(back, ("chan", "seg"), route + [(2 * i, 2 * i) for i in range(blocks)])
-        route = [(2 * i, 2 * ((i - 1) % blocks) + 1) for i in range(blocks)]
-        far = lax.ppermute(back, ("chan", "seg"), route + [(2 * i + 1, 2 * i) for i in range(blocks)])
+        route_near, route_far = returns(blocks, parts)
+        near = lax.ppermute(back, ("chan", "seg", "freq"), route_near)
+        far = lax.ppermute(back, ("chan", "seg", "freq"), route_far)
         returned = jnp.where(has_next & (span == 1), near.astype(jnp.float32) + far.astype(jnp.float32), 0.0)
         result = mine + other.astype(jnp.float32) + returned
         result = result * jnp.where(span == 0, inverse[:, :half], inverse[:, half:])

time: 78.5 us -> 72.8 us (0.927)
  starting transfers between devices: 26.3 us -> 9.39 us
  waiting for transfers between devices: 12.3 us -> 19 us
  local copies, waits for them, and re-layouts: 5.57 us -> 10.6 us
  Pallas kernels: 32.3 us -> 31.1 us
  other arithmetic: 1.05 us -> 2.1 us
    ppermute x6, starting transfers between devices: 22.1 us -> 2.77 us  [the longest x1 1.75 us: shards(): near = lax.ppermute(back, ('chan', 'seg', 'freq'), route_near)]
    ppermute x6, waiting for transfers between devices: 3.12 us -> 13 us  [the longest x4 12 us: swap(): return lax.ppermute(block, ('chan', 'freq'), route)]
    ppermute x1, waiting for transfers between devices: 7.5 us -> 0.01 us  [shards(): lax.ppermute(seg_counts, 'chan', [(i, (i - 1) % blocks) for i in range(bl...]
    unnamed x10 -> x24, local copies, waits for them, and re-layouts: 4.69 us -> 9.68 us
    ppermute x1, waiting for transfers between devices: 0.01 us -> 4.15 us  [shards(): other = lax.ppermute(other, 'seg', [(0, 1), (1, 0)])]
    ppermute x1, starting transfers between devices: 2.51 us -> 5.05 us  [shards(): lax.ppermute(seg_counts, 'chan', [(i, (i - 1) % blocks) for i in range(bl...]
    transpose x1, other arithmetic: 0.1 us -> 1.13 us  [shards(): return jnp.transpose(result, (1, 0, 2))]
    pallas_call x2, Pallas kernels: 22 us -> 21.1 us  [whiten(): pl.pallas_call(functools.partial(whiten_kernel, plan), out_shape=out_shap...]
  transfers between devices with their start and end apart: 9 -> 9, of which waited for: 3 -> 5; matrix products, arithmetic and copies ran while one was open for 0% -> 1% of each run, Pallas kernels for 19% -> 36%
where the time goes in v4:
time: 72.8 us; the launch traced here: 72.3 us
  Pallas kernels  31.1 us (43%)
  waiting for transfers between devices  19 us (26%)
  local copies, waits for them, and re-layouts  10.6 us (15%)
  starting transfers between devices  9.39 us (13%)
  other arithmetic  2.1 us (3%)
    pallas_call x2, Pallas kernels, whiten(): pl.pallas_call(functools.partial(whiten_kernel, plan), out_shape=out_shap...  21.1 us
    ppermute x4, waiting for transfers between devices, swap(): return lax.ppermute(block, ('chan', 'freq'), route)  12 us
    pallas_call x2, Pallas kernels, correlate(): pl.pallas_call(functools.partial(correlate_kernel, plan), out_shape=out_s...  10 us
    unnamed x24, local copies, waits for them, and re-layouts  9.68 us
    ppermute x1, starting transfers between devices, shards(): lax.ppermute(seg_counts, 'chan', [(i, (i - 1) % blocks) for i in range(bl...  5.05 us
    ppermute x1, waiting for transfers between devices, shards(): other = lax.ppermute(other, 'seg', [(0, 1), (1, 0)])  4.15 us
    ppermute x1, waiting for transfers between devices, shards(): lax.ppermute(send, 'freq', [(0, 1), (1, 0)]).astype(jnp.float32)  1.93 us
    ppermute x1, starting transfers between devices, shards(): near = lax.ppermute(back, ('chan', 'seg', 'freq'), route_near)  1.75 us
  transfers between devices with their start and end apart: 9, of which 5 were waited for; matrix products, arithmetic and copies ran while one was open for 1% of the time, Pallas kernels for 36%

profile of v4, /device:TPU:0, one launch (start us, length us, event | category | flops | bytes accessed | tf_op | source)
XLA Modules:
  0.0 72.3 jit_solution(15391530045979953418)
XLA Ops:
  0.0 5.0 %collective-permute-start = (s32[128]{0:T(128)}, s32[128]{0:T(128)S(1)}, u32[]{:S(2)}, u32[]{:S(2)}) collective-permute-start(s32[128]{0:T(128)} %param.8), channel_id=1, source_target_pairs={{0,12},{4,0},{8,4},{12,8},{1,13},{5,1},{9,5},{13,9},{2,14},{6,2},{... | collective-permute-start | bytes 1544 | tf_op jit(solution)/shard_map/ppermute | solution.py:390
  5.0 0.7 fusion.1.refs_1_
  5.8 2.5 %copy-done = bf16[5,128,4096]{2,1,0:T(8,128)(2,1)S(1)} copy-done((bf16[5,128,4096]{2,1,0:T(8,128)(2,1)S(1)}, bf16[5,128,4096]{2,1,0:T(8,128)(2,1)}, u32[]{:S(2)}) %copy-start) | copy-done | bytes 5242904
  8.3 12.9 %whiten.2 = (bf16[5,64,1024]{2,1,0:T(8,128)(2,1)S(1)}, bf16[5,64,1024]{2,1,0:T(8,128)(2,1)S(1)}, f32[640,256]{1,0:T(8,128)S(1)}, bf16[3,640,128]{2,1,0:T(8,128)(2,1)S(1)}) custom-call(s32[3]{0:T(128)S(1)} %pad_add_fusion.1.scalars, bf16[2,9,4096,256]{3,2,1,0:T(8,128)(2,1)} %constant.30.clone.table_ref, bf16[640,4096]{1,0:T(8,128)(2,1)S(1)} %bitcast.11, ...), custom_call_target="tpu_custom_call" | custom-call | flops 8053063680 | bytes 17825792 | tf_op jit(solution)/shard_map/whiten/pallas_call | solution.py:162
  21.4 8.2 %whiten.3 = (bf16[5,64,1024]{2,1,0:T(8,128)(2,1)S(1)}, bf16[5,64,1024]{2,1,0:T(8,128)(2,1)S(1)}) custom-call(s32[3]{0:T(128)S(1)} %pad_add_fusion.1.scalars, bf16[2,9,4096,256]{3,2,1,0:T(8,128)(2,1)} %constant.30.clone.table_ref, bf16[640,4096]{1,0:T(8,128)(2,1)S(1)} %bitcast.12, f32[1,128]{1,0:T(1,128)S(1)} %fusion.1.refs_1_, ...), custom_call_target="tpu_custom_call" | custom-call | flops 4026531840 | bytes 11534336 | tf_op jit(solution)/shard_map/whiten/pallas_call | solution.py:162
  29.7 7.8 %collective-permute-done.1.got_one_ref = bf16[5,64,1024]{2,1,0:T(8,128)(2,1)S(1)} collective-permute-done((bf16[5,64,1024]{2,1,0:T(8,128)(2,1)S(1)}, bf16[5,64,1024]{2,1,0:T(8,128)(2,1)S(1)}, u32[]{:S(2)}, u32[]{:S(2)}) %collective-permute-start.1) | collective-permute-done | bytes 655392 | tf_op jit(solution)/shard_map/ppermute | solution.py:339
  37.5 0.9 %copy-done.6 = bf16[5,64,1024]{2,1,0:T(8,128)(2,1)} copy-done((bf16[5,64,1024]{2,1,0:T(8,128)(2,1)}, bf16[5,64,1024]{2,1,0:T(8,128)(2,1)S(1)}, u32[]{:S(2)}) %copy-start.6) | copy-done | bytes 655384
  38.3 0.9 %copy-done.8 = bf16[5,64,1024]{2,1,0:T(8,128)(2,1)} copy-done((bf16[5,64,1024]{2,1,0:T(8,128)(2,1)}, bf16[5,64,1024]{2,1,0:T(8,128)(2,1)S(1)}, u32[]{:S(2)}) %copy-start.8) | copy-done | bytes 655384
  39.2 0.9 %collective-permute-start.3 = (bf16[5,64,1024]{2,1,0:T(8,128)(2,1)S(1)}, bf16[5,64,1024]{2,1,0:T(8,128)(2,1)S(1)}, u32[]{:S(2)}, u32[]{:S(2)}) collective-permute-start(bf16[5,64,1024]{2,1,0:T(8,128)(2,1)S(1)} %get-tuple-element.30.one_ref), channel_id=1, source_target_pairs={{0,4},{1,5},{4,0},{5,1},{8,12},{9,13},{12,8},{13,9},{2,6},{3,7},{6... | collective-permute-start | bytes 1966088 | tf_op jit(solution)/shard_map/ppermute | solution.py:339
  40.2 2.2 %copy-done.1 = bf16[2,2048,512]{2,1,0:T(8,128)(2,1)S(1)} copy-done((bf16[2,2048,512]{2,1,0:T(8,128)(2,1)S(1)}, bf16[2,2048,512]{2,1,0:T(8,128)(2,1)}, u32[]{:S(2)}) %copy-start.1) | copy-done | bytes 4194328
  42.4 1.1 %copy-done.5 = bf16[5,64,1024]{2,1,0:T(8,128)(2,1)S(1)} copy-done((bf16[5,64,1024]{2,1,0:T(8,128)(2,1)S(1)}, bf16[5,64,1024]{2,1,0:T(8,128)(2,1)}, u32[]{:S(2)}) %copy-start.5) | copy-done | bytes 655384
  43.4 1.1 %copy-done.7 = bf16[5,64,1024]{2,1,0:T(8,128)(2,1)S(1)} copy-done((bf16[5,64,1024]{2,1,0:T(8,128)(2,1)S(1)}, bf16[5,64,1024]{2,1,0:T(8,128)(2,1)}, u32[]{:S(2)}) %copy-start.7) | copy-done | bytes 655384
  44.5 1.1 %copy-done.9 = bf16[5,64,1024]{2,1,0:T(8,128)(2,1)S(1)} copy-done((bf16[5,64,1024]{2,1,0:T(8,128)(2,1)S(1)}, bf16[5,64,1024]{2,1,0:T(8,128)(2,1)}, u32[]{:S(2)}) %copy-start.9) | copy-done | bytes 655384
  45.6 4.6 %correlate.2 = (f32[512,512]{1,0:T(8,128)S(1)}, f32[4,128,256]{2,1,0:T(8,128)S(1)}) custom-call(s32[7]{0:T(128)S(1)} %pad_add_fusion.scalars, bf16[5,64,1024]{2,1,0:T(8,128)(2,1)S(1)} %get-tuple-element.28.one_ref, bf16[5,64,1024]{2,1,0:T(8,128)(2,1)S(1)} %copy-done.5, bf16[5,64,1024]{2,1,0:T(8,128)(2,1)S(1)} %copy-done.7, ...), custom_call_target="tpu_custom_call" | custom-call | flops 1879048192 | bytes 2621440 | tf_op jit(solution)/shard_map/correlate/pallas_call | solution.py:308
  50.3 4.2 %collective-permute-done.3.got_one_ref = bf16[5,64,1024]{2,1,0:T(8,128)(2,1)S(1)} collective-permute-done((bf16[5,64,1024]{2,1,0:T(8,128)(2,1)S(1)}, bf16[5,64,1024]{2,1,0:T(8,128)(2,1)S(1)}, u32[]{:S(2)}, u32[]{:S(2)}) %collective-permute-start.3) | collective-permute-done | bytes 655392 | tf_op jit(solution)/shard_map/ppermute | solution.py:339
  54.5 5.4 %correlate.3 = (f32[4,192,256]{2,1,0:T(8,128)S(1)}, bf16[4,192,256]{2,1,0:T(8,128)(2,1)}) custom-call(s32[7]{0:T(128)S(1)} %pad_add_fusion.scalars, bf16[5,64,1024]{2,1,0:T(8,128)(2,1)S(1)} %get-tuple-element.30.one_ref, bf16[5,64,1024]{2,1,0:T(8,128)(2,1)S(1)} %get-tuple-element.31.two_ref, bf16[5,64,1024]{2,1,0:T(8,128)(2,1)S(1)} %collective-permute-done.3.got_one_ref, ...), custom_call_target="tpu_custom_call" | custom-call | flops 1879048192 | bytes 2621440 | tf_op jit(solution)/shard_map/correlate/pallas_call | solution.py:308
  59.9 1.9 %collective-permute-done.5 = bf16[4,192,256]{2,1,0:T(8,128)(2,1)S(1)} collective-permute-done((bf16[4,192,256]{2,1,0:T(8,128)(2,1)}, bf16[4,192,256]{2,1,0:T(8,128)(2,1)S(1)}, u32[]{:S(2)}, u32[]{:S(2)}) %collective-permute-start.5) | collective-permute-done | bytes 393248 | tf_op jit(solution)/shard_map/ppermute | solution.py:418
  61.8 0.1 convert_add_fusion
  61.9 1.6 %collective-permute-start.6 = (bf16[4,64,256]{2,1,0:T(8,128)(2,1)S(1)}, bf16[4,64,256]{2,1,0:T(8,128)(2,1)S(1)}, u32[]{:S(2)}, u32[]{:S(2)}) collective-permute-start(bf16[4,64,256]{2,1,0:T(8,128)(2,1)S(1)} %get-tuple-element.39), channel_id=1, source_target_pairs={{0,2},{2,0},{1,3},{3,1},{4,6},{6,4},{5,7},{7,5},{8,10},{10,8},{9,1... | collective-permute-start | bytes 393224 | tf_op jit(solution)/shard_map/ppermute | solution.py:424
  63.5 1.7 %collective-permute-start.7 = (bf16[4,64,256]{2,1,0:T(8,128)(2,1)S(1)}, bf16[4,64,256]{2,1,0:T(8,128)(2,1)S(1)}, u32[]{:S(2)}, u32[]{:S(2)}) collective-permute-start(bf16[4,64,256]{2,1,0:T(8,128)(2,1)S(1)} %get-tuple-element.40), channel_id=1, source_target_pairs={{2,0},{3,1},{0,4},{1,5},{6,2},{7,3},{4,8},{5,9},{10,6},{11,7},{8,1... | collective-permute-start | bytes 393224 | tf_op jit(solution)/shard_map/ppermute | solution.py:426
  65.2 4.2 %collective-permute-done.6 = bf16[4,64,256]{2,1,0:T(8,128)(2,1)S(1)} collective-permute-done((bf16[4,64,256]{2,1,0:T(8,128)(2,1)S(1)}, bf16[4,64,256]{2,1,0:T(8,128)(2,1)S(1)}, u32[]{:S(2)}, u32[]{:S(2)}) %collective-permute-start.6) | collective-permute-done | bytes 131104 | tf_op jit(solution)/shard_map/ppermute | solution.py:424
  69.4 0.9 %collective-permute-done.7 = bf16[4,64,256]{2,1,0:T(8,128)(2,1)S(1)} collective-permute-done((bf16[4,64,256]{2,1,0:T(8,128)(2,1)S(1)}, bf16[4,64,256]{2,1,0:T(8,128)(2,1)S(1)}, u32[]{:S(2)}, u32[]{:S(2)}) %collective-permute-start.7) | collective-permute-done | bytes 131104 | tf_op jit(solution)/shard_map/ppermute | solution.py:426
  70.3 1.1 %multiply_bitcast_fusion = f32[64,4,256]{2,0,1:T(8,128)S(1)} fusion(f32[4,128,256]{2,1,0:T(8,128)} %copy-done.3, bf16[4,64,256]{2,1,0:T(8,128)(2,1)S(1)} %collective-permute-done.8, bf16[4,64,256]{2,1,0:T(8,128)(2,1)S(1)} %collective-permute-done.7, bf16[4,64,256]{2,1,0:T(8,128)(2,1)S(1)} %collective-permute-done.6, f32[4,192,256]{2,1,0:T(8,128)S(1)} %convert_add_fusion, ...), kind=kLoop, calls=%fused_computation.2 | loop fusion | flops 655360 | bytes 1703938 | tf_op jit(solution)/shard_map/transpose | solution.py:435
  71.5 0.9 %copy.7 = f32[64,4,256]{2,1,0:T(4,128)} copy(f32[64,4,256]{2,0,1:T(8,128)S(1)} %multiply_bitcast_fusion) | data formatting | bytes 524288 | tf_op jit(solution)/shard_map/transpose | solution.py:435
  (29 shorter events, 0.4 us)
Async XLA Ops:
  0.0 21.2 %collective-permute-start = (s32[128]{0:T(128)}, s32[128]{0:T(128)S(1)}, u32[]{:S(2)}, u32[]{:S(2)}) collective-permute-start(s32[128]{0:T(128)} %param.8), channel_id=1, source_target_pairs={{0,12},{4,0},{8,4},{12,8},{1,13},{5,1},{9,5},{13,9},{2,14},{6,2},{... | collective-permute-start | bytes 1544 | tf_op jit(solution)/shard_map/ppermute | solution.py:390
  5.8 2.5 %copy-start = (bf16[5,128,4096]{2,1,0:T(8,128)(2,1)S(1)}, bf16[5,128,4096]{2,1,0:T(8,128)(2,1)}, u32[]{:S(2)}) copy-start(bf16[5,128,4096]{2,1,0:T(8,128)(2,1)} %param.6) | copy-start | bytes 15728644
  21.2 8.5 %copy-start.4 = (bf16[5,64,1024]{2,1,0:T(8,128)(2,1)}, bf16[5,64,1024]{2,1,0:T(8,128)(2,1)S(1)}, u32[]{:S(2)}) copy-start(bf16[5,64,1024]{2,1,0:T(8,128)(2,1)S(1)} %get-tuple-element.29.two_ref) | copy-start | bytes 1966084
  21.2 16.3 %collective-permute-start.1 = (bf16[5,64,1024]{2,1,0:T(8,128)(2,1)S(1)}, bf16[5,64,1024]{2,1,0:T(8,128)(2,1)S(1)}, u32[]{:S(2)}, u32[]{:S(2)}) collective-permute-start(bf16[5,64,1024]{2,1,0:T(8,128)(2,1)S(1)} %get-tuple-element.28.one_ref), channel_id=1, source_target_pairs={{0,4},{1,5},{4,0},{5,1},{8,12},{9,13},{12,8},{13,9},{2,6},{3,7},{6... | collective-permute-start | bytes 1966088 | tf_op jit(solution)/shard_map/ppermute | solution.py:339
  21.3 17.0 %collective-permute-start.2 = (bf16[5,64,1024]{2,1,0:T(8,128)(2,1)S(1)}, bf16[5,64,1024]{2,1,0:T(8,128)(2,1)S(1)}, u32[]{:S(2)}, u32[]{:S(2)}) collective-permute-start(bf16[5,64,1024]{2,1,0:T(8,128)(2,1)S(1)} %get-tuple-element.29.two_ref), channel_id=1, source_target_pairs={{0,1},{1,0},{4,8},{5,9},{8,4},{9,5},{12,13},{13,12},{2,3},{3,2},{6... | collective-permute-start | bytes 1966088 | tf_op jit(solution)/shard_map/ppermute | solution.py:339
  21.4 18.7 %copy-start.11 = (s32[4]{0:T(128)S(1)}, s32[4]{0:T(128)}, u32[]{:S(2)}) copy-start(s32[4]{0:T(128)} %param.9) | copy-start | bytes 52
  21.4 18.8 %copy-start.10 = (s32[128]{0:T(128)S(1)}, s32[128]{0:T(128)}, u32[]{:S(2)}) copy-start(s32[128]{0:T(128)} %param.8) | copy-start | bytes 1540
  37.5 0.9 %copy-start.6 = (bf16[5,64,1024]{2,1,0:T(8,128)(2,1)}, bf16[5,64,1024]{2,1,0:T(8,128)(2,1)S(1)}, u32[]{:S(2)}) copy-start(bf16[5,64,1024]{2,1,0:T(8,128)(2,1)S(1)} %collective-permute-done.1.got_one_ref) | copy-start | bytes 1966084
  38.3 0.9 %copy-start.8 = (bf16[5,64,1024]{2,1,0:T(8,128)(2,1)}, bf16[5,64,1024]{2,1,0:T(8,128)(2,1)S(1)}, u32[]{:S(2)}) copy-start(bf16[5,64,1024]{2,1,0:T(8,128)(2,1)S(1)} %collective-permute-done.2.got_two_ref) | copy-start | bytes 1966084
  39.2 15.3 %collective-permute-start.3 = (bf16[5,64,1024]{2,1,0:T(8,128)(2,1)S(1)}, bf16[5,64,1024]{2,1,0:T(8,128)(2,1)S(1)}, u32[]{:S(2)}, u32[]{:S(2)}) collective-permute-start(bf16[5,64,1024]{2,1,0:T(8,128)(2,1)S(1)} %get-tuple-element.30.one_ref), channel_id=1, source_target_pairs={{0,4},{1,5},{4,0},{5,1},{8,12},{9,13},{12,8},{13,9},{2,6},{3,7},{6... | collective-permute-start | bytes 1966088 | tf_op jit(solution)/shard_map/ppermute | solution.py:339
  40.1 14.4 %collective-permute-start.4 = (bf16[5,64,1024]{2,1,0:T(8,128)(2,1)S(1)}, bf16[5,64,1024]{2,1,0:T(8,128)(2,1)S(1)}, u32[]{:S(2)}, u32[]{:S(2)}) collective-permute-start(bf16[5,64,1024]{2,1,0:T(8,128)(2,1)S(1)} %get-tuple-element.31.two_ref), channel_id=1, source_target_pairs={{0,1},{1,0},{4,8},{5,9},{8,4},{9,5},{12,13},{13,12},{2,3},{3,2},{6... | collective-permute-start | bytes 1966088 | tf_op jit(solution)/shard_map/ppermute | solution.py:339
  40.2 2.2 %copy-start.1 = (bf16[2,2048,512]{2,1,0:T(8,128)(2,1)S(1)}, bf16[2,2048,512]{2,1,0:T(8,128)(2,1)}, u32[]{:S(2)}) copy-start(bf16[2,2048,512]{2,1,0:T(8,128)(2,1)} %constant.31.clone.delay_ref) | copy-start | bytes 12582916
  42.4 1.1 %copy-start.5 = (bf16[5,64,1024]{2,1,0:T(8,128)(2,1)S(1)}, bf16[5,64,1024]{2,1,0:T(8,128)(2,1)}, u32[]{:S(2)}) copy-start(bf16[5,64,1024]{2,1,0:T(8,128)(2,1)} %copy-done.4) | copy-start | bytes 1966084
  43.4 1.1 %copy-start.7 = (bf16[5,64,1024]{2,1,0:T(8,128)(2,1)S(1)}, bf16[5,64,1024]{2,1,0:T(8,128)(2,1)}, u32[]{:S(2)}) copy-start(bf16[5,64,1024]{2,1,0:T(8,128)(2,1)} %copy-done.6) | copy-start | bytes 1966084
  44.5 1.1 %copy-start.9 = (bf16[5,64,1024]{2,1,0:T(8,128)(2,1)S(1)}, bf16[5,64,1024]{2,1,0:T(8,128)(2,1)}, u32[]{:S(2)}) copy-start(bf16[5,64,1024]{2,1,0:T(8,128)(2,1)} %copy-done.8) | copy-start | bytes 1966084
  45.6 8.9 %copy-start.2 = (bf16[2,2048,512]{2,1,0:T(8,128)(2,1)S(1)}, bf16[2,2048,512]{2,1,0:T(8,128)(2,1)}, u32[]{:S(2)}) copy-start(bf16[2,2048,512]{2,1,0:T(8,128)(2,1)} %constant.31.clone.delay_ref) | copy-start | bytes 12582916
  50.3 9.6 %copy-start.3 = (f32[4,128,256]{2,1,0:T(8,128)}, f32[4,128,256]{2,1,0:T(8,128)S(1)}, u32[]{:S(2)}) copy-start(f32[4,128,256]{2,1,0:T(8,128)S(1)} %get-tuple-element.38) | copy-start | bytes 1572868
  59.9 1.9 %collective-permute-start.5 = (bf16[4,192,256]{2,1,0:T(8,128)(2,1)}, bf16[4,192,256]{2,1,0:T(8,128)(2,1)S(1)}, u32[]{:S(2)}, u32[]{:S(2)}) collective-permute-start(bf16[4,192,256]{2,1,0:T(8,128)(2,1)} %get-tuple-element.37), channel_id=1, source_target_pairs={{0,1},{1,0},{2,3},{3,2},{4,5},{5,4},{6,7},{7,6},{8,9},{9,8},{10,11... | collective-permute-start | bytes 1179656 | tf_op jit(solution)/shard_map/ppermute | solution.py:418
  61.9 7.5 %collective-permute-start.6 = (bf16[4,64,256]{2,1,0:T(8,128)(2,1)S(1)}, bf16[4,64,256]{2,1,0:T(8,128)(2,1)S(1)}, u32[]{:S(2)}, u32[]{:S(2)}) collective-permute-start(bf16[4,64,256]{2,1,0:T(8,128)(2,1)S(1)} %get-tuple-element.39), channel_id=1, source_target_pairs={{0,2},{2,0},{1,3},{3,1},{4,6},{6,4},{5,7},{7,5},{8,10},{10,8},{9,1... | collective-permute-start | bytes 393224 | tf_op jit(solution)/shard_map/ppermute | solution.py:424
  63.5 6.8 %collective-permute-start.7 = (bf16[4,64,256]{2,1,0:T(8,128)(2,1)S(1)}, bf16[4,64,256]{2,1,0:T(8,128)(2,1)S(1)}, u32[]{:S(2)}, u32[]{:S(2)}) collective-permute-start(bf16[4,64,256]{2,1,0:T(8,128)(2,1)S(1)} %get-tuple-element.40), channel_id=1, source_target_pairs={{2,0},{3,1},{0,4},{1,5},{6,2},{7,3},{4,8},{5,9},{10,6},{11,7},{8,1... | collective-permute-start | bytes 393224 | tf_op jit(solution)/shard_map/ppermute | solution.py:426
  65.2 5.1 %collective-permute-start.8 = (bf16[4,64,256]{2,1,0:T(8,128)(2,1)S(1)}, bf16[4,64,256]{2,1,0:T(8,128)(2,1)S(1)}, u32[]{:S(2)}, u32[]{:S(2)}) collective-permute-start(bf16[4,64,256]{2,1,0:T(8,128)(2,1)S(1)} %get-tuple-element.40), channel_id=1, source_target_pairs={{0,1},{1,0},{2,4},{3,5},{4,2},{5,3},{6,8},{7,9},{8,6},{9,7},{10,12... | collective-permute-start | bytes 393224 | tf_op jit(solution)/shard_map/ppermute | solution.py:427

commit v5 on v4

--- a/solution.py
+++ b/solution.py
@@ -399,8 +399,7 @@
         one, two, *passed = whiten(plan, scalars, operands, fourier, segs, chans)
         operands = operands[:2] + passed
         if groups:
-            send_one, send_two, *earlier = lax.optimization_barrier((one, two, *groups[-1][2:]))
-            groups[-1] = (*groups[-1][:2], *earlier)
+            send_one, send_two = one, two
         else:
             send_one, send_two, next_counts = lax.optimization_barrier((one, two, next_counts))
         got_one, got_two = swap(send_one, 0), swap(send_two, 1)

time: 72.8 us -> 71.6 us (0.984)
  local copies, waits for them, and re-layouts: 10.6 us -> 5.57 us
  Pallas kernels: 31.1 us -> 33 us
  starting transfers between devices: 9.39 us -> 10.6 us
  waiting for transfers between devices: 19 us -> 20 us
    unnamed x24 -> x12, local copies, waits for them, and re-layouts: 9.68 us -> 4.7 us
    ppermute x1, waiting for transfers between devices: 0.95 us -> 4.31 us  [shards(): near = lax.ppermute(back, ('chan', 'seg', 'freq'), route_near)]
    ppermute x1, waiting for transfers between devices: 4.15 us -> 2.01 us  [shards(): other = lax.ppermute(other, 'seg', [(0, 1), (1, 0)])]
    pallas_call x2, Pallas kernels: 10 us -> 11.2 us  [correlate(): pl.pallas_call(functools.partial(correlate_kernel, plan), out_shape=out_s...]
    ppermute x1, starting transfers between devices: 1.56 us -> 0.46 us  [shards(): other = lax.ppermute(other, 'seg', [(0, 1), (1, 0)])]
    ppermute x1, starting transfers between devices: 1.75 us -> 2.81 us  [shards(): near = lax.ppermute(back, ('chan', 'seg', 'freq'), route_near)]
    ppermute x4, starting transfers between devices: 1.02 us -> 2.06 us  [swap(): return lax.ppermute(block, ('chan', 'freq'), route)]
  transfers between devices with their start and end apart: 9 -> 9, of which waited for: 5 -> 5; matrix products, arithmetic and copies ran while one was open for 1% -> 1% of each run, Pallas kernels for 36% -> 39%
where the time goes in v5:
time: 71.6 us; the launch traced here: 71.3 us
  Pallas kernels  33 us (46%)
  waiting for transfers between devices  20 us (28%)
  starting transfers between devices  10.6 us (15%)
  local copies, waits for them, and re-layouts  5.57 us (8%)
  other arithmetic  2.1 us (3%)
    pallas_call x2, Pallas kernels, whiten(): pl.pallas_call(functools.partial(whiten_kernel, plan), out_shape=out_shap...  21.7 us
    ppermute x4, waiting for transfers between devices, swap(): return lax.ppermute(block, ('chan', 'freq'), route)  11.7 us
    pallas_call x2, Pallas kernels, correlate(): pl.pallas_call(functools.partial(correlate_kernel, plan), out_shape=out_s...  11.2 us
    ppermute x1, starting transfers between devices, shards(): lax.ppermute(seg_counts, 'chan', [(i, (i - 1) % blocks) for i in range(bl...  5.05 us
    unnamed x12, local copies, waits for them, and re-layouts  4.7 us
    ppermute x1, waiting for transfers between devices, shards(): near = lax.ppermute(back, ('chan', 'seg', 'freq'), route_near)  4.31 us
    ppermute x1, starting transfers between devices, shards(): near = lax.ppermute(back, ('chan', 'seg', 'freq'), route_near)  2.81 us
    ppermute x4, starting transfers between devices, swap(): return lax.ppermute(block, ('chan', 'freq'), route)  2.06 us
  transfers between devices with their start and end apart: 9, of which 5 were waited for; matrix products, arithmetic and copies ran while one was open for 1% of the time, Pallas kernels for 39%

profile of v5, /device:TPU:0, one launch (start us, length us, event | category | flops | bytes accessed | tf_op | source)
XLA Modules:
  0.0 71.3 jit_solution(4365874287619133129)
XLA Ops:
  0.0 5.0 %collective-permute-start.2 = (s32[128]{0:T(128)}, s32[128]{0:T(128)S(1)}, u32[]{:S(2)}, u32[]{:S(2)}) collective-permute-start(s32[128]{0:T(128)} %param.8), channel_id=1, source_target_pairs={{0,12},{4,0},{8,4},{12,8},{1,13},{5,1},{9,5},{13,9},{2,14},{6,2},{... | collective-permute-start | bytes 1544 | tf_op jit(solution)/shard_map/ppermute | solution.py:390
  5.0 0.7 fusion.1.refs_1_
  5.7 0.1 pad_add_fusion.1.scalars
  5.8 2.5 %copy-done = bf16[5,128,4096]{2,1,0:T(8,128)(2,1)S(1)} copy-done((bf16[5,128,4096]{2,1,0:T(8,128)(2,1)S(1)}, bf16[5,128,4096]{2,1,0:T(8,128)(2,1)}, u32[]{:S(2)}) %copy-start) | copy-done | bytes 5242904
  8.3 13.5 %whiten.2 = (bf16[5,64,1024]{2,1,0:T(8,128)(2,1)S(1)}, bf16[5,64,1024]{2,1,0:T(8,128)(2,1)}, f32[640,256]{1,0:T(8,128)S(1)}, bf16[3,640,128]{2,1,0:T(8,128)(2,1)S(1)}) custom-call(s32[3]{0:T(128)S(1)} %pad_add_fusion.1.scalars, bf16[2,9,4096,256]{3,2,1,0:T(8,128)(2,1)} %constant.30.clone.table_ref, bf16[640,4096]{1,0:T(8,128)(2,1)S(1)} %bitcast.11, ...), custom_call_target="tpu_custom_call" | custom-call | flops 8053063680 | bytes 17825792 | tf_op jit(solution)/shard_map/whiten/pallas_call | solution.py:162
  21.8 0.1 collective-permute-start.4
  21.9 0.0 copy-start.5
  21.9 8.2 %whiten.3 = (bf16[5,64,1024]{2,1,0:T(8,128)(2,1)S(1)}, bf16[5,64,1024]{2,1,0:T(8,128)(2,1)S(1)}) custom-call(s32[3]{0:T(128)S(1)} %pad_add_fusion.1.scalars, bf16[2,9,4096,256]{3,2,1,0:T(8,128)(2,1)} %constant.30.clone.table_ref, bf16[640,4096]{1,0:T(8,128)(2,1)S(1)} %bitcast.12, f32[1,128]{1,0:T(1,128)S(1)} %fusion.1.refs_1_, ...), custom_call_target="tpu_custom_call" | custom-call | flops 4026531840 | bytes 11534336 | tf_op jit(solution)/shard_map/whiten/pallas_call | solution.py:162
  30.2 2.0 %collective-permute-start = (bf16[5,64,1024]{2,1,0:T(8,128)(2,1)S(1)}, bf16[5,64,1024]{2,1,0:T(8,128)(2,1)S(1)}, u32[]{:S(2)}, u32[]{:S(2)}) collective-permute-start(bf16[5,64,1024]{2,1,0:T(8,128)(2,1)S(1)} %get-tuple-element.20.one_ref), channel_id=1, source_target_pairs={{0,4},{1,5},{4,0},{5,1},{8,12},{9,13},{12,8},{13,9},{2,6},{3,7},{6... | collective-permute-start | bytes 1966088 | tf_op jit(solution)/shard_map/ppermute | solution.py:339
  32.2 0.1 pad_add_fusion.scalars
  32.2 7.3 %collective-permute-done.3.got_one_ref = bf16[5,64,1024]{2,1,0:T(8,128)(2,1)} collective-permute-done((bf16[5,64,1024]{2,1,0:T(8,128)(2,1)S(1)}, bf16[5,64,1024]{2,1,0:T(8,128)(2,1)}, u32[]{:S(2)}, u32[]{:S(2)}) %collective-permute-start.3) | collective-permute-done | bytes 655392 | tf_op jit(solution)/shard_map/ppermute | solution.py:339
  39.6 2.2 %copy-done.1 = bf16[2,2048,512]{2,1,0:T(8,128)(2,1)S(1)} copy-done((bf16[2,2048,512]{2,1,0:T(8,128)(2,1)S(1)}, bf16[2,2048,512]{2,1,0:T(8,128)(2,1)}, u32[]{:S(2)}) %copy-start.1) | copy-done | bytes 4194328
  41.8 5.9 %correlate.2 = (f32[512,512]{1,0:T(8,128)S(1)}, f32[4,128,256]{2,1,0:T(8,128)S(1)}) custom-call(s32[7]{0:T(128)S(1)} %pad_add_fusion.scalars, bf16[5,64,1024]{2,1,0:T(8,128)(2,1)S(1)} %get-tuple-element.24.one_ref, bf16[5,64,1024]{2,1,0:T(8,128)(2,1)} %get-tuple-element.25.two_ref, bf16[5,64,1024]{2,1,0:T(8,128)(2,1)} %collective-permute-done.3.got_one_ref, ...), custom_call_target="tpu_custom_call" | custom-call | flops 1879048192 | bytes 2621440 | tf_op jit(solution)/shard_map/correlate/pallas_call | solution.py:308
  47.7 4.4 %collective-permute-done.got_one_ref = bf16[5,64,1024]{2,1,0:T(8,128)(2,1)S(1)} collective-permute-done((bf16[5,64,1024]{2,1,0:T(8,128)(2,1)S(1)}, bf16[5,64,1024]{2,1,0:T(8,128)(2,1)S(1)}, u32[]{:S(2)}, u32[]{:S(2)}) %collective-permute-start) | collective-permute-done | bytes 655392 | tf_op jit(solution)/shard_map/ppermute | solution.py:339
  52.1 5.3 %correlate.3 = (f32[4,192,256]{2,1,0:T(8,128)S(1)}, bf16[4,192,256]{2,1,0:T(8,128)(2,1)}) custom-call(s32[7]{0:T(128)S(1)} %pad_add_fusion.scalars, bf16[5,64,1024]{2,1,0:T(8,128)(2,1)S(1)} %get-tuple-element.20.one_ref, bf16[5,64,1024]{2,1,0:T(8,128)(2,1)S(1)} %get-tuple-element.21.two_ref, bf16[5,64,1024]{2,1,0:T(8,128)(2,1)S(1)} %collective-permute-done.got_one_ref, ...), custom_call_target="tpu_custom_call" | custom-call | flops 1879048192 | bytes 2621440 | tf_op jit(solution)/shard_map/correlate/pallas_call | solution.py:308
  57.4 1.9 %collective-permute-done.5 = bf16[4,192,256]{2,1,0:T(8,128)(2,1)S(1)} collective-permute-done((bf16[4,192,256]{2,1,0:T(8,128)(2,1)}, bf16[4,192,256]{2,1,0:T(8,128)(2,1)S(1)}, u32[]{:S(2)}, u32[]{:S(2)}) %collective-permute-start.5) | collective-permute-done | bytes 393248 | tf_op jit(solution)/shard_map/ppermute | solution.py:417
  59.3 0.1 convert_add_fusion
  59.5 0.2 collective-permute-start.8
  59.7 2.8 %collective-permute-start.7 = (bf16[4,64,256]{2,1,0:T(8,128)(2,1)S(1)}, bf16[4,64,256]{2,1,0:T(8,128)(2,1)S(1)}, u32[]{:S(2)}, u32[]{:S(2)}) collective-permute-start(bf16[4,64,256]{2,1,0:T(8,128)(2,1)S(1)} %get-tuple-element.32), channel_id=1, source_target_pairs={{2,0},{3,1},{0,4},{1,5},{6,2},{7,3},{4,8},{5,9},{10,6},{11,7},{8,1... | collective-permute-start | bytes 393224 | tf_op jit(solution)/shard_map/ppermute | solution.py:425
  62.5 0.5 collective-permute-start.6
  63.0 4.3 %collective-permute-done.7 = bf16[4,64,256]{2,1,0:T(8,128)(2,1)S(1)} collective-permute-done((bf16[4,64,256]{2,1,0:T(8,128)(2,1)S(1)}, bf16[4,64,256]{2,1,0:T(8,128)(2,1)S(1)}, u32[]{:S(2)}, u32[]{:S(2)}) %collective-permute-start.7) | collective-permute-done | bytes 131104 | tf_op jit(solution)/shard_map/ppermute | solution.py:425
  67.3 2.0 %collective-permute-done.6 = bf16[4,64,256]{2,1,0:T(8,128)(2,1)S(1)} collective-permute-done((bf16[4,64,256]{2,1,0:T(8,128)(2,1)S(1)}, bf16[4,64,256]{2,1,0:T(8,128)(2,1)S(1)}, u32[]{:S(2)}, u32[]{:S(2)}) %collective-permute-start.6) | collective-permute-done | bytes 131104 | tf_op jit(solution)/shard_map/ppermute | solution.py:423
  69.3 1.1 %multiply_bitcast_fusion = f32[64,4,256]{2,0,1:T(8,128)S(1)} fusion(f32[4,128,256]{2,1,0:T(8,128)} %copy-done.3, bf16[4,64,256]{2,1,0:T(8,128)(2,1)S(1)} %collective-permute-done.8, bf16[4,64,256]{2,1,0:T(8,128)(2,1)S(1)} %collective-permute-done.7, bf16[4,64,256]{2,1,0:T(8,128)(2,1)S(1)} %collective-permute-done.6, f32[4,192,256]{2,1,0:T(8,128)S(1)} %convert_add_fusion, ...), kind=kLoop, calls=%fused_computation.2 | loop fusion | flops 655360 | bytes 1703938 | tf_op jit(solution)/shard_map/transpose | solution.py:434
  70.4 0.9 %copy.7 = f32[64,4,256]{2,1,0:T(4,128)} copy(f32[64,4,256]{2,0,1:T(8,128)S(1)} %multiply_bitcast_fusion) | data formatting | bytes 524288 | tf_op jit(solution)/shard_map/transpose | solution.py:434
  (17 shorter events, 0.1 us)
Async XLA Ops:
  0.0 21.8 %collective-permute-start.2 = (s32[128]{0:T(128)}, s32[128]{0:T(128)S(1)}, u32[]{:S(2)}, u32[]{:S(2)}) collective-permute-start(s32[128]{0:T(128)} %param.8), channel_id=1, source_target_pairs={{0,12},{4,0},{8,4},{12,8},{1,13},{5,1},{9,5},{13,9},{2,14},{6,2},{... | collective-permute-start | bytes 1544 | tf_op jit(solution)/shard_map/ppermute | solution.py:390
  5.8 2.5 %copy-start = (bf16[5,128,4096]{2,1,0:T(8,128)(2,1)S(1)}, bf16[5,128,4096]{2,1,0:T(8,128)(2,1)}, u32[]{:S(2)}) copy-start(bf16[5,128,4096]{2,1,0:T(8,128)(2,1)} %param.6) | copy-start | bytes 15728644
  21.8 17.8 %collective-permute-start.3 = (bf16[5,64,1024]{2,1,0:T(8,128)(2,1)S(1)}, bf16[5,64,1024]{2,1,0:T(8,128)(2,1)}, u32[]{:S(2)}, u32[]{:S(2)}) collective-permute-start(bf16[5,64,1024]{2,1,0:T(8,128)(2,1)S(1)} %get-tuple-element.24.one_ref), channel_id=1, source_target_pairs={{0,4},{1,5},{4,0},{5,1},{8,12},{9,13},{12,8},{13,9},{2,6},{3,7},{6... | collective-permute-start | bytes 1966088 | tf_op jit(solution)/shard_map/ppermute | solution.py:339
  21.8 17.8 %collective-permute-start.4 = (bf16[5,64,1024]{2,1,0:T(8,128)(2,1)}, bf16[5,64,1024]{2,1,0:T(8,128)(2,1)}, u32[]{:S(2)}, u32[]{:S(2)}) collective-permute-start(bf16[5,64,1024]{2,1,0:T(8,128)(2,1)} %get-tuple-element.25.two_ref), channel_id=1, source_target_pairs={{0,1},{1,0},{4,8},{5,9},{8,4},{9,5},{12,13},{13,12},{2,3},{3,2},{6... | collective-permute-start | bytes 1966088 | tf_op jit(solution)/shard_map/ppermute | solution.py:339
  21.9 10.3 %copy-start.5 = (s32[4]{0:T(128)S(1)}, s32[4]{0:T(128)}, u32[]{:S(2)}) copy-start(s32[4]{0:T(128)} %param.9) | copy-start | bytes 52
  21.9 17.7 %copy-start.4 = (s32[128]{0:T(128)S(1)}, s32[128]{0:T(128)}, u32[]{:S(2)}) copy-start(s32[128]{0:T(128)} %param.8) | copy-start | bytes 1540
  30.2 21.9 %collective-permute-start = (bf16[5,64,1024]{2,1,0:T(8,128)(2,1)S(1)}, bf16[5,64,1024]{2,1,0:T(8,128)(2,1)S(1)}, u32[]{:S(2)}, u32[]{:S(2)}) collective-permute-start(bf16[5,64,1024]{2,1,0:T(8,128)(2,1)S(1)} %get-tuple-element.20.one_ref), channel_id=1, source_target_pairs={{0,4},{1,5},{4,0},{5,1},{8,12},{9,13},{12,8},{13,9},{2,6},{3,7},{6... | collective-permute-start | bytes 1966088 | tf_op jit(solution)/shard_map/ppermute | solution.py:339
  32.2 19.9 %collective-permute-start.1 = (bf16[5,64,1024]{2,1,0:T(8,128)(2,1)S(1)}, bf16[5,64,1024]{2,1,0:T(8,128)(2,1)S(1)}, u32[]{:S(2)}, u32[]{:S(2)}) collective-permute-start(bf16[5,64,1024]{2,1,0:T(8,128)(2,1)S(1)} %get-tuple-element.21.two_ref), channel_id=1, source_target_pairs={{0,1},{1,0},{4,8},{5,9},{8,4},{9,5},{12,13},{13,12},{2,3},{3,2},{6... | collective-permute-start | bytes 1966088 | tf_op jit(solution)/shard_map/ppermute | solution.py:339
  39.6 2.2 %copy-start.1 = (bf16[2,2048,512]{2,1,0:T(8,128)(2,1)S(1)}, bf16[2,2048,512]{2,1,0:T(8,128)(2,1)}, u32[]{:S(2)}) copy-start(bf16[2,2048,512]{2,1,0:T(8,128)(2,1)} %constant.31.clone.delay_ref) | copy-start | bytes 12582916
  41.8 10.3 %copy-start.2 = (bf16[2,2048,512]{2,1,0:T(8,128)(2,1)S(1)}, bf16[2,2048,512]{2,1,0:T(8,128)(2,1)}, u32[]{:S(2)}) copy-start(bf16[2,2048,512]{2,1,0:T(8,128)(2,1)} %constant.31.clone.delay_ref) | copy-start | bytes 12582916
  47.7 9.7 %copy-start.3 = (f32[4,128,256]{2,1,0:T(8,128)}, f32[4,128,256]{2,1,0:T(8,128)S(1)}, u32[]{:S(2)}) copy-start(f32[4,128,256]{2,1,0:T(8,128)S(1)} %get-tuple-element.30) | copy-start | bytes 1572868
  57.4 1.9 %collective-permute-start.5 = (bf16[4,192,256]{2,1,0:T(8,128)(2,1)}, bf16[4,192,256]{2,1,0:T(8,128)(2,1)S(1)}, u32[]{:S(2)}, u32[]{:S(2)}) collective-permute-start(bf16[4,192,256]{2,1,0:T(8,128)(2,1)} %get-tuple-element.29), channel_id=1, source_target_pairs={{0,1},{1,0},{2,3},{3,2},{4,5},{5,4},{6,7},{7,6},{8,9},{9,8},{10,11... | collective-permute-start | bytes 1179656 | tf_op jit(solution)/shard_map/ppermute | solution.py:417
  59.5 3.5 %collective-permute-start.8 = (bf16[4,64,256]{2,1,0:T(8,128)(2,1)S(1)}, bf16[4,64,256]{2,1,0:T(8,128)(2,1)S(1)}, u32[]{:S(2)}, u32[]{:S(2)}) collective-permute-start(bf16[4,64,256]{2,1,0:T(8,128)(2,1)S(1)} %get-tuple-element.32), channel_id=1, source_target_pairs={{0,1},{1,0},{2,4},{3,5},{4,2},{5,3},{6,8},{7,9},{8,6},{9,7},{10,12... | collective-permute-start | bytes 393224 | tf_op jit(solution)/shard_map/ppermute | solution.py:426
  59.7 7.6 %collective-permute-start.7 = (bf16[4,64,256]{2,1,0:T(8,128)(2,1)S(1)}, bf16[4,64,256]{2,1,0:T(8,128)(2,1)S(1)}, u32[]{:S(2)}, u32[]{:S(2)}) collective-permute-start(bf16[4,64,256]{2,1,0:T(8,128)(2,1)S(1)} %get-tuple-element.32), channel_id=1, source_target_pairs={{2,0},{3,1},{0,4},{1,5},{6,2},{7,3},{4,8},{5,9},{10,6},{11,7},{8,1... | collective-permute-start | bytes 393224 | tf_op jit(solution)/shard_map/ppermute | solution.py:425
  62.5 6.8 %collective-permute-start.6 = (bf16[4,64,256]{2,1,0:T(8,128)(2,1)S(1)}, bf16[4,64,256]{2,1,0:T(8,128)(2,1)S(1)}, u32[]{:S(2)}, u32[]{:S(2)}) collective-permute-start(bf16[4,64,256]{2,1,0:T(8,128)(2,1)S(1)} %get-tuple-element.31), channel_id=1, source_target_pairs={{0,2},{2,0},{1,3},{3,1},{4,6},{6,4},{5,7},{7,5},{8,10},{10,8},{9,1... | collective-permute-start | bytes 393224 | tf_op jit(solution)/shard_map/ppermute | solution.py:423

commit v6 on v5

--- a/solution.py
+++ b/solution.py
@@ -16,7 +16,7 @@
 TILE = 128
 EPSILON = 1e-06
 MIB = 1 << 20
-GROUPS = (6, 9)
+GROUPS = (5, 8, 9)
 
 
 def tables(length, parts):
@@ -27,7 +27,7 @@
     cos16 = cosines.astype(np.float32).astype(ml_dtypes.bfloat16)
     sin16 = sines.astype(np.float32).astype(ml_dtypes.bfloat16)
     samples = np.arange(length)[:, None]
-    fourier = np.zeros((parts, tiles + 1, length, 2 * TILE), ml_dtypes.bfloat16)
+    fourier = np.zeros((parts, tiles + 2, length, 2 * TILE), ml_dtypes.bfloat16)
     for part in range(parts):
         for tile in range(tiles + 1):
             first = part * bins_dev + (tile - 1) * TILE
@@ -44,7 +44,7 @@
             fourier[part, tile, :, :TILE] = np.where(keep, cos16[phases], zero)
             fourier[part, tile, :, TILE:] = np.where(keep, sin16[phases], zero)
     lag_part = LAGS // parts
-    delay = np.zeros((parts, 2 * bins_dev, LAGS), ml_dtypes.bfloat16)
+    delay = np.zeros((2 * bins_dev, LAGS), ml_dtypes.bfloat16)
     scaling = 1.0 / math.sqrt(F)
     for part in range(parts):
         shifts = np.roll(np.arange(LAGS), -part * lag_part) - LAGS // 2
@@ -52,9 +52,11 @@
             bin_index = part * bins_dev + tile * TILE + np.arange(TILE)
             phases = bin_index[:, None] * shifts[None, :] % length
             rows = tile * 2 * TILE
-            delay[part, rows : rows + TILE] = (cosines[phases] * scaling).astype(ml_dtypes.bfloat16)
-            delay[part, rows + TILE : rows + 2 * TILE] = (sines[phases] * scaling).astype(ml_dtypes.bfloat16)
-    return fourier, delay
+            delay[rows : rows + TILE] = (cosines[phases] * scaling).astype(ml_dtypes.bfloat16)
+            delay[rows + TILE : rows + 2 * TILE] = (sines[phases] * scaling).astype(ml_dtypes.bfloat16)
+        blocks = delay.reshape(tiles, 2 * TILE, parts, lag_part).transpose(2, 0, 1, 3)
+        fourier[part, tiles + 1, : tiles * parts * 2 * TILE, :lag_part] = blocks.reshape(-1, lag_part)
+    return fourier
 
 
 def whiten_kernel(plan, scalars, table_ref, *refs):
@@ -174,7 +176,7 @@
             out_specs=out_specs,
             scratch_shapes=scratch,
         ),
-        compiler_params=pltpu.CompilerParams(vmem_limit_bytes=36 * MIB),
+        compiler_params=pltpu.CompilerParams(vmem_limit_bytes=24 * MIB),
         cost_estimate=pl.CostEstimate(
             flops=2 * total * length * 2 * TILE * made,
             bytes_accessed=2 * length * 2 * TILE * made + 2 * total * length,
@@ -188,7 +190,7 @@
     return jnp.minimum(chans // 2, chans - offset) // 16 * 16
 
 
-def correlate_kernel(plan, scalars, one_ref, two_ref, got_one_ref, got_two_ref, delay_ref, *refs):
+def correlate_kernel(plan, scalars, one_ref, two_ref, got_one_ref, got_two_ref, table_hbm, *refs):
     tile_first, is_first, is_last = plan
     refs = list(refs)
     if is_first:
@@ -198,133 +200,133 @@
     if is_last:
         keep_ref, send_ref = refs.pop(0), refs.pop(0)
     else:
-        total = refs.pop(0)
+        total_ref = refs.pop(0)
     if is_first:
         inverse_ref = refs.pop(0)
-    if is_last:
-        total = refs.pop(0)
-    select, frame, far, cross = refs
-    step, last = pl.program_id(0), pl.num_programs(0) - 1
-    segs, half, _ = one_ref.shape
+    select, frame, far, cross, delay, sems = refs
+    segs, half, columns = one_ref.shape
+    tiles = columns // (2 * TILE)
     chans = 2 * half
     slots = cross.shape[0] // chans
+    parts, depth, width = delay.shape
+    place, length = table_hbm.shape[1] - 1, table_hbm.shape[2] // parts
     even, known = scalars[1] == 0, scalars[2]
 
-    @pl.when(step == 0)
-    def _():
-        total[...] = jnp.zeros_like(total) if is_first else sum_ref[...]
-        row = lax.broadcasted_iota(jnp.int32, (chans, 2 * chans), 0)
-        column = lax.broadcasted_iota(jnp.int32, (chans, 2 * chans), 1)
+    copies = []
+    for part in range(parts):
+        rows = pl.ds(part * length + tile_first * 2 * TILE, depth)
+        source = table_hbm.at[scalars[0], place, rows, :]
+        copies.append(pltpu.make_async_copy(source, delay.at[part], sems.at[part]))
+        copies[part].start()
+
+    row = lax.broadcasted_iota(jnp.int32, (chans, 2 * chans), 0)
+    column = lax.broadcasted_iota(jnp.int32, (chans, 2 * chans), 1)
+    for slot in range(slots):
+        offset = scalars[3 + slot]
+        match = (column == row + window_start(offset, chans) + offset) & (column < known)
+        select[slot * chans : (slot + 1) * chans] = match.astype(jnp.float32).astype(jnp.bfloat16)
+
+    order = ((one_ref, 2, 1), (two_ref, 1, 2), (got_one_ref, 3, 0), (got_two_ref, 0, 3))
+    for tile in range(tiles):
+        for ref, if_even, if_odd in order:
+            spot = pl.ds(pl.multiple_of(jnp.where(even, if_even * half, if_odd * half), half), half)
+            for seg in range(segs):
+                frame[tile, seg, spot, :] = ref[seg, :, tile * 2 * TILE : (tile + 1) * 2 * TILE]
+        for seg in range(segs):
+            far[tile, seg] = jnp.dot(select[...], frame[tile, seg], preferred_element_type=jnp.float32)
         for slot in range(slots):
-            offset = scalars[3 + slot]
-            match = (column == row + window_start(offset, chans) + offset) & (column < known)
-            select[slot * chans : (slot + 1) * chans] = match.astype(jnp.float32).astype(jnp.bfloat16)
-        if is_first:
-            row = lax.broadcasted_iota(jnp.int32, (chans, chans), 0)
-            column = lax.broadcasted_iota(jnp.int32, (chans, chans), 1)
-            own, following = own_counts[...].astype(jnp.float32), next_counts[...].astype(jnp.float32)
-            mine = jnp.sum(jnp.where(row == column, own, 0.0), axis=1, keepdims=True)
-            for slot in range(slots):
-                target = row + scalars[3 + slot]
-                partner = jnp.where(column == target, own, 0.0) + jnp.where(column + chans == target, following, 0.0)
-                partner = jnp.sum(partner, axis=1, keepdims=True)
-                divisor = jnp.maximum(jnp.minimum(mine, partner), 1.0)
-                inverse_ref[slot] = jnp.broadcast_to(1.0 / divisor, inverse_ref.shape[1:])
-
-    order = ((one_ref, 2, 1), (two_ref, 1, 2), (got_one_ref, 3, 0), (got_two_ref, 0, 3))
-    for ref, if_even, if_odd in order:
-        spot = pl.ds(pl.multiple_of(jnp.where(even, if_even * half, if_odd * half), half), half)
-        for seg in range(segs):
-            frame[seg, spot, :] = ref[seg]
-    for seg in range(segs):
-        far[seg] = jnp.dot(select[...], frame[seg], preferred_element_type=jnp.float32)
-    for slot in range(slots):
-        start = window_start(scalars[3 + slot], chans)
-
-        def rows(index, carry, slot=slot, start=start):
-            real = jnp.zeros((16, TILE), jnp.float32)
-            imag = jnp.zeros((16, TILE), jnp.float32)
-            base = pl.multiple_of(start + index * 16, 16)
-            spot = pl.multiple_of(slot * chans + index * 16, 16)
-            for seg in range(segs):
-                own = frame[seg, pl.ds(base, 16), :].astype(jnp.float32)
-                own_re, own_im = own[:, :TILE], own[:, TILE:]
-                far_re, far_im = far[seg, pl.ds(spot, 16), :TILE], far[seg, pl.ds(spot, 16), TILE:]
-                real += own_re * far_re + own_im * far_im
-                imag += own_im * far_re - own_re * far_im
-            cross[pl.ds(spot, 16), :TILE] = real.astype(jnp.bfloat16)
-            cross[pl.ds(spot, 16), TILE:] = imag.astype(jnp.bfloat16)
-            return carry
-
-        lax.fori_loop(0, chans // 16, rows, 0, unroll=True)
-    total[...] += jnp.dot(cross[...], delay_ref[...], preferred_element_type=jnp.float32)
-
+            start = window_start(scalars[3 + slot], chans)
+            for index in range(chans // 16):
+                real = jnp.zeros((16, TILE), jnp.float32)
+                imag = jnp.zeros((16, TILE), jnp.float32)
+                base = pl.multiple_of(start + index * 16, 16)
+                spot = slice(slot * chans + index * 16, slot * chans + index * 16 + 16)
+                for seg in range(segs):
+                    own = frame[tile, seg, pl.ds(base, 16), :].astype(jnp.float32)
+                    own_re, own_im = own[:, :TILE], own[:, TILE:]
+                    far_re, far_im = far[tile, seg, spot, :TILE], far[tile, seg, spot, TILE:]
+                    real += own_re * far_re + own_im * far_im
+                    imag += own_im * far_re - own_re * far_im
+                lane = tile * 2 * TILE
+                cross[spot, lane : lane + TILE] = real.astype(jnp.bfloat16)
+                cross[spot, lane + TILE : lane + 2 * TILE] = imag.astype(jnp.bfloat16)
+
+    if is_first:
+        row = lax.broadcasted_iota(jnp.int32, (chans, chans), 0)
+        column = lax.broadcasted_iota(jnp.int32, (chans, chans), 1)
+        own, following = own_counts[...].astype(jnp.float32), next_counts[...].astype(jnp.float32)
+        mine = jnp.sum(jnp.where(row == column, own, 0.0), axis=1, keepdims=True)
+        for slot in range(slots):
+            target = row + scalars[3 + slot]
+            partner = jnp.where(column == target, own, 0.0) + jnp.where(column + chans == target, following, 0.0)
+            partner = jnp.sum(partner, axis=1, keepdims=True)
+            divisor = jnp.maximum(jnp.minimum(mine, partner), 1.0)
+            inverse_ref[slot] = jnp.broadcast_to(1.0 / divisor, inverse_ref.shape[1:])
     if is_last:
-
-        @pl.when(step == last)
-        def _():
-            keep = keep_ref.shape[2]
-            keep_ref[...] = jnp.zeros_like(keep_ref)
-            send_ref[...] = jnp.zeros_like(send_ref)
-            for slot in range(slots):
-                start = pl.multiple_of(window_start(scalars[3 + slot], chans), 16)
-                block = total[slot * chans : (slot + 1) * chans]
-                keep_ref[slot, pl.ds(start, chans), :] = block[:, :keep]
-                send_ref[slot, pl.ds(start, chans), :] = block[:, keep:].astype(send_ref.dtype)
-
-
-def correlate(plan, scalars, one, two, got_one, got_two, delay, extra, parts):
+        keep_ref[...] = jnp.zeros_like(keep_ref)
+        send_ref[...] = jnp.zeros_like(send_ref)
+
+    for part in range(parts):
+        copies[part].wait()
+        lanes = slice(part * width, (part + 1) * width)
+        for slot in range(slots):
+            spot = slice(slot * chans, (slot + 1) * chans)
+            term = jnp.dot(cross[spot], delay[part], preferred_element_type=jnp.float32)
+            if not is_first:
+                term += sum_ref[spot, lanes]
+            if not is_last:
+                total_ref[spot, lanes] = term
+                continue
+            rows = pl.ds(pl.multiple_of(window_start(scalars[3 + slot], chans), 16), chans)
+            if part == 0:
+                keep_ref[slot, rows, :] = term
+            else:
+                send_ref[slot, rows, lanes.start - width : lanes.stop - width] = term.astype(send_ref.dtype)
+
+
+def correlate(plan, scalars, one, two, got_one, got_two, table, extra):
     tile_first, is_first, is_last = plan
     segs, half, columns = one.shape
     chans = 2 * half
     tiles = columns // (2 * TILE)
     slots = scalars.shape[0] - 3
-    lags = delay.shape[2]
-    keep = lags // parts
-    spec = pl.BlockSpec((segs, half, 2 * TILE), lambda j, s: (0, 0, j))
-    flat = pl.BlockSpec(memory_space=pltpu.VMEM)
-    vector = pl.BlockSpec((1, chans), lambda j, s: (0, 0))
-    frame = lambda width: pl.BlockSpec((slots, 3 * half, width), lambda j, s: (0, 0, 0))
-    scratch = [
-        pltpu.VMEM((slots * chans, 2 * chans), jnp.bfloat16),
-        pltpu.VMEM((segs, 2 * chans, 2 * TILE), jnp.bfloat16),
-        pltpu.VMEM((segs, slots * chans, 2 * TILE), jnp.float32),
-        pltpu.VMEM((slots * chans, 2 * TILE), jnp.bfloat16),
-    ]
-    out_shape, out_specs = [], []
+    parts, keep = table.shape[0], table.shape[3]
+    lags = parts * keep
+    here = pl.BlockSpec(memory_space=pltpu.VMEM)
     if is_last:
-        out_shape += [
+        out_shape = [
             jax.ShapeDtypeStruct((slots, 3 * half, keep), jnp.float32),
             jax.ShapeDtypeStruct((slots, 3 * half, lags - keep), jnp.bfloat16),
         ]
-        out_specs += [frame(keep), frame(lags - keep)]
-        scratch = [pltpu.VMEM((slots * chans, lags), jnp.float32)] + scratch
     else:
-        out_shape += [jax.ShapeDtypeStruct((slots * chans, lags), jnp.float32)]
-        out_specs += [flat]
+        out_shape = [jax.ShapeDtypeStruct((slots * chans, lags), jnp.float32)]
     if is_first:
         out_shape += [jax.ShapeDtypeStruct((slots, chans, keep), jnp.float32)]
-        out_specs += [flat]
     return pl.pallas_call(
         functools.partial(correlate_kernel, plan),
         out_shape=out_shape,
         grid_spec=pltpu.PrefetchScalarGridSpec(
             num_scalar_prefetch=1,
-            grid=(tiles,),
-            in_specs=[spec, spec, spec, spec]
-            + [pl.BlockSpec((None, 2 * TILE, lags), lambda j, s: (s[0], tile_first + j, 0))]
-            + ([vector, vector] if is_first else [flat]),
-            out_specs=out_specs,
-            scratch_shapes=scratch,
+            grid=(),
+            in_specs=[here] * 4 + [pl.BlockSpec(memory_space=pl.ANY)] + [here] * len(extra),
+            out_specs=[here] * len(out_shape),
+            scratch_shapes=[
+                pltpu.VMEM((slots * chans, 2 * chans), jnp.bfloat16),
+                pltpu.VMEM((tiles, segs, 2 * chans, 2 * TILE), jnp.bfloat16),
+                pltpu.VMEM((tiles, segs, slots * chans, 2 * TILE), jnp.float32),
+                pltpu.VMEM((slots * chans, columns), jnp.bfloat16),
+                pltpu.VMEM((parts, columns, keep), jnp.bfloat16),
+                pltpu.SemaphoreType.DMA((parts,)),
+            ],
         ),
-        compiler_params=pltpu.CompilerParams(vmem_limit_bytes=32 * MIB),
+        compiler_params=pltpu.CompilerParams(vmem_limit_bytes=28 * MIB),
         cost_estimate=pl.CostEstimate(
             flops=tiles * 2 * slots * chans * 2 * TILE * (segs * 2 * chans + lags),
             bytes_accessed=tiles * (4 * segs * half * 2 * TILE * 2),
             transcendentals=0,
         ),
         name="correlate",
-    )(scalars, one, two, got_one, got_two, delay, *extra)
+    )(scalars, one, two, got_one, got_two, table, *extra)
 
 
 def swap(block, first):
@@ -379,16 +381,16 @@
     half = chans // 2
     parts, spans, blocks = lax.axis_size("freq"), lax.axis_size("seg"), lax.axis_size("chan")
     assert parts == 2
-    fourier, delay = (jnp.asarray(table) for table in tables(length, parts))
-    tiles = fourier.shape[1] - 1
+    table = jnp.asarray(tables(length, parts))
+    tiles = table.shape[1] - 2
     part = lax.axis_index("freq").astype(jnp.int32)
     span = lax.axis_index("seg").astype(jnp.int32)
     place = lax.axis_index("chan").astype(jnp.int32)
     has_next = place < blocks - 1
     counts = seg_counts.reshape(1, chans)
     limits = jnp.where(dead_mask > 0, seg_counts, 0).astype(jnp.float32).reshape(1, chans)
-    next_counts = lax.ppermute(seg_counts, "chan", [(i, (i - 1) % blocks) for i in range(blocks)]).reshape(1, chans)
     parity = place & 1
+    next_counts = swap(seg_counts, 0), swap(seg_counts, 1)
     scalars = jnp.stack([part, span * segs, parity])
     known = jnp.where(has_next, 4 * half, 3 * half)
     settings = jnp.concatenate([jnp.stack([part, parity, known]), offsets])
@@ -396,19 +398,20 @@
     groups, operands, made = [], [traces.reshape(segs * chans, length), limits], 0
     for stop in GROUPS:
         plan = ((made, stop), (max(made - 1, 1), stop - 1 if stop <= tiles else tiles + 1), tiles)
-        one, two, *passed = whiten(plan, scalars, operands, fourier, segs, chans)
+        one, two, *passed = whiten(plan, scalars, operands, table, segs, chans)
         operands = operands[:2] + passed
         if groups:
             send_one, send_two = one, two
         else:
             send_one, send_two, next_counts = lax.optimization_barrier((one, two, next_counts))
+            next_counts = jnp.where(parity == 0, *next_counts).reshape(1, chans)
         got_one, got_two = swap(send_one, 0), swap(send_two, 1)
         groups.append((one, two, got_one, got_two))
         made = stop
     extra, tile_first = [counts, next_counts], 0
     for index, group in enumerate(groups):
         plan = (tile_first, index == 0, index == len(groups) - 1)
-        results = list(correlate(plan, settings, *group, delay, extra, parts))
+        results = list(correlate(plan, settings, *group, table, extra))
         if index == 0:
             inverse = results.pop()
         extra = results

time: 71.6 us -> 65.7 us (0.918)
  waiting for transfers between devices: 20 us -> 7.78 us
  Pallas kernels: 33 us -> 38.5 us
  starting transfers between devices: 10.6 us -> 12.7 us
  other arithmetic: 2.1 us -> 1.07 us
    ppermute x4 -> x8, waiting for transfers between devices: 11.7 us -> 1.63 us  [swap(): return lax.ppermute(block, ('chan', 'freq'), route)]
    ppermute x4 -> x8, starting transfers between devices: 2.06 us -> 8.51 us  [swap(): return lax.ppermute(block, ('chan', 'freq'), route)]
    ppermute x1 -> x0, starting transfers between devices: 5.05 us -> none  [shards(): lax.ppermute(seg_counts, 'chan', [(i, (i - 1) % blocks) for i in range(bl...]
    pallas_call x2 -> x3, Pallas kernels: 11.2 us -> 14.2 us  [correlate(): pl.pallas_call(functools.partial(correlate_kernel, plan), out_shape=out_s...]
    pallas_call x2 -> x3, Pallas kernels: 21.7 us -> 24.3 us  [whiten(): pl.pallas_call(functools.partial(whiten_kernel, plan), out_shape=out_shap...]
    ppermute x1, waiting for transfers between devices: 4.31 us -> 2.25 us  [shards(): near = lax.ppermute(back, ('chan', 'seg', 'freq'), route_near)]
    ppermute x1, starting transfers between devices: 0.46 us -> 2.42 us  [shards(): other = lax.ppermute(other, 'seg', [(0, 1), (1, 0)])]
    ppermute x1, starting transfers between devices: 2.81 us -> 1.69 us  [shards(): near = lax.ppermute(back, ('chan', 'seg', 'freq'), route_near)]
  transfers between devices with their start and end apart: 9 -> 12, of which waited for: 5 -> 5; matrix products, arithmetic and copies ran while one was open for 1% -> 1% of each run, Pallas kernels for 39% -> 52%
where the time goes in v6:
time: 65.7 us; the launch traced here: 65.3 us
  Pallas kernels  38.5 us (59%)
  starting transfers between devices  12.7 us (19%)
  waiting for transfers between devices  7.78 us (12%)
  local copies, waits for them, and re-layouts  5.21 us (8%)
  other arithmetic  1.07 us (2%)
    pallas_call x3, Pallas kernels, whiten(): pl.pallas_call(functools.partial(whiten_kernel, plan), out_shape=out_shap...  24.3 us
    pallas_call x3, Pallas kernels, correlate(): pl.pallas_call(functools.partial(correlate_kernel, plan), out_shape=out_s...  14.2 us
    ppermute x8, starting transfers between devices, swap(): return lax.ppermute(block, ('chan', 'freq'), route)  8.51 us
    unnamed x10, local copies, waits for them, and re-layouts  4.33 us
    ppermute x1, starting transfers between devices, shards(): other = lax.ppermute(other, 'seg', [(0, 1), (1, 0)])  2.42 us
    ppermute x1, waiting for transfers between devices, shards(): near = lax.ppermute(back, ('chan', 'seg', 'freq'), route_near)  2.25 us
    ppermute x1, waiting for transfers between devices, shards(): other = lax.ppermute(other, 'seg', [(0, 1), (1, 0)])  2.2 us
    ppermute x1, waiting for transfers between devices, shards(): lax.ppermute(send, 'freq', [(0, 1), (1, 0)]).astype(jnp.float32)  1.7 us
  transfers between devices with their start and end apart: 12, of which 5 were waited for; matrix products, arithmetic and copies ran while one was open for 1% of the time, Pallas kernels for 52%

profile of v6, /device:TPU:0, one launch (start us, length us, event | category | flops | bytes accessed | tf_op | source)
XLA Modules:
  0.0 65.3 jit_solution(16161812457278115962)
XLA Ops:
  0.0 3.0 %collective-permute-start.4 = (s32[128]{0:T(128)}, s32[128]{0:T(128)S(1)}, u32[]{:S(2)}, u32[]{:S(2)}) collective-permute-start(s32[128]{0:T(128)} %param.7), channel_id=1, source_target_pairs={{0,4},{1,5},{4,0},{5,1},{8,12},{9,13},{12,8},{13,9},{2,6},{3,7},{6... | collective-permute-start | bytes 1544 | tf_op jit(solution)/shard_map/ppermute | solution.py:341
  3.0 0.7 %fusion.2.refs_1_ = f32[1,128]{1,0:T(1,128)S(1)} fusion(s32[128]{0:T(128)} %param.7, s32[128]{0:T(128)} %param.6), kind=kLoop, calls=%fused_computation.8 | loop fusion | flops 384 | bytes 1536 | tf_op jit(solution)/shard_map/reshape | solution.py:391
  3.8 2.5 %copy-done = bf16[5,128,4096]{2,1,0:T(8,128)(2,1)S(1)} copy-done((bf16[5,128,4096]{2,1,0:T(8,128)(2,1)S(1)}, bf16[5,128,4096]{2,1,0:T(8,128)(2,1)}, u32[]{:S(2)}) %copy-start) | copy-done | bytes 5242904
  6.3 11.1 %whiten.3 = (bf16[5,64,768]{2,1,0:T(8,128)(2,1)S(1)}, bf16[5,64,768]{2,1,0:T(8,128)(2,1)S(1)}, f32[640,256]{1,0:T(8,128)S(1)}, bf16[3,640,128]{2,1,0:T(8,128)(2,1)S(1)}) custom-call(s32[3]{0:T(128)S(1)} %pad_add_fusion.1.scalars, bf16[2,10,4096,256]{3,2,1,0:T(8,128)(2,1)} %constant.28.clone.table_ref.table_hbm, bf16[640,4096]{1,0:T(8,128)(2,1)S(1)} %bitcast.12, ...), custom_call_target="tpu_custom_call" | custom-call | flops 6710886400 | bytes 15728640 | tf_op jit(solution)/shard_map/whiten/pallas_call | solution.py:164
  17.4 3.2 %collective-permute-start.6 = (bf16[5,64,768]{2,1,0:T(8,128)(2,1)S(1)}, bf16[5,64,768]{2,1,0:T(8,128)(2,1)S(1)}, u32[]{:S(2)}, u32[]{:S(2)}) collective-permute-start(bf16[5,64,768]{2,1,0:T(8,128)(2,1)S(1)} %get-tuple-element.33.one_ref), channel_id=1, source_target_pairs={{0,4},{1,5},{4,0},{5,1},{8,12},{9,13},{12,8},{13,9},{2,6},{3,7},{6... | collective-permute-start | bytes 1474568 | tf_op jit(solution)/shard_map/ppermute | solution.py:341
  20.6 7.9 %whiten.4 = (bf16[5,64,768]{2,1,0:T(8,128)(2,1)S(1)}, bf16[5,64,768]{2,1,0:T(8,128)(2,1)S(1)}, f32[640,256]{1,0:T(8,128)S(1)}, bf16[3,640,128]{2,1,0:T(8,128)(2,1)S(1)}) custom-call(s32[3]{0:T(128)S(1)} %pad_add_fusion.1.scalars, bf16[2,10,4096,256]{3,2,1,0:T(8,128)(2,1)} %constant.28.clone.table_ref.table_hbm, bf16[640,4096]{1,0:T(8,128)(2,1)S(1)} %bitcast.13, ...), custom_call_target="tpu_custom_call" | custom-call | flops 4026531840 | bytes 11534336 | tf_op jit(solution)/shard_map/whiten/pallas_call | solution.py:164
  28.5 0.5 collective-permute-start.2
  29.0 0.1 collective-permute-start.3
  29.2 5.3 %whiten.5 = (bf16[5,64,512]{2,1,0:T(8,128)(2,1)}, bf16[5,64,512]{2,1,0:T(8,128)(2,1)}) custom-call(s32[3]{0:T(128)S(1)} %pad_add_fusion.1.scalars, bf16[2,10,4096,256]{3,2,1,0:T(8,128)(2,1)} %constant.28.clone.table_ref.table_hbm, bf16[640,4096]{1,0:T(8,128)(2,1)S(1)} %bitcast.14, f32[1,128]{1,0:T(1,128)S(1)} %fusion.2.refs_1_, ...), custom_call_target="tpu_custom_call" | custom-call | flops 1342177280 | bytes 7340032 | tf_op jit(solution)/shard_map/whiten/pallas_call | solution.py:164
  34.5 1.6 %collective-permute-start = (bf16[5,64,512]{2,1,0:T(8,128)(2,1)}, bf16[5,64,512]{2,1,0:T(8,128)(2,1)}, u32[]{:S(2)}, u32[]{:S(2)}) collective-permute-start(bf16[5,64,512]{2,1,0:T(8,128)(2,1)} %get-tuple-element.27.one_ref), channel_id=1, source_target_pairs={{0,4},{1,5},{4,0},{5,1},{8,12},{9,13},{12,8},{13,9},{2,6},{3,7},{6... | collective-permute-start | bytes 983048 | tf_op jit(solution)/shard_map/ppermute | solution.py:341
  36.2 0.8 %copy-done.1 = bf16[5,64,768]{2,1,0:T(8,128)(2,1)} copy-done((bf16[5,64,768]{2,1,0:T(8,128)(2,1)}, bf16[5,64,768]{2,1,0:T(8,128)(2,1)S(1)}, u32[]{:S(2)}) %copy-start.1) | copy-done | bytes 491544
  37.0 1.0 %copy-done.2 = bf16[5,64,768]{2,1,0:T(8,128)(2,1)S(1)} copy-done((bf16[5,64,768]{2,1,0:T(8,128)(2,1)S(1)}, bf16[5,64,768]{2,1,0:T(8,128)(2,1)}, u32[]{:S(2)}) %copy-start.2) | copy-done | bytes 491544
  38.0 4.3 %correlate.3 = (f32[512,512]{1,0:T(8,128)S(1)}, f32[4,128,256]{2,1,0:T(8,128)S(1)}) custom-call(s32[7]{0:T(128)S(1)} %pad_add_fusion.scalars, bf16[5,64,768]{2,1,0:T(8,128)(2,1)S(1)} %get-tuple-element.33.one_ref, bf16[5,64,768]{2,1,0:T(8,128)(2,1)S(1)} %get-tuple-element.34.two_ref, bf16[5,64,768]{2,1,0:T(8,128)(2,1)S(1)} %collective-permute-done.6.got_one_ref, ...), custom_call_target="tpu_custom_call" | custom-call | flops 1409286144 | bytes 1966080 | tf_op jit(solution)/shard_map/correlate/pallas_call | solution.py:305
  42.3 0.4 collective-permute-done.2.got_one_ref
  42.7 5.4 %correlate.4.refs_0_ = f32[512,512]{1,0:T(8,128)S(1)} custom-call(s32[7]{0:T(128)S(1)} %pad_add_fusion.scalars, bf16[5,64,768]{2,1,0:T(8,128)(2,1)S(1)} %get-tuple-element.29.one_ref, bf16[5,64,768]{2,1,0:T(8,128)(2,1)S(1)} %get-tuple-element.30.two_ref, bf16[5,64,768]{2,1,0:T(8,128)(2,1)} %collective-permute-done.2.got_one_ref, ...), custom_call_target="tpu_custom_call" | custom-call | flops 1409286144 | bytes 1966080 | tf_op jit(solution)/shard_map/correlate/pallas_call | solution.py:305
  48.1 1.3 %collective-permute-done.got_one_ref = bf16[5,64,512]{2,1,0:T(8,128)(2,1)} collective-permute-done((bf16[5,64,512]{2,1,0:T(8,128)(2,1)}, bf16[5,64,512]{2,1,0:T(8,128)(2,1)}, u32[]{:S(2)}, u32[]{:S(2)}) %collective-permute-start) | collective-permute-done | bytes 327712 | tf_op jit(solution)/shard_map/ppermute | solution.py:341
  49.3 4.5 %correlate.5 = (f32[4,192,256]{2,1,0:T(8,128)S(1)}, bf16[4,192,256]{2,1,0:T(8,128)(2,1)S(1)}) custom-call(s32[7]{0:T(128)S(1)} %pad_add_fusion.scalars, bf16[5,64,512]{2,1,0:T(8,128)(2,1)} %get-tuple-element.27.one_ref, bf16[5,64,512]{2,1,0:T(8,128)(2,1)} %get-tuple-element.28.two_ref, bf16[5,64,512]{2,1,0:T(8,128)(2,1)} %collective-permute-done.got_one_ref, ...), custom_call_target="tpu_custom_call" | custom-call | flops 939524096 | bytes 1310720 | tf_op jit(solution)/shard_map/correlate/pallas_call | solution.py:305
  54.0 1.7 %collective-permute-done.8 = bf16[4,192,256]{2,1,0:T(8,128)(2,1)S(1)} collective-permute-done((bf16[4,192,256]{2,1,0:T(8,128)(2,1)S(1)}, bf16[4,192,256]{2,1,0:T(8,128)(2,1)S(1)}, u32[]{:S(2)}, u32[]{:S(2)}) %collective-permute-start.8) | collective-permute-done | bytes 393248 | tf_op jit(solution)/shard_map/ppermute | solution.py:420
  55.8 1.7 %collective-permute-start.10 = (bf16[4,64,256]{2,1,0:T(8,128)(2,1)S(1)}, bf16[4,64,256]{2,1,0:T(8,128)(2,1)S(1)}, u32[]{:S(2)}, u32[]{:S(2)}) collective-permute-start(bf16[4,64,256]{2,1,0:T(8,128)(2,1)S(1)} %get-tuple-element.42), channel_id=1, source_target_pairs={{2,0},{3,1},{0,4},{1,5},{6,2},{7,3},{4,8},{5,9},{10,6},{11,7},{8,1... | collective-permute-start | bytes 393224 | tf_op jit(solution)/shard_map/ppermute | solution.py:428
  57.5 2.4 %collective-permute-start.9 = (bf16[4,64,256]{2,1,0:T(8,128)(2,1)S(1)}, bf16[4,64,256]{2,1,0:T(8,128)(2,1)S(1)}, u32[]{:S(2)}, u32[]{:S(2)}) collective-permute-start(bf16[4,64,256]{2,1,0:T(8,128)(2,1)S(1)} %get-tuple-element.41), channel_id=1, source_target_pairs={{0,2},{2,0},{1,3},{3,1},{4,6},{6,4},{5,7},{7,5},{8,10},{10,8},{9,1... | collective-permute-start | bytes 393224 | tf_op jit(solution)/shard_map/ppermute | solution.py:426
  59.9 2.3 %collective-permute-done.10 = bf16[4,64,256]{2,1,0:T(8,128)(2,1)S(1)} collective-permute-done((bf16[4,64,256]{2,1,0:T(8,128)(2,1)S(1)}, bf16[4,64,256]{2,1,0:T(8,128)(2,1)S(1)}, u32[]{:S(2)}, u32[]{:S(2)}) %collective-permute-start.10) | collective-permute-done | bytes 131104 | tf_op jit(solution)/shard_map/ppermute | solution.py:428
  62.2 2.2 %collective-permute-done.9 = bf16[4,64,256]{2,1,0:T(8,128)(2,1)S(1)} collective-permute-done((bf16[4,64,256]{2,1,0:T(8,128)(2,1)S(1)}, bf16[4,64,256]{2,1,0:T(8,128)(2,1)S(1)}, u32[]{:S(2)}, u32[]{:S(2)}) %collective-permute-start.9) | collective-permute-done | bytes 131104 | tf_op jit(solution)/shard_map/ppermute | solution.py:426
  64.4 0.1 multiply_bitcast_fusion
  64.5 0.9 %copy.6 = f32[64,4,256]{2,1,0:T(4,128)} copy(f32[64,4,256]{2,0,1:T(8,128)S(1)} %multiply_bitcast_fusion) | data formatting | bytes 524288 | tf_op jit(solution)/shard_map/transpose | solution.py:437
  (24 shorter events, 0.4 us)
Async XLA Ops:
  0.0 17.4 %collective-permute-start.4 = (s32[128]{0:T(128)}, s32[128]{0:T(128)S(1)}, u32[]{:S(2)}, u32[]{:S(2)}) collective-permute-start(s32[128]{0:T(128)} %param.7), channel_id=1, source_target_pairs={{0,4},{1,5},{4,0},{5,1},{8,12},{9,13},{12,8},{13,9},{2,6},{3,7},{6... | collective-permute-start | bytes 1544 | tf_op jit(solution)/shard_map/ppermute | solution.py:341
  3.0 14.3 %collective-permute-start.5 = (s32[128]{0:T(128)}, s32[128]{0:T(128)S(1)}, u32[]{:S(2)}, u32[]{:S(2)}) collective-permute-start(s32[128]{0:T(128)} %param.7), channel_id=1, source_target_pairs={{0,1},{1,0},{4,8},{5,9},{8,4},{9,5},{12,13},{13,12},{2,3},{3,2},{6... | collective-permute-start | bytes 1544 | tf_op jit(solution)/shard_map/ppermute | solution.py:341
  3.8 2.5 %copy-start = (bf16[5,128,4096]{2,1,0:T(8,128)(2,1)S(1)}, bf16[5,128,4096]{2,1,0:T(8,128)(2,1)}, u32[]{:S(2)}) copy-start(bf16[5,128,4096]{2,1,0:T(8,128)(2,1)} %param.5) | copy-start | bytes 15728644
  17.4 18.8 %collective-permute-start.6 = (bf16[5,64,768]{2,1,0:T(8,128)(2,1)S(1)}, bf16[5,64,768]{2,1,0:T(8,128)(2,1)S(1)}, u32[]{:S(2)}, u32[]{:S(2)}) collective-permute-start(bf16[5,64,768]{2,1,0:T(8,128)(2,1)S(1)} %get-tuple-element.33.one_ref), channel_id=1, source_target_pairs={{0,4},{1,5},{4,0},{5,1},{8,12},{9,13},{12,8},{13,9},{2,6},{3,7},{6... | collective-permute-start | bytes 1474568 | tf_op jit(solution)/shard_map/ppermute | solution.py:341
  20.6 15.6 %collective-permute-start.7 = (bf16[5,64,768]{2,1,0:T(8,128)(2,1)S(1)}, bf16[5,64,768]{2,1,0:T(8,128)(2,1)S(1)}, u32[]{:S(2)}, u32[]{:S(2)}) collective-permute-start(bf16[5,64,768]{2,1,0:T(8,128)(2,1)S(1)} %get-tuple-element.34.two_ref), channel_id=1, source_target_pairs={{0,1},{1,0},{4,8},{5,9},{8,4},{9,5},{12,13},{13,12},{2,3},{3,2},{6... | collective-permute-start | bytes 1474568 | tf_op jit(solution)/shard_map/ppermute | solution.py:341
  20.6 15.5 %copy-start.4 = (s32[4]{0:T(128)S(1)}, s32[4]{0:T(128)}, u32[]{:S(2)}) copy-start(s32[4]{0:T(128)} %param.8) | copy-start | bytes 52
  20.6 16.4 %copy-start.3 = (s32[128]{0:T(128)S(1)}, s32[128]{0:T(128)}, u32[]{:S(2)}) copy-start(s32[128]{0:T(128)} %param.7) | copy-start | bytes 1540
  28.5 14.2 %collective-permute-start.2 = (bf16[5,64,768]{2,1,0:T(8,128)(2,1)S(1)}, bf16[5,64,768]{2,1,0:T(8,128)(2,1)}, u32[]{:S(2)}, u32[]{:S(2)}) collective-permute-start(bf16[5,64,768]{2,1,0:T(8,128)(2,1)S(1)} %get-tuple-element.29.one_ref), channel_id=1, source_target_pairs={{0,4},{1,5},{4,0},{5,1},{8,12},{9,13},{12,8},{13,9},{2,6},{3,7},{6... | collective-permute-start | bytes 1474568 | tf_op jit(solution)/shard_map/ppermute | solution.py:341
  29.0 13.7 %collective-permute-start.3 = (bf16[5,64,768]{2,1,0:T(8,128)(2,1)S(1)}, bf16[5,64,768]{2,1,0:T(8,128)(2,1)}, u32[]{:S(2)}, u32[]{:S(2)}) collective-permute-start(bf16[5,64,768]{2,1,0:T(8,128)(2,1)S(1)} %get-tuple-element.30.two_ref), channel_id=1, source_target_pairs={{0,1},{1,0},{4,8},{5,9},{8,4},{9,5},{12,13},{13,12},{2,3},{3,2},{6... | collective-permute-start | bytes 1474568 | tf_op jit(solution)/shard_map/ppermute | solution.py:341
  34.5 14.9 %collective-permute-start = (bf16[5,64,512]{2,1,0:T(8,128)(2,1)}, bf16[5,64,512]{2,1,0:T(8,128)(2,1)}, u32[]{:S(2)}, u32[]{:S(2)}) collective-permute-start(bf16[5,64,512]{2,1,0:T(8,128)(2,1)} %get-tuple-element.27.one_ref), channel_id=1, source_target_pairs={{0,4},{1,5},{4,0},{5,1},{8,12},{9,13},{12,8},{13,9},{2,6},{3,7},{6... | collective-permute-start | bytes 983048 | tf_op jit(solution)/shard_map/ppermute | solution.py:341
  36.1 13.2 %collective-permute-start.1 = (bf16[5,64,512]{2,1,0:T(8,128)(2,1)}, bf16[5,64,512]{2,1,0:T(8,128)(2,1)S(1)}, u32[]{:S(2)}, u32[]{:S(2)}) collective-permute-start(bf16[5,64,512]{2,1,0:T(8,128)(2,1)} %get-tuple-element.28.two_ref), channel_id=1, source_target_pairs={{0,1},{1,0},{4,8},{5,9},{8,4},{9,5},{12,13},{13,12},{2,3},{3,2},{6... | collective-permute-start | bytes 983048 | tf_op jit(solution)/shard_map/ppermute | solution.py:341
  36.2 0.8 %copy-start.1 = (bf16[5,64,768]{2,1,0:T(8,128)(2,1)}, bf16[5,64,768]{2,1,0:T(8,128)(2,1)S(1)}, u32[]{:S(2)}) copy-start(bf16[5,64,768]{2,1,0:T(8,128)(2,1)S(1)} %collective-permute-done.7.got_two_ref) | copy-start | bytes 1474564
  37.0 1.0 %copy-start.2 = (bf16[5,64,768]{2,1,0:T(8,128)(2,1)S(1)}, bf16[5,64,768]{2,1,0:T(8,128)(2,1)}, u32[]{:S(2)}) copy-start(bf16[5,64,768]{2,1,0:T(8,128)(2,1)} %copy-done.1) | copy-start | bytes 1474564
  53.9 1.8 %collective-permute-start.8 = (bf16[4,192,256]{2,1,0:T(8,128)(2,1)S(1)}, bf16[4,192,256]{2,1,0:T(8,128)(2,1)S(1)}, u32[]{:S(2)}, u32[]{:S(2)}) collective-permute-start(bf16[4,192,256]{2,1,0:T(8,128)(2,1)S(1)} %get-tuple-element.39), channel_id=1, source_target_pairs={{0,1},{1,0},{2,3},{3,2},{4,5},{5,4},{6,7},{7,6},{8,9},{9,8},{10,11... | collective-permute-start | bytes 1179656 | tf_op jit(solution)/shard_map/ppermute | solution.py:420
  55.8 6.4 %collective-permute-start.10 = (bf16[4,64,256]{2,1,0:T(8,128)(2,1)S(1)}, bf16[4,64,256]{2,1,0:T(8,128)(2,1)S(1)}, u32[]{:S(2)}, u32[]{:S(2)}) collective-permute-start(bf16[4,64,256]{2,1,0:T(8,128)(2,1)S(1)} %get-tuple-element.42), channel_id=1, source_target_pairs={{2,0},{3,1},{0,4},{1,5},{6,2},{7,3},{4,8},{5,9},{10,6},{11,7},{8,1... | collective-permute-start | bytes 393224 | tf_op jit(solution)/shard_map/ppermute | solution.py:428
  57.5 4.7 %collective-permute-start.11 = (bf16[4,64,256]{2,1,0:T(8,128)(2,1)S(1)}, bf16[4,64,256]{2,1,0:T(8,128)(2,1)S(1)}, u32[]{:S(2)}, u32[]{:S(2)}) collective-permute-start(bf16[4,64,256]{2,1,0:T(8,128)(2,1)S(1)} %get-tuple-element.42), channel_id=1, source_target_pairs={{0,1},{1,0},{2,4},{3,5},{4,2},{5,3},{6,8},{7,9},{8,6},{9,7},{10,12... | collective-permute-start | bytes 393224 | tf_op jit(solution)/shard_map/ppermute | solution.py:429
  57.5 6.9 %collective-permute-start.9 = (bf16[4,64,256]{2,1,0:T(8,128)(2,1)S(1)}, bf16[4,64,256]{2,1,0:T(8,128)(2,1)S(1)}, u32[]{:S(2)}, u32[]{:S(2)}) collective-permute-start(bf16[4,64,256]{2,1,0:T(8,128)(2,1)S(1)} %get-tuple-element.41), channel_id=1, source_target_pairs={{0,2},{2,0},{1,3},{3,1},{4,6},{6,4},{5,7},{7,5},{8,10},{10,8},{9,1... | collective-permute-start | bytes 393224 | tf_op jit(solution)/shard_map/ppermute | solution.py:426

commit v7 on v6

v7 whole, which is shorter than its diff:
```python
import functools
import math

import jax
import jax.numpy as jnp
import numpy as np
from jax import lax
from jax.experimental import pallas as pl
from jax.experimental.pallas import tpu as pltpu
from jax.sharding import PartitionSpec as P
import ml_dtypes

HALF = 32
LAGS = 512
F = 2048
TILE = 128
EPSILON = 1e-06
MIB = 1 << 20
EXTRA = 16
LAG_TILES = 4
GROUPS = (4, 7, 9)
AHEAD = (5, 8, 9)


def tables(length, parts):
    bins_dev = F // parts
    tiles = bins_dev // TILE
    cosines = np.cos(np.arange(length) * (2.0 * math.pi / length))
    sines = -np.sin(np.arange(length) * (2.0 * math.pi / length))
    cos16 = cosines.astype(np.float32).astype(ml_dtypes.bfloat16)
    sin16 = sines.astype(np.float32).astype(ml_dtypes.bfloat16)
    samples = np.arange(length)[:, None]
    fourier = np.zeros((parts, tiles + 2, length, 2 * TILE), ml_dtypes.bfloat16)
    lag_part = LAGS // parts
    delay = np.zeros((2 * bins_dev, LAGS), ml_dtypes.bfloat16)
    scaling = 1.0 / math.sqrt(F)
    for part in range(parts):
        shifts = np.roll(np.arange(LAGS), -part * lag_part) - LAGS // 2
        for tile in range(tiles + 1):
            place = tile * TILE + np.arange(TILE)
            bin_index = F - 1 - place if part else place
            phases = samples * bin_index[None, :] % length
            width = TILE if tile < tiles else HALF
            fourier[part, tile, :, :width] = cos16[phases[:, :width]]
            fourier[part, tile, :, TILE : TILE + width] = sin16[phases[:, :width]]
            if tile < tiles:
                phases = bin_index[:, None] * shifts[None, :] % length
                rows = tile * 2 * TILE
                delay[rows : rows + TILE] = (cosines[phases] * scaling).astype(ml_dtypes.bfloat16)
                delay[rows + TILE : rows + 2 * TILE] = (sines[phases] * scaling).astype(ml_dtypes.bfloat16)
        blocks = delay.reshape(tiles, 2 * TILE, parts, lag_part).transpose(2, 0, 1, 3)
        fourier[part, tiles + 1, : tiles * parts * 2 * TILE, :lag_part] = blocks.reshape(-1, lag_part)
    return fourier


def whiten_kernel(plan, names, *refs):
    first, stop, further, tiles = plan
    refs = dict(zip(names, refs))
    x, counts, table_hbm = refs["x"], refs["counts"], refs["table"]
    one_ref, two_ref, eff, band, sems = (refs[name] for name in ("one", "two", "eff", "band", "sems"))
    chans = eff.shape[0]
    total, length = x.shape
    segs, half = total // chans, chans // 2
    even = lax.axis_index("chan") & 1 == 0
    buffers, had = refs.get("buffers"), first + (refs["table_in"].shape[0] if first else 0)

    def fetch(tile):
        source = table_hbm.at[lax.axis_index("freq"), tile]
        target = refs["table_out"].at[tile - stop] if tile >= stop else buffers.at[tile - had]
        return pltpu.make_async_copy(source, target, sems.at[tile - first])

    def table_of(tile):
        return refs["table_in"].at[tile - first] if tile < had else buffers.at[tile - had]

    def spectrum_of(tile):
        if tile < first:
            return refs["spectrum_in"]
        return refs["spectrum_out"] if tile == stop - 1 <= tiles - 1 else refs["spectra"].at[tile - first]

    def power_of(tile):
        if tile < first:
            return refs["power_in"].at[tile - first + 2]
        return refs["power_out"].at[tile - stop + 2] if stop - 2 <= tile and stop <= tiles else refs["power"].at[tile - first]

    def store(tile):
        block = jnp.dot(x[...], table_of(tile)[...], preferred_element_type=jnp.float32)
        spectrum_of(tile)[...] = block
        re, im = block[:, :TILE], block[:, TILE:]
        power_of(tile)[...] = (re * re + im * im).astype(jnp.bfloat16)

    def finish(tile):
        window = jnp.dot(power_of(tile)[...], band[TILE : 2 * TILE], preferred_element_type=jnp.float32)
        window += jnp.dot(power_of(tile + 1)[...], band[2 * TILE :], preferred_element_type=jnp.float32)
        if tile:
            window += jnp.dot(power_of(tile - 1)[...], band[:TILE], preferred_element_type=jnp.float32)
        bin_index = tile * TILE + lax.broadcasted_iota(jnp.int32, (1, TILE), 1)
        number = jnp.minimum(bin_index + HALF, F - 1) - jnp.maximum(bin_index - HALF, 0) + 1
        inverse = 1.0 / number.astype(jnp.float32)
        at = (tile - max(first - 1, 0)) * 2 * TILE
        for seg in range(segs):
            rows = slice(seg * chans, (seg + 1) * chans)
            scale = lax.rsqrt(window[rows] * inverse + EPSILON)
            scale = jnp.where(eff[...] > seg, scale, 0.0)
            place = slice(seg * half, (seg + 1) * half)
            for lane in (0, TILE):
                white = spectrum_of(tile)[rows, lane : lane + TILE] * scale
                lo, hi = white[:half], white[half:]
                one_ref[place, at + lane : at + lane + TILE] = jnp.where(even, hi, lo).astype(jnp.bfloat16)
                two_ref[place, at + lane : at + lane + TILE] = jnp.where(even, lo, hi).astype(jnp.bfloat16)

    head = max(had, 1)
    stretches = [list(range(first, head))] + [list(range(tile, min(tile + 2, stop))) for tile in range(head, stop, 2)]
    if not first:
        fetch(0).start()
        vectors, load_sems = refs["vectors"], refs["load_sems"]
        loads = []
        for seg in range(segs):
            rows = pl.ds(seg * chans, chans)
            loads.append(pltpu.make_async_copy(refs["x_hbm"].at[rows], x.at[rows], load_sems.at[seg]))
        loads.append(pltpu.make_async_copy(refs["counts_hbm"], vectors.at[0], load_sems.at[segs]))
        loads.append(pltpu.make_async_copy(refs["alive_hbm"], vectors.at[1], load_sems.at[segs + 1]))
        for load in loads:
            load.start()
    row = lax.broadcasted_iota(jnp.int32, (3 * TILE, TILE), 0)
    column = lax.broadcasted_iota(jnp.int32, (3 * TILE, TILE), 1)
    band[...] = (jnp.abs(row - TILE - column) <= HALF).astype(jnp.float32).astype(jnp.bfloat16)

    def limits():
        left = counts[0:1, :] - (lax.axis_index("seg") * segs).astype(jnp.float32)
        eff[...] = jnp.transpose(jnp.broadcast_to(left, (chans, chans)))

    if first:
        limits()
    for index, stretch in enumerate(stretches):
        later = stretches[index + 1] if index + 1 < len(stretches) else range(stop, further)
        for tile in later:
            fetch(tile).start()
        for tile in stretch:
            if tile >= had:
                fetch(tile).wait()
        if not first and index == 0:
            for load in loads:
                load.wait()
        if not first and index == 0:
            counts[0:1] = jnp.where(vectors[1] > 0, vectors[0], 0).astype(jnp.float32)
            counts[1:2] = vectors[0].astype(jnp.float32)
            limits()
            row = jnp.broadcast_to(counts[1:2, :].astype(jnp.bfloat16), (EXTRA, chans))
            for ref in (one_ref, two_ref):
                for lane in range(0, ref.shape[1], chans):
                    ref[segs * half :, lane : lane + chans] = row
        for tile in stretch:
            store(tile)
    for tile in range(max(first - 1, 0), stop - 1):
        finish(tile)
    for tile in range(stop, further):
        fetch(tile).wait()


def held(arrays):
    return [pltpu.with_memory_space_constraint(array, pltpu.VMEM) for array in arrays]


def whiten(plan, given, table, segs, chans):
    first, stop, further, tiles = plan
    total, length = segs * chans, table.shape[2]
    made = stop - first
    done = stop - 1 - max(first - 1, 0)
    send = total // 2 + (0 if first else EXTRA)
    here, away = pl.BlockSpec(memory_space=pltpu.VMEM), pl.BlockSpec(memory_space=pl.ANY)
    outs = {name: pltpu.VMEM((send, 2 * TILE * done), jnp.bfloat16) for name in ("one", "two")}
    handed = {}
    scratch = {
        "spectra": pltpu.VMEM((made, total, 2 * TILE), jnp.float32),
        "power": pltpu.VMEM((made, total, TILE), jnp.bfloat16),
        "band": pltpu.VMEM((3 * TILE, TILE), jnp.bfloat16),
        "eff": pltpu.VMEM((chans, chans), jnp.float32),
        "sems": pltpu.SemaphoreType.DMA((further - first,)),
    }
    lacking = made - (given["table_in"].shape[0] if first else 0)
    if lacking:
        scratch["buffers"] = pltpu.VMEM((lacking, length, 2 * TILE), jnp.bfloat16)
    if not first:
        handed["x"] = pltpu.VMEM((total, length), jnp.bfloat16)
        handed["counts"] = pltpu.VMEM((2, chans), jnp.float32)
        scratch["vectors"] = pltpu.VMEM((2, 1, chans), jnp.int32)
        scratch["load_sems"] = pltpu.SemaphoreType.DMA((segs + 2,))
    if stop <= tiles:
        handed["spectrum_out"] = pltpu.VMEM((total, 2 * TILE), jnp.float32)
        handed["power_out"] = pltpu.VMEM((2, total, TILE), jnp.bfloat16)
        handed["table_out"] = pltpu.VMEM((further - stop, length, 2 * TILE), jnp.bfloat16)
    if first:
        operands = held(given.values())
    else:
        operands = [pltpu.with_memory_space_constraint(array, pltpu.HBM) for array in given.values()]
    names = ["table", *given, *outs, *handed, *scratch]
    results = pl.pallas_call(
        functools.partial(whiten_kernel, plan, names),
        out_shape=[*outs.values(), *handed.values()],
        in_specs=[away] + [here if first else away] * len(operands),
        out_specs=[here] * (len(outs) + len(handed)),
        scratch_shapes=list(scratch.values()),
        compiler_params=pltpu.CompilerParams(vmem_limit_bytes=24 * MIB),
        cost_estimate=pl.CostEstimate(
            flops=2 * total * length * 2 * TILE * made,
            bytes_accessed=2 * length * 2 * TILE * made + 2 * total * length,
            transcendentals=0,
        ),
        name="whiten",
    )(table, *operands)
    handed = dict(zip(handed, results[2:]))
    kept = {name: handed.get(name, given.get(name)) for name in ("x", "counts")}
    passed = {name.replace("_out", "_in"): array for name, array in handed.items() if name.endswith("_out")}
    return results[0], results[1], {**kept, **passed}


def window_start(offset, chans):
    return jnp.minimum(chans // 2, chans - offset) // 16 * 16


def correlate_kernel(plan, offsets, one_ref, two_ref, got_one_ref, got_two_ref, table_hbm, *refs):
    tile_first, is_first, is_last = plan
    refs = list(refs)
    earlier = refs.pop(0)
    if is_last:
        keep_ref, send_ref = refs.pop(0), refs.pop(0)
    else:
        total = refs.pop(0)
    if is_first:
        inverse_ref = refs.pop(0)
    if is_last:
        total = refs.pop(0)
    select, frame, far, cross, delay, sems = refs
    tiles, segs, span, _ = frame.shape
    chans, half = span // 2, span // 4
    slots = cross.shape[0] // chans
    parts, depth, width = delay.shape
    last_place, length = table_hbm.shape[1] - 1, table_hbm.shape[2] // parts
    place = lax.axis_index("chan")
    even = place & 1 == 0
    known = jnp.where(place < lax.axis_size("chan") - 1, 4 * half, 3 * half)

    copies = []
    for part in range(parts):
        rows = pl.ds(part * length + tile_first * 2 * TILE, depth)
        source = table_hbm.at[lax.axis_index("freq"), last_place, rows, :]
        copies.append(pltpu.make_async_copy(source, delay.at[part], sems.at[part]))
        copies[part].start()

    row = lax.broadcasted_iota(jnp.int32, (chans, 2 * chans), 0)
    column = lax.broadcasted_iota(jnp.int32, (chans, 2 * chans), 1)
    for slot in range(slots):
        offset = offsets[slot]
        match = (column == row + window_start(offset, chans) + offset) & (column < known)
        select[slot * chans : (slot + 1) * chans] = match.astype(jnp.float32).astype(jnp.bfloat16)
    if is_first:
        row = lax.broadcasted_iota(jnp.int32, (chans, chans), 0)
        column = lax.broadcasted_iota(jnp.int32, (chans, chans), 1)
        own = earlier[1:2, :]
        following = [ref[segs * half :, :chans].astype(jnp.float32)[:1] for ref in (got_one_ref, got_two_ref)]
        following = jnp.where(even, *following)
        mine = jnp.sum(jnp.where(row == column, own, 0.0), axis=1, keepdims=True)
        for slot in range(slots):
            target = row + offsets[slot]
            partner = jnp.where(column == target, own, 0.0) + jnp.where(column + chans == target, following, 0.0)
            partner = jnp.sum(partner, axis=1, keepdims=True)
            divisor = jnp.maximum(jnp.minimum(mine, partner), 1.0)
            inverse_ref[slot] = jnp.broadcast_to(1.0 / divisor, inverse_ref.shape[1:])
    if is_last:
        keep_ref[...] = jnp.zeros_like(keep_ref)
        send_ref[...] = jnp.zeros_like(send_ref)

    order = ((one_ref, 2, 1), (two_ref, 1, 2), (got_one_ref, 3, 0), (got_two_ref, 0, 3))
    done = 0
    for tile in range(tiles):
        for ref, if_even, if_odd in order:
            spot = pl.ds(pl.multiple_of(jnp.where(even, if_even * half, if_odd * half), half), half)
            for seg in range(segs):
                rows = slice(seg * half, (seg + 1) * half)
                frame[tile, seg, spot, :] = ref[rows, tile * 2 * TILE : (tile + 1) * 2 * TILE]
        turn = tile % far.shape[0]
        for seg in range(segs):
            far[turn, seg] = jnp.dot(select[...], frame[tile, seg], preferred_element_type=jnp.float32)
        for slot in range(slots):
            start = window_start(offsets[slot], chans)
            for index in range(chans // 16):
                real = jnp.zeros((16, TILE), jnp.float32)
                imag = jnp.zeros((16, TILE), jnp.float32)
                base = pl.multiple_of(start + index * 16, 16)
                spot = slice(slot * chans + index * 16, slot * chans + index * 16 + 16)
                for seg in range(segs):
                    own = frame[tile, seg, pl.ds(base, 16), :].astype(jnp.float32)
                    own_re, own_im = own[:, :TILE], own[:, TILE:]
                    far_re, far_im = far[turn, seg, spot, :TILE], far[turn, seg, spot, TILE:]
                    real += own_re * far_re + own_im * far_im
                    imag += own_im * far_re - own_re * far_im
                lane = tile * 2 * TILE
                cross[spot, lane : lane + TILE] = real.astype(jnp.bfloat16)
                cross[spot, lane + TILE : lane + 2 * TILE] = imag.astype(jnp.bfloat16)
        if tile + 1 < tiles and (tile + 1) % LAG_TILES:
            continue
        lanes = slice(done * 2 * TILE, (tile + 1) * 2 * TILE)
        for part in range(parts):
            if not done:
                copies[part].wait()
            for slot in range(slots):
                spot, columns = slice(slot * chans, (slot + 1) * chans), slice(part * width, (part + 1) * width)
                term = jnp.dot(cross[spot, lanes], delay[part, lanes], preferred_element_type=jnp.float32)
                if done:
                    term += total[spot, columns]
                elif not is_first:
                    term += earlier[spot, columns]
                if not is_last or tile + 1 < tiles:
                    total[spot, columns] = term
                    continue
                rows = pl.ds(pl.multiple_of(window_start(offsets[slot], chans), 16), chans)
                if part == 0:
                    keep_ref[slot, rows, :] = term
                else:
                    send_ref[slot, rows, (part - 1) * width : part * width] = term.astype(send_ref.dtype)
        done = tile + 1


def correlate(plan, offsets, sent, got, table, earlier, segs, chans):
    tile_first, is_first, is_last = plan
    half, columns = chans // 2, sent[0].shape[1]
    tiles = columns // (2 * TILE)
    slots = offsets.shape[0]
    parts, keep = table.shape[0], table.shape[3]
    lags = parts * keep
    here = pl.BlockSpec(memory_space=pltpu.VMEM)
    scratch = [
        pltpu.VMEM((slots * chans, 2 * chans), jnp.bfloat16),
        pltpu.VMEM((tiles, segs, 2 * chans, 2 * TILE), jnp.bfloat16),
        pltpu.VMEM((2, segs, slots * chans, 2 * TILE), jnp.float32),
        pltpu.VMEM((slots * chans, columns), jnp.bfloat16),
        pltpu.VMEM((parts, columns, keep), jnp.bfloat16),
        pltpu.SemaphoreType.DMA((parts,)),
    ]
    if is_last:
        out_shape = [
            pltpu.VMEM((slots, 3 * half, keep), jnp.float32),
            pltpu.VMEM((slots, 3 * half, lags - keep), jnp.bfloat16),
        ]
        scratch = [pltpu.VMEM((slots * chans, lags), jnp.float32)] + scratch
    else:
        out_shape = [pltpu.VMEM((slots * chans, lags), jnp.float32)]
    if is_first:
        out_shape += [pltpu.VMEM((slots, chans, keep), jnp.float32)]
    return pl.pallas_call(
        functools.partial(correlate_kernel, plan),
        out_shape=out_shape,
        grid_spec=pltpu.PrefetchScalarGridSpec(
            num_scalar_prefetch=1,
            grid=(),
            in_specs=[here] * 4 + [pl.BlockSpec(memory_space=pl.ANY), here],
            out_specs=[here] * len(out_shape),
            scratch_shapes=scratch,
        ),
        compiler_params=pltpu.CompilerParams(vmem_limit_bytes=20 * MIB),
        cost_estimate=pl.CostEstimate(
            flops=tiles * 2 * slots * chans * 2 * TILE * (segs * 2 * chans + lags),
            bytes_accessed=tiles * (4 * segs * half * 2 * TILE * 2),
            transcendentals=0,
        ),
        name="correlate",
    )(offsets, *held([*sent, *got]), table, *held([earlier]))


def swap(block, first):
    blocks, parts = lax.axis_size("chan"), lax.axis_size("freq")
    route = []
    for i in range(blocks):
        partner = i + 1 if (i - first) % 2 == 0 else i - 1
        alone = not 0 <= partner < blocks
        for part in range(parts):
            target = i * parts + (part + 1) % parts if alone else partner * parts + part
            route.append((i * parts + part, target))
    return lax.ppermute(block, ("chan", "freq"), route)


def returns(blocks, parts):
    near, far = {}, {}
    last = blocks - 1
    for i in range(blocks):
        near[i, 1] = (i - 1, 1) if i else (0, 0)
        near[i, 0] = (i + 1, 0) if i < last else (last, 1)
        far[i, 0] = (i - 1, 1) if i else (0, 0)
        far[i, 1] = (i + 1, 0) if i < last else (last, 1)
    routes = []
    for steps in (near, far):
        route = []
        for source, target in steps.items():
            for part in range(parts):
                end = (part + 1) % parts if source == target else part
                route.append(((2 * source[0] + source[1]) * parts + part, (2 * target[0] + target[1]) * parts + end))
        routes.append(route)
    return routes


def reduced(span, keep, chans, has_next):
    spans, blocks = lax.axis_size("seg"), lax.axis_size("chan")
    half = chans // 2
    back = lax.ppermute(keep[:, :half].astype(jnp.bfloat16), "chan", [(i, (i - 1) % blocks) for i in range(blocks)])
    back = jnp.where(has_next, back.astype(jnp.float32), 0.0)
    keep = keep[:, half:] + jnp.pad(back, ((0, 0), (chans - half, 0), (0, 0)))
    piece = chans // spans
    result = lax.dynamic_slice_in_dim(keep, span * piece, piece, 1)
    for step in range(1, spans):
        target = lax.rem(span + step, spans)
        block = lax.dynamic_slice_in_dim(keep, target * piece, piece, 1).astype(jnp.bfloat16)
        block = lax.ppermute(block, "seg", [(i, (i + step) % spans) for i in range(spans)])
        result = result + block.astype(jnp.float32)
    return result


def shards(traces, dead_mask, seg_counts, offsets):
    segs, chans, length = traces.shape
    half = chans // 2
    parts, spans, blocks = lax.axis_size("freq"), lax.axis_size("seg"), lax.axis_size("chan")
    assert parts == 2
    table = jnp.asarray(tables(length, parts))
    tiles = table.shape[1] - 2
    span = lax.axis_index("seg").astype(jnp.int32)
    has_next = lax.axis_index("chan") < blocks - 1
    given = {
        "x_hbm": traces.reshape(segs * chans, length),
        "counts_hbm": seg_counts.reshape(1, chans),
        "alive_hbm": dead_mask.reshape(1, chans),
    }
    groups, made = [], 0
    for stop, further in zip(GROUPS, AHEAD):
        one, two, given = whiten((made, stop, further, tiles), given, table, segs, chans)
        groups.append((max(made - 1, 0), segs, (one, two), (swap(one, 0), swap(two, 1))))
        made = stop
    earlier = given["counts"]
    for index, (tile_first, number, sent, got) in enumerate(groups):
        plan = (tile_first, index == 0, index == len(groups) - 1)
        results = list(correlate(plan, offsets, sent, got, table, earlier, number, chans))
        if index == 0:
            inverse = results.pop()
        earlier = results[0]
    keep, send = results
    keep = keep + lax.ppermute(send, "freq", [(0, 1), (1, 0)]).astype(jnp.float32)
    if spans == 2:
        lower, upper = keep[:, half:chans], keep[:, chans:]
        mine = jnp.where(span == 0, lower, upper)
        other = jnp.where(span == 0, upper, lower).astype(jnp.bfloat16)
        back = keep[:, :half].astype(jnp.bfloat16)
        other = lax.ppermute(other, "seg", [(0, 1), (1, 0)])
        route_near, route_far = returns(blocks, parts)
        near = lax.ppermute(back, ("chan", "seg", "freq"), route_near)
        far = lax.ppermute(back, ("chan", "seg", "freq"), route_far)
        returned = jnp.where(has_next & (span == 1), near.astype(jnp.float32) + far.astype(jnp.float32), 0.0)
        result = mine + other.astype(jnp.float32) + returned
        result = result * jnp.where(span == 0, inverse[:, :half], inverse[:, half:])
    else:
        piece = chans // spans
        result = reduced(span, keep, chans, has_next)
        result = result * lax.dynamic_slice_in_dim(inverse, span * piece, piece, 1)
    return jnp.transpose(result, (1, 0, 2))


def solution(mesh):
    in_specs = (
        P("seg", ("groups", "chan"), None),
        P(("groups", "chan")),
        P(("groups", "chan")),
        P(),
    )
    out_specs = P(("groups", "chan", "seg"), None, "freq")
    return jax.shard_map(shards, mesh=mesh, in_specs=in_specs, out_specs=out_specs, check_vma=False)
```

time: 65.7 us -> 60.4 us (0.919)
  local copies, waits for them, and re-layouts: 5.21 us -> 0.88 us
  starting transfers between devices: 12.7 us -> 11.5 us
  other arithmetic: 1.07 us -> 0.22 us
  waiting for transfers between devices: 7.78 us -> 8.59 us
    unnamed x10 -> x2, local copies, waits for them, and re-layouts: 4.33 us -> 0.01 us
    pallas_call x3, Pallas kernels: 14.2 us -> 12.1 us  [correlate(): pl.pallas_call(functools.partial(correlate_kernel, plan), out_shape=out_s...]
    pallas_call x3, Pallas kernels: 24.3 us -> 26.3 us  [whiten(): pl.pallas_call(functools.partial(whiten_kernel, plan, names), out_shape=[...]
    ppermute x8 -> x6, starting transfers between devices: 8.51 us -> 6.97 us  [swap(): return lax.ppermute(block, ('chan', 'freq'), route)]
    ppermute x8 -> x6, waiting for transfers between devices: 1.63 us -> 2.9 us  [swap(): return lax.ppermute(block, ('chan', 'freq'), route)]
    ppermute x1, starting transfers between devices: 1.69 us -> 2.7 us  [shards(): near = lax.ppermute(back, ('chan', 'seg', 'freq'), route_near)]
    ppermute x1, starting transfers between devices: 2.42 us -> 1.72 us  [shards(): other = lax.ppermute(other, 'seg', [(0, 1), (1, 0)])]
    reshape x2 -> x0, other arithmetic: 0.69 us -> none  [the longest x1 0.69 us: shards(): jnp.where(dead_mask > 0, seg_counts, 0).astype(jnp.float32)]
  transfers between devices with their start and end apart: 12 -> 10, of which waited for: 5 -> 5; matrix products, arithmetic and copies ran while one was open for 1% -> 0% of each run, Pallas kernels for 52% -> 38%
where the time goes in v7:
time: 60.4 us; the launch traced here: 59.6 us
  Pallas kernels  38.4 us (64%)
  starting transfers between devices  11.5 us (19%)
  waiting for transfers between devices  8.59 us (14%)
  local copies, waits for them, and re-layouts  0.88 us (1%)
    pallas_call x3, Pallas kernels, whiten(): pl.pallas_call(functools.partial(whiten_kernel, plan, names), out_shape=[...  26.3 us
    pallas_call x3, Pallas kernels, correlate(): pl.pallas_call(functools.partial(correlate_kernel, plan), out_shape=out_s...  12.1 us
    ppermute x6, starting transfers between devices, swap(): return lax.ppermute(block, ('chan', 'freq'), route)  6.97 us
    ppermute x6, waiting for transfers between devices, swap(): return lax.ppermute(block, ('chan', 'freq'), route)  2.9 us
    ppermute x1, starting transfers between devices, shards(): near = lax.ppermute(back, ('chan', 'seg', 'freq'), route_near)  2.7 us
    ppermute x1, waiting for transfers between devices, shards(): near = lax.ppermute(back, ('chan', 'seg', 'freq'), route_near)  2.01 us
    ppermute x1, waiting for transfers between devices, shards(): other = lax.ppermute(other, 'seg', [(0, 1), (1, 0)])  1.98 us
    ppermute x1, starting transfers between devices, shards(): other = lax.ppermute(other, 'seg', [(0, 1), (1, 0)])  1.72 us
  transfers between devices with their start and end apart: 10, of which 5 were waited for; matrix products, arithmetic and copies ran while one was open for 0% of the time, Pallas kernels for 38%

profile of v7, /device:TPU:0, one launch (start us, length us, event | category | flops | bytes accessed | tf_op | source)
XLA Modules:
  0.0 59.6 jit_solution(11358581497145762871)
XLA Ops:
  0.0 12.5 %whiten.3 = (bf16[336,768]{1,0:T(8,128)(2,1)S(1)}, bf16[336,768]{1,0:T(8,128)(2,1)S(1)}, bf16[640,4096]{1,0:T(8,128)(2,1)S(1)}, f32[2,128]{1,0:T(2,128)S(1)}, f3...) custom-call(bf16[2,10,4096,256]{3,2,1,0:T(8,128)(2,1)} %constant.19.clone.refs_0_.table_hbm, ...), custom_call_target="tpu_custom_call" | custom-call | flops 5368709120 | bytes 13631488 | tf_op jit(solution)/shard_map/whiten/pallas_call | solution.py:197
  12.5 3.1 %collective-permute-start.4 = (bf16[336,768]{1,0:T(8,128)(2,1)S(1)}, bf16[336,768]{1,0:T(8,128)(2,1)S(1)}, u32[]{:S(2)}, u32[]{:S(2)}) collective-permute-start(bf16[336,768]{1,0:T(8,128)(2,1)S(1)} %get-tuple-element.35.one_ref), channel_id=1, source_target_pairs={{0,4},{1,5},{4,0},{5,1},{8,12},{9,13},{12,8},{13,9},{2,6},{3,7},{6... | collective-permute-start | bytes 1548296 | tf_op jit(solution)/shard_map/ppermute | solution.py:379
  15.6 0.0 collective-permute-start.5
  15.6 7.7 %whiten.4 = (bf16[320,768]{1,0:T(8,128)(2,1)S(1)}, bf16[320,768]{1,0:T(8,128)(2,1)S(1)}, f32[640,256]{1,0:T(8,128)S(1)}, bf16[2,640,128]{2,1,0:T(8,128)(2,1)S(1)}, bf16[1,4096,256]{2,1,0:T(8,128)(2,1)S(1)}) custom-call(bf16[2,10,4096,256]{3,2,1,0:T(8,128)(2,1)} %constant.19.clone.refs_0_.table_hbm, bf16[640,4096]{1,0:T(8,128)(2,1)S(1)} %get-tuple-element.23.refs_1_, ...), custom_call_target="tpu_custom_call" | custom-call | flops 4026531840 | bytes 11534336 | tf_op jit(solution)/shard_map/whiten/pallas_call | solution.py:197
  23.3 3.2 %collective-permute-start.2 = (bf16[320,768]{1,0:T(8,128)(2,1)S(1)}, bf16[320,768]{1,0:T(8,128)(2,1)S(1)}, u32[]{:S(2)}, u32[]{:S(2)}) collective-permute-start(bf16[320,768]{1,0:T(8,128)(2,1)S(1)} %get-tuple-element.33.one_ref), channel_id=1, source_target_pairs={{0,4},{1,5},{4,0},{5,1},{8,12},{9,13},{12,8},{13,9},{2,6},{3,7},{6... | collective-permute-start | bytes 1474568 | tf_op jit(solution)/shard_map/ppermute | solution.py:379
  26.5 0.0 collective-permute-start.3
  26.5 6.1 %whiten.5 = (bf16[320,512]{1,0:T(8,128)(2,1)S(1)}, bf16[320,512]{1,0:T(8,128)(2,1)S(1)}) custom-call(bf16[2,10,4096,256]{3,2,1,0:T(8,128)(2,1)} %constant.19.clone.refs_0_.table_hbm, bf16[640,4096]{1,0:T(8,128)(2,1)S(1)} %get-tuple-element.23.refs_1_, f32[2,128]{1,0:T(2,128)S(1)} %get-tuple-element.24.refs_2_.refs_0_, ...), custom_call_target="tpu_custom_call" | custom-call | flops 2684354560 | bytes 9437184 | tf_op jit(solution)/shard_map/whiten/pallas_call | solution.py:197
  32.7 0.5 collective-permute-start
  33.2 0.1 collective-permute-start.1
  33.3 0.0 collective-permute-done.5.got_two_ref
  33.3 4.5 %correlate.3 = (f32[512,512]{1,0:T(8,128)S(1)}, f32[4,128,256]{2,1,0:T(8,128)S(1)}) custom-call(s32[4]{0:T(128)S(1)} %copy-done, bf16[336,768]{1,0:T(8,128)(2,1)S(1)} %get-tuple-element.35.one_ref, bf16[336,768]{1,0:T(8,128)(2,1)S(1)} %get-tuple-element.36.two_ref, bf16[336,768]{1,0:T(8,128)(2,1)S(1)} %collective-permute-done.4.got_one_ref, ...), custom_call_target="tpu_custom_call" | custom-call | flops 1409286144 | bytes 1966080 | tf_op jit(solution)/shard_map/correlate/pallas_call | solution.py:350
  37.8 0.8 %collective-permute-done.2.got_one_ref = bf16[320,768]{1,0:T(8,128)(2,1)S(1)} collective-permute-done((bf16[320,768]{1,0:T(8,128)(2,1)S(1)}, bf16[320,768]{1,0:T(8,128)(2,1)S(1)}, u32[]{:S(2)}, u32[]{:S(2)}) %collective-permute-start.2) | collective-permute-done | bytes 491552 | tf_op jit(solution)/shard_map/ppermute | solution.py:379
  38.7 4.2 %correlate.4.refs_0_ = f32[512,512]{1,0:T(8,128)S(1)} custom-call(s32[4]{0:T(128)S(1)} %copy-done, bf16[320,768]{1,0:T(8,128)(2,1)S(1)} %get-tuple-element.33.one_ref, bf16[320,768]{1,0:T(8,128)(2,1)S(1)} %get-tuple-element.34.two_ref, bf16[320,768]{1,0:T(8,128)(2,1)S(1)} %collective-permute-done.2.got_one_ref, ...), custom_call_target="tpu_custom_call" | custom-call | flops 1409286144 | bytes 1966080 | tf_op jit(solution)/shard_map/correlate/pallas_call | solution.py:350
  42.9 2.0 %collective-permute-done.got_one_ref = bf16[320,512]{1,0:T(8,128)(2,1)S(1)} collective-permute-done((bf16[320,512]{1,0:T(8,128)(2,1)S(1)}, bf16[320,512]{1,0:T(8,128)(2,1)S(1)}, u32[]{:S(2)}, u32[]{:S(2)}) %collective-permute-start) | collective-permute-done | bytes 327712 | tf_op jit(solution)/shard_map/ppermute | solution.py:379
  44.9 3.4 %correlate.5 = (f32[4,192,256]{2,1,0:T(8,128)S(1)}, bf16[4,192,256]{2,1,0:T(8,128)(2,1)S(1)}) custom-call(s32[4]{0:T(128)S(1)} %copy-done, bf16[320,512]{1,0:T(8,128)(2,1)S(1)} %get-tuple-element.31.one_ref, bf16[320,512]{1,0:T(8,128)(2,1)S(1)} %get-tuple-element.32.two_ref, bf16[320,512]{1,0:T(8,128)(2,1)S(1)} %collective-permute-done.got_one_ref, ...), custom_call_target="tpu_custom_call" | custom-call | flops 939524096 | bytes 1310720 | tf_op jit(solution)/shard_map/correlate/pallas_call | solution.py:350
  48.3 0.1 collective-permute-start.6
  48.4 1.7 %collective-permute-done.6 = bf16[4,192,256]{2,1,0:T(8,128)(2,1)S(1)} collective-permute-done((bf16[4,192,256]{2,1,0:T(8,128)(2,1)S(1)}, bf16[4,192,256]{2,1,0:T(8,128)(2,1)S(1)}, u32[]{:S(2)}, u32[]{:S(2)}) %collective-permute-start.6) | collective-permute-done | bytes 393248 | tf_op jit(solution)/shard_map/ppermute | solution.py:444
  50.1 0.1 convert_add_fusion
  50.3 1.7 %collective-permute-start.7 = (bf16[4,64,256]{2,1,0:T(8,128)(2,1)S(1)}, bf16[4,64,256]{2,1,0:T(8,128)(2,1)S(1)}, u32[]{:S(2)}, u32[]{:S(2)}) collective-permute-start(bf16[4,64,256]{2,1,0:T(8,128)(2,1)S(1)} %get-tuple-element.41), channel_id=1, source_target_pairs={{0,2},{2,0},{1,3},{3,1},{4,6},{6,4},{5,7},{7,5},{8,10},{10,8},{9,1... | collective-permute-start | bytes 393224 | tf_op jit(solution)/shard_map/ppermute | solution.py:450
  52.0 2.7 %collective-permute-start.8 = (bf16[4,64,256]{2,1,0:T(8,128)(2,1)S(1)}, bf16[4,64,256]{2,1,0:T(8,128)(2,1)S(1)}, u32[]{:S(2)}, u32[]{:S(2)}) collective-permute-start(bf16[4,64,256]{2,1,0:T(8,128)(2,1)S(1)} %get-tuple-element.42), channel_id=1, source_target_pairs={{2,0},{3,1},{0,4},{1,5},{6,2},{7,3},{4,8},{5,9},{10,6},{11,7},{8,1... | collective-permute-start | bytes 393224 | tf_op jit(solution)/shard_map/ppermute | solution.py:452
  54.7 2.0 %collective-permute-done.7 = bf16[4,64,256]{2,1,0:T(8,128)(2,1)S(1)} collective-permute-done((bf16[4,64,256]{2,1,0:T(8,128)(2,1)S(1)}, bf16[4,64,256]{2,1,0:T(8,128)(2,1)S(1)}, u32[]{:S(2)}, u32[]{:S(2)}) %collective-permute-start.7) | collective-permute-done | bytes 131104 | tf_op jit(solution)/shard_map/ppermute | solution.py:450
  56.7 2.0 %collective-permute-done.8 = bf16[4,64,256]{2,1,0:T(8,128)(2,1)S(1)} collective-permute-done((bf16[4,64,256]{2,1,0:T(8,128)(2,1)S(1)}, bf16[4,64,256]{2,1,0:T(8,128)(2,1)S(1)}, u32[]{:S(2)}, u32[]{:S(2)}) %collective-permute-start.8) | collective-permute-done | bytes 131104 | tf_op jit(solution)/shard_map/ppermute | solution.py:452
  58.7 0.1 multiply_bitcast_fusion
  58.8 0.9 %copy.6 = f32[64,4,256]{2,1,0:T(4,128)} copy(f32[64,4,256]{2,0,1:T(8,128)S(1)} %multiply_bitcast_fusion) | data formatting | bytes 524288 | tf_op jit(solution)/shard_map/transpose | solution.py:461
  (8 shorter events, 0.1 us)
Async XLA Ops:
  12.5 20.6 %collective-permute-start.4 = (bf16[336,768]{1,0:T(8,128)(2,1)S(1)}, bf16[336,768]{1,0:T(8,128)(2,1)S(1)}, u32[]{:S(2)}, u32[]{:S(2)}) collective-permute-start(bf16[336,768]{1,0:T(8,128)(2,1)S(1)} %get-tuple-element.35.one_ref), channel_id=1, source_target_pairs={{0,4},{1,5},{4,0},{5,1},{8,12},{9,13},{12,8},{13,9},{2,6},{3,7},{6... | collective-permute-start | bytes 1548296 | tf_op jit(solution)/shard_map/ppermute | solution.py:379
  15.6 17.7 %collective-permute-start.5 = (bf16[336,768]{1,0:T(8,128)(2,1)S(1)}, bf16[336,768]{1,0:T(8,128)(2,1)S(1)}, u32[]{:S(2)}, u32[]{:S(2)}) collective-permute-start(bf16[336,768]{1,0:T(8,128)(2,1)S(1)} %get-tuple-element.36.two_ref), channel_id=1, source_target_pairs={{0,1},{1,0},{4,8},{5,9},{8,4},{9,5},{12,13},{13,12},{2,3},{3,2},{6... | collective-permute-start | bytes 1548296 | tf_op jit(solution)/shard_map/ppermute | solution.py:379
  23.3 15.3 %collective-permute-start.2 = (bf16[320,768]{1,0:T(8,128)(2,1)S(1)}, bf16[320,768]{1,0:T(8,128)(2,1)S(1)}, u32[]{:S(2)}, u32[]{:S(2)}) collective-permute-start(bf16[320,768]{1,0:T(8,128)(2,1)S(1)} %get-tuple-element.33.one_ref), channel_id=1, source_target_pairs={{0,4},{1,5},{4,0},{5,1},{8,12},{9,13},{12,8},{13,9},{2,6},{3,7},{6... | collective-permute-start | bytes 1474568 | tf_op jit(solution)/shard_map/ppermute | solution.py:379
  26.5 12.1 %collective-permute-start.3 = (bf16[320,768]{1,0:T(8,128)(2,1)S(1)}, bf16[320,768]{1,0:T(8,128)(2,1)S(1)}, u32[]{:S(2)}, u32[]{:S(2)}) collective-permute-start(bf16[320,768]{1,0:T(8,128)(2,1)S(1)} %get-tuple-element.34.two_ref), channel_id=1, source_target_pairs={{0,1},{1,0},{4,8},{5,9},{8,4},{9,5},{12,13},{13,12},{2,3},{3,2},{6... | collective-permute-start | bytes 1474568 | tf_op jit(solution)/shard_map/ppermute | solution.py:379
  26.5 6.8 %copy-start = (s32[4]{0:T(128)S(1)}, s32[4]{0:T(128)}, u32[]{:S(2)}) copy-start(s32[4]{0:T(128)} %offsets.5) | copy-start | bytes 52
  32.7 12.3 %collective-permute-start = (bf16[320,512]{1,0:T(8,128)(2,1)S(1)}, bf16[320,512]{1,0:T(8,128)(2,1)S(1)}, u32[]{:S(2)}, u32[]{:S(2)}) collective-permute-start(bf16[320,512]{1,0:T(8,128)(2,1)S(1)} %get-tuple-element.31.one_ref), channel_id=1, source_target_pairs={{0,4},{1,5},{4,0},{5,1},{8,12},{9,13},{12,8},{13,9},{2,6},{3,7},{6... | collective-permute-start | bytes 983048 | tf_op jit(solution)/shard_map/ppermute | solution.py:379
  33.2 11.8 %collective-permute-start.1 = (bf16[320,512]{1,0:T(8,128)(2,1)S(1)}, bf16[320,512]{1,0:T(8,128)(2,1)S(1)}, u32[]{:S(2)}, u32[]{:S(2)}) collective-permute-start(bf16[320,512]{1,0:T(8,128)(2,1)S(1)} %get-tuple-element.32.two_ref), channel_id=1, source_target_pairs={{0,1},{1,0},{4,8},{5,9},{8,4},{9,5},{12,13},{13,12},{2,3},{3,2},{6... | collective-permute-start | bytes 983048 | tf_op jit(solution)/shard_map/ppermute | solution.py:379
  48.3 1.8 %collective-permute-start.6 = (bf16[4,192,256]{2,1,0:T(8,128)(2,1)S(1)}, bf16[4,192,256]{2,1,0:T(8,128)(2,1)S(1)}, u32[]{:S(2)}, u32[]{:S(2)}) collective-permute-start(bf16[4,192,256]{2,1,0:T(8,128)(2,1)S(1)} %get-tuple-element.39), channel_id=1, source_target_pairs={{0,1},{1,0},{2,3},{3,2},{4,5},{5,4},{6,7},{7,6},{8,9},{9,8},{10,11... | collective-permute-start | bytes 1179656 | tf_op jit(solution)/shard_map/ppermute | solution.py:444
  50.3 6.4 %collective-permute-start.7 = (bf16[4,64,256]{2,1,0:T(8,128)(2,1)S(1)}, bf16[4,64,256]{2,1,0:T(8,128)(2,1)S(1)}, u32[]{:S(2)}, u32[]{:S(2)}) collective-permute-start(bf16[4,64,256]{2,1,0:T(8,128)(2,1)S(1)} %get-tuple-element.41), channel_id=1, source_target_pairs={{0,2},{2,0},{1,3},{3,1},{4,6},{6,4},{5,7},{7,5},{8,10},{10,8},{9,1... | collective-permute-start | bytes 393224 | tf_op jit(solution)/shard_map/ppermute | solution.py:450
  52.0 6.7 %collective-permute-start.8 = (bf16[4,64,256]{2,1,0:T(8,128)(2,1)S(1)}, bf16[4,64,256]{2,1,0:T(8,128)(2,1)S(1)}, u32[]{:S(2)}, u32[]{:S(2)}) collective-permute-start(bf16[4,64,256]{2,1,0:T(8,128)(2,1)S(1)} %get-tuple-element.42), channel_id=1, source_target_pairs={{2,0},{3,1},{0,4},{1,5},{6,2},{7,3},{4,8},{5,9},{10,6},{11,7},{8,1... | collective-permute-start | bytes 393224 | tf_op jit(solution)/shard_map/ppermute | solution.py:452
  54.7 4.0 %collective-permute-start.9 = (bf16[4,64,256]{2,1,0:T(8,128)(2,1)S(1)}, bf16[4,64,256]{2,1,0:T(8,128)(2,1)S(1)}, u32[]{:S(2)}, u32[]{:S(2)}) collective-permute-start(bf16[4,64,256]{2,1,0:T(8,128)(2,1)S(1)} %get-tuple-element.42), channel_id=1, source_target_pairs={{0,1},{1,0},{2,4},{3,5},{4,2},{5,3},{6,8},{7,9},{8,6},{9,7},{10,12... | collective-permute-start | bytes 393224 | tf_op jit(solution)/shard_map/ppermute | solution.py:453

commit v8 on v7

--- a/solution.py
+++ b/solution.py
@@ -62,7 +62,7 @@
     total, length = x.shape
     segs, half = total // chans, chans // 2
     even = lax.axis_index("chan") & 1 == 0
-    buffers, had = refs.get("buffers"), first + (refs["table_in"].shape[0] if first else 0)
+    buffers, had = refs.get("buffers"), first + (refs["table_in"].shape[0] if "table_in" in refs else 0)
 
     def fetch(tile):
         source = table_hbm.at[lax.axis_index("freq"), tile]
@@ -82,11 +82,11 @@
             return refs["power_in"].at[tile - first + 2]
         return refs["power_out"].at[tile - stop + 2] if stop - 2 <= tile and stop <= tiles else refs["power"].at[tile - first]
 
-    def store(tile):
-        block = jnp.dot(x[...], table_of(tile)[...], preferred_element_type=jnp.float32)
-        spectrum_of(tile)[...] = block
+    def store(tile, rows):
+        block = jnp.dot(x[rows], table_of(tile)[...], preferred_element_type=jnp.float32)
+        spectrum_of(tile)[rows] = block
         re, im = block[:, :TILE], block[:, TILE:]
-        power_of(tile)[...] = (re * re + im * im).astype(jnp.bfloat16)
+        power_of(tile)[rows] = (re * re + im * im).astype(jnp.bfloat16)
 
     def finish(tile):
         window = jnp.dot(power_of(tile)[...], band[TILE : 2 * TILE], preferred_element_type=jnp.float32)
@@ -108,19 +108,35 @@
                 one_ref[place, at + lane : at + lane + TILE] = jnp.where(even, hi, lo).astype(jnp.bfloat16)
                 two_ref[place, at + lane : at + lane + TILE] = jnp.where(even, lo, hi).astype(jnp.bfloat16)
 
-    head = max(had, 1)
-    stretches = [list(range(first, head))] + [list(range(tile, min(tile + 2, stop))) for tile in range(head, stop, 2)]
-    if not first:
-        fetch(0).start()
+    rows = slice(0, total)
+    if first:
+        head = max(had, first + 1)
+        own = [fetch(tile) for tile in range(had, head)]
+        stretches = [(own, [(tile, rows) for tile in range(first, head)])]
+    else:
+        head = 2
         vectors, load_sems = refs["vectors"], refs["load_sems"]
+        early = (segs + 1) // 2
         loads = []
         for seg in range(segs):
-            rows = pl.ds(seg * chans, chans)
-            loads.append(pltpu.make_async_copy(refs["x_hbm"].at[rows], x.at[rows], load_sems.at[seg]))
-        loads.append(pltpu.make_async_copy(refs["counts_hbm"], vectors.at[0], load_sems.at[segs]))
-        loads.append(pltpu.make_async_copy(refs["alive_hbm"], vectors.at[1], load_sems.at[segs + 1]))
-        for load in loads:
-            load.start()
+            place = pl.ds(seg * chans, chans)
+            loads.append(pltpu.make_async_copy(refs["x_hbm"].at[place], x.at[place], load_sems.at[seg]))
+        whole = [
+            pltpu.make_async_copy(refs["counts_hbm"], vectors.at[0], load_sems.at[segs]),
+            pltpu.make_async_copy(refs["alive_hbm"], vectors.at[1], load_sems.at[segs + 1]),
+        ]
+        stretches = [
+            ([fetch(0), *loads[:early], *whole], [(0, slice(0, early * chans))]),
+            ([*loads[early:], fetch(1)], [(0, slice(early * chans, total)), (1, rows)]),
+        ]
+    if (stop - head) % 2:
+        stretches.append(([fetch(head)], [(head, rows)]))
+        head += 1
+    for tile in range(head, stop, 2):
+        stretches.append(([fetch(tile), fetch(tile + 1)], [(tile, rows), (tile + 1, rows)]))
+    stretches.append(([fetch(tile) for tile in range(stop, further)], []))
+    for copy in stretches[0][0]:
+        copy.start()
     row = lax.broadcasted_iota(jnp.int32, (3 * TILE, TILE), 0)
     column = lax.broadcasted_iota(jnp.int32, (3 * TILE, TILE), 1)
     band[...] = (jnp.abs(row - TILE - column) <= HALF).astype(jnp.float32).astype(jnp.bfloat16)
@@ -131,16 +147,11 @@
 
     if first:
         limits()
-    for index, stretch in enumerate(stretches):
-        later = stretches[index + 1] if index + 1 < len(stretches) else range(stop, further)
-        for tile in later:
-            fetch(tile).start()
-        for tile in stretch:
-            if tile >= had:
-                fetch(tile).wait()
-        if not first and index == 0:
-            for load in loads:
-                load.wait()
+    for index, (copies, products) in enumerate(stretches[:-1]):
+        for copy in stretches[index + 1][0]:
+            copy.start()
+        for copy in copies:
+            copy.wait()
         if not first and index == 0:
             counts[0:1] = jnp.where(vectors[1] > 0, vectors[0], 0).astype(jnp.float32)
             counts[1:2] = vectors[0].astype(jnp.float32)
@@ -149,12 +160,12 @@
             for ref in (one_ref, two_ref):
                 for lane in range(0, ref.shape[1], chans):
                     ref[segs * half :, lane : lane + chans] = row
-        for tile in stretch:
-            store(tile)
+        for product in products:
+            store(*product)
     for tile in range(max(first - 1, 0), stop - 1):
         finish(tile)
-    for tile in range(stop, further):
-        fetch(tile).wait()
+    for copy in stretches[-1][0]:
+        copy.wait()
 
 
 def held(arrays):
@@ -175,9 +186,9 @@
         "power": pltpu.VMEM((made, total, TILE), jnp.bfloat16),
         "band": pltpu.VMEM((3 * TILE, TILE), jnp.bfloat16),
         "eff": pltpu.VMEM((chans, chans), jnp.float32),
-        "sems": pltpu.SemaphoreType.DMA((further - first,)),
+        "sems": pltpu.SemaphoreType.DMA((max(further, stop) - first,)),
     }
-    lacking = made - (given["table_in"].shape[0] if first else 0)
+    lacking = made - (given["table_in"].shape[0] if "table_in" in given else 0)
     if lacking:
         scratch["buffers"] = pltpu.VMEM((lacking, length, 2 * TILE), jnp.bfloat16)
     if not first:
@@ -188,6 +199,7 @@
     if stop <= tiles:
         handed["spectrum_out"] = pltpu.VMEM((total, 2 * TILE), jnp.float32)
         handed["power_out"] = pltpu.VMEM((2, total, TILE), jnp.bfloat16)
+    if further > stop:
         handed["table_out"] = pltpu.VMEM((further - stop, length, 2 * TILE), jnp.bfloat16)
     if first:
         operands = held(given.values())

time: 60.4 us -> 59.2 us (0.980)
  Pallas kernels: 38.4 us -> 37 us
    pallas_call x3, Pallas kernels: 26.3 us -> 25.1 us  [whiten(): pl.pallas_call(functools.partial(whiten_kernel, plan, names), out_shape=[...]
where the time goes in v8:
time: 59.2 us; the launch traced here: 58.4 us
  Pallas kernels  37 us (62%)
  starting transfers between devices  11.5 us (19%)
  waiting for transfers between devices  8.79 us (15%)
  local copies, waits for them, and re-layouts  0.88 us (1%)
    pallas_call x3, Pallas kernels, whiten(): pl.pallas_call(functools.partial(whiten_kernel, plan, names), out_shape=[...  25.1 us
    pallas_call x3, Pallas kernels, correlate(): pl.pallas_call(functools.partial(correlate_kernel, plan), out_shape=out_s...  11.9 us
    ppermute x6, starting transfers between devices, swap(): return lax.ppermute(block, ('chan', 'freq'), route)  6.97 us
    ppermute x6, waiting for transfers between devices, swap(): return lax.ppermute(block, ('chan', 'freq'), route)  3.08 us
    ppermute x1, starting transfers between devices, shards(): near = lax.ppermute(back, ('chan', 'seg', 'freq'), route_near)  2.7 us
    ppermute x1, waiting for transfers between devices, shards(): near = lax.ppermute(back, ('chan', 'seg', 'freq'), route_near)  2.01 us
    ppermute x1, waiting for transfers between devices, shards(): other = lax.ppermute(other, 'seg', [(0, 1), (1, 0)])  1.99 us
    ppermute x1, starting transfers between devices, shards(): other = lax.ppermute(other, 'seg', [(0, 1), (1, 0)])  1.7 us
  transfers between devices with their start and end apart: 10, of which 5 were waited for; matrix products, arithmetic and copies ran while one was open for 0% of the time, Pallas kernels for 38%

profile of v8, /device:TPU:0, one launch (start us, length us, event | category | flops | bytes accessed | tf_op | source)
XLA Modules:
  0.0 58.4 jit_solution(7178283229774638863)
XLA Ops:
  0.0 11.3 %whiten.3 = (bf16[336,768]{1,0:T(8,128)(2,1)S(1)}, bf16[336,768]{1,0:T(8,128)(2,1)S(1)}, bf16[640,4096]{1,0:T(8,128)(2,1)S(1)}, f32[2,128]{1,0:T(2,128)S(1)}, f3...) custom-call(bf16[2,10,4096,256]{3,2,1,0:T(8,128)(2,1)} %constant.19.clone.refs_0_.table_hbm, ...), custom_call_target="tpu_custom_call" | custom-call | flops 5368709120 | bytes 13631488 | tf_op jit(solution)/shard_map/whiten/pallas_call | solution.py:209
  11.3 3.1 %collective-permute-start.4 = (bf16[336,768]{1,0:T(8,128)(2,1)S(1)}, bf16[336,768]{1,0:T(8,128)(2,1)S(1)}, u32[]{:S(2)}, u32[]{:S(2)}) collective-permute-start(bf16[336,768]{1,0:T(8,128)(2,1)S(1)} %get-tuple-element.35.one_ref), channel_id=1, source_target_pairs={{0,4},{1,5},{4,0},{5,1},{8,12},{9,13},{12,8},{13,9},{2,6},{3,7},{6... | collective-permute-start | bytes 1548296 | tf_op jit(solution)/shard_map/ppermute | solution.py:391
  14.4 7.7 %whiten.4 = (bf16[320,768]{1,0:T(8,128)(2,1)S(1)}, bf16[320,768]{1,0:T(8,128)(2,1)S(1)}, f32[640,256]{1,0:T(8,128)S(1)}, bf16[2,640,128]{2,1,0:T(8,128)(2,1)S(1)}, bf16[1,4096,256]{2,1,0:T(8,128)(2,1)S(1)}) custom-call(bf16[2,10,4096,256]{3,2,1,0:T(8,128)(2,1)} %constant.19.clone.refs_0_.table_hbm, bf16[640,4096]{1,0:T(8,128)(2,1)S(1)} %get-tuple-element.23.refs_1_, ...), custom_call_target="tpu_custom_call" | custom-call | flops 4026531840 | bytes 11534336 | tf_op jit(solution)/shard_map/whiten/pallas_call | solution.py:209
  22.1 3.2 %collective-permute-start.2 = (bf16[320,768]{1,0:T(8,128)(2,1)S(1)}, bf16[320,768]{1,0:T(8,128)(2,1)S(1)}, u32[]{:S(2)}, u32[]{:S(2)}) collective-permute-start(bf16[320,768]{1,0:T(8,128)(2,1)S(1)} %get-tuple-element.33.one_ref), channel_id=1, source_target_pairs={{0,4},{1,5},{4,0},{5,1},{8,12},{9,13},{12,8},{13,9},{2,6},{3,7},{6... | collective-permute-start | bytes 1474568 | tf_op jit(solution)/shard_map/ppermute | solution.py:391
  25.3 6.1 %whiten.5 = (bf16[320,512]{1,0:T(8,128)(2,1)S(1)}, bf16[320,512]{1,0:T(8,128)(2,1)S(1)}) custom-call(bf16[2,10,4096,256]{3,2,1,0:T(8,128)(2,1)} %constant.19.clone.refs_0_.table_hbm, bf16[640,4096]{1,0:T(8,128)(2,1)S(1)} %get-tuple-element.23.refs_1_, f32[2,128]{1,0:T(2,128)S(1)} %get-tuple-element.24.refs_2_.refs_0_, ...), custom_call_target="tpu_custom_call" | custom-call | flops 2684354560 | bytes 9437184 | tf_op jit(solution)/shard_map/whiten/pallas_call | solution.py:209
  31.4 0.5 collective-permute-start
  31.9 0.0 collective-permute-done.4.got_one_ref
  31.9 0.1 collective-permute-start.1
  32.1 0.0 collective-permute-done.5.got_two_ref
  32.1 4.3 %correlate.3 = (f32[512,512]{1,0:T(8,128)S(1)}, f32[4,128,256]{2,1,0:T(8,128)S(1)}) custom-call(s32[4]{0:T(128)S(1)} %copy-done, bf16[336,768]{1,0:T(8,128)(2,1)S(1)} %get-tuple-element.35.one_ref, bf16[336,768]{1,0:T(8,128)(2,1)S(1)} %get-tuple-element.36.two_ref, bf16[336,768]{1,0:T(8,128)(2,1)S(1)} %collective-permute-done.4.got_one_ref, ...), custom_call_target="tpu_custom_call" | custom-call | flops 1409286144 | bytes 1966080 | tf_op jit(solution)/shard_map/correlate/pallas_call | solution.py:362
  36.4 1.0 %collective-permute-done.2.got_one_ref = bf16[320,768]{1,0:T(8,128)(2,1)S(1)} collective-permute-done((bf16[320,768]{1,0:T(8,128)(2,1)S(1)}, bf16[320,768]{1,0:T(8,128)(2,1)S(1)}, u32[]{:S(2)}, u32[]{:S(2)}) %collective-permute-start.2) | collective-permute-done | bytes 491552 | tf_op jit(solution)/shard_map/ppermute | solution.py:391
  37.4 0.0 collective-permute-done.3.got_two_ref
  37.4 4.2 %correlate.4.refs_0_ = f32[512,512]{1,0:T(8,128)S(1)} custom-call(s32[4]{0:T(128)S(1)} %copy-done, bf16[320,768]{1,0:T(8,128)(2,1)S(1)} %get-tuple-element.33.one_ref, bf16[320,768]{1,0:T(8,128)(2,1)S(1)} %get-tuple-element.34.two_ref, bf16[320,768]{1,0:T(8,128)(2,1)S(1)} %collective-permute-done.2.got_one_ref, ...), custom_call_target="tpu_custom_call" | custom-call | flops 1409286144 | bytes 1966080 | tf_op jit(solution)/shard_map/correlate/pallas_call | solution.py:362
  41.7 2.1 %collective-permute-done.got_one_ref = bf16[320,512]{1,0:T(8,128)(2,1)S(1)} collective-permute-done((bf16[320,512]{1,0:T(8,128)(2,1)S(1)}, bf16[320,512]{1,0:T(8,128)(2,1)S(1)}, u32[]{:S(2)}, u32[]{:S(2)}) %collective-permute-start) | collective-permute-done | bytes 327712 | tf_op jit(solution)/shard_map/ppermute | solution.py:391
  43.7 3.4 %correlate.5 = (f32[4,192,256]{2,1,0:T(8,128)S(1)}, bf16[4,192,256]{2,1,0:T(8,128)(2,1)S(1)}) custom-call(s32[4]{0:T(128)S(1)} %copy-done, bf16[320,512]{1,0:T(8,128)(2,1)S(1)} %get-tuple-element.31.one_ref, bf16[320,512]{1,0:T(8,128)(2,1)S(1)} %get-tuple-element.32.two_ref, bf16[320,512]{1,0:T(8,128)(2,1)S(1)} %collective-permute-done.got_one_ref, ...), custom_call_target="tpu_custom_call" | custom-call | flops 939524096 | bytes 1310720 | tf_op jit(solution)/shard_map/correlate/pallas_call | solution.py:362
  47.1 0.1 collective-permute-start.6
  47.2 1.7 %collective-permute-done.6 = bf16[4,192,256]{2,1,0:T(8,128)(2,1)S(1)} collective-permute-done((bf16[4,192,256]{2,1,0:T(8,128)(2,1)S(1)}, bf16[4,192,256]{2,1,0:T(8,128)(2,1)S(1)}, u32[]{:S(2)}, u32[]{:S(2)}) %collective-permute-start.6) | collective-permute-done | bytes 393248 | tf_op jit(solution)/shard_map/ppermute | solution.py:456
  48.9 0.1 convert_add_fusion
  49.0 1.7 %collective-permute-start.7 = (bf16[4,64,256]{2,1,0:T(8,128)(2,1)S(1)}, bf16[4,64,256]{2,1,0:T(8,128)(2,1)S(1)}, u32[]{:S(2)}, u32[]{:S(2)}) collective-permute-start(bf16[4,64,256]{2,1,0:T(8,128)(2,1)S(1)} %get-tuple-element.41), channel_id=1, source_target_pairs={{0,2},{2,0},{1,3},{3,1},{4,6},{6,4},{5,7},{7,5},{8,10},{10,8},{9,1... | collective-permute-start | bytes 393224 | tf_op jit(solution)/shard_map/ppermute | solution.py:462
  50.7 2.7 %collective-permute-start.8 = (bf16[4,64,256]{2,1,0:T(8,128)(2,1)S(1)}, bf16[4,64,256]{2,1,0:T(8,128)(2,1)S(1)}, u32[]{:S(2)}, u32[]{:S(2)}) collective-permute-start(bf16[4,64,256]{2,1,0:T(8,128)(2,1)S(1)} %get-tuple-element.42), channel_id=1, source_target_pairs={{2,0},{3,1},{0,4},{1,5},{6,2},{7,3},{4,8},{5,9},{10,6},{11,7},{8,1... | collective-permute-start | bytes 393224 | tf_op jit(solution)/shard_map/ppermute | solution.py:464
  53.5 2.0 %collective-permute-done.7 = bf16[4,64,256]{2,1,0:T(8,128)(2,1)S(1)} collective-permute-done((bf16[4,64,256]{2,1,0:T(8,128)(2,1)S(1)}, bf16[4,64,256]{2,1,0:T(8,128)(2,1)S(1)}, u32[]{:S(2)}, u32[]{:S(2)}) %collective-permute-start.7) | collective-permute-done | bytes 131104 | tf_op jit(solution)/shard_map/ppermute | solution.py:462
  55.4 2.0 %collective-permute-done.8 = bf16[4,64,256]{2,1,0:T(8,128)(2,1)S(1)} collective-permute-done((bf16[4,64,256]{2,1,0:T(8,128)(2,1)S(1)}, bf16[4,64,256]{2,1,0:T(8,128)(2,1)S(1)}, u32[]{:S(2)}, u32[]{:S(2)}) %collective-permute-start.8) | collective-permute-done | bytes 131104 | tf_op jit(solution)/shard_map/ppermute | solution.py:464
  57.5 0.1 multiply_bitcast_fusion
  57.6 0.9 %copy.6 = f32[64,4,256]{2,1,0:T(4,128)} copy(f32[64,4,256]{2,0,1:T(8,128)S(1)} %multiply_bitcast_fusion) | data formatting | bytes 524288 | tf_op jit(solution)/shard_map/transpose | solution.py:473
  (8 shorter events, 0.1 us)
Async XLA Ops:
  11.3 20.6 %collective-permute-start.4 = (bf16[336,768]{1,0:T(8,128)(2,1)S(1)}, bf16[336,768]{1,0:T(8,128)(2,1)S(1)}, u32[]{:S(2)}, u32[]{:S(2)}) collective-permute-start(bf16[336,768]{1,0:T(8,128)(2,1)S(1)} %get-tuple-element.35.one_ref), channel_id=1, source_target_pairs={{0,4},{1,5},{4,0},{5,1},{8,12},{9,13},{12,8},{13,9},{2,6},{3,7},{6... | collective-permute-start | bytes 1548296 | tf_op jit(solution)/shard_map/ppermute | solution.py:391
  14.4 17.7 %collective-permute-start.5 = (bf16[336,768]{1,0:T(8,128)(2,1)S(1)}, bf16[336,768]{1,0:T(8,128)(2,1)S(1)}, u32[]{:S(2)}, u32[]{:S(2)}) collective-permute-start(bf16[336,768]{1,0:T(8,128)(2,1)S(1)} %get-tuple-element.36.two_ref), channel_id=1, source_target_pairs={{0,1},{1,0},{4,8},{5,9},{8,4},{9,5},{12,13},{13,12},{2,3},{3,2},{6... | collective-permute-start | bytes 1548296 | tf_op jit(solution)/shard_map/ppermute | solution.py:391
  22.1 15.3 %collective-permute-start.2 = (bf16[320,768]{1,0:T(8,128)(2,1)S(1)}, bf16[320,768]{1,0:T(8,128)(2,1)S(1)}, u32[]{:S(2)}, u32[]{:S(2)}) collective-permute-start(bf16[320,768]{1,0:T(8,128)(2,1)S(1)} %get-tuple-element.33.one_ref), channel_id=1, source_target_pairs={{0,4},{1,5},{4,0},{5,1},{8,12},{9,13},{12,8},{13,9},{2,6},{3,7},{6... | collective-permute-start | bytes 1474568 | tf_op jit(solution)/shard_map/ppermute | solution.py:391
  25.3 12.1 %collective-permute-start.3 = (bf16[320,768]{1,0:T(8,128)(2,1)S(1)}, bf16[320,768]{1,0:T(8,128)(2,1)S(1)}, u32[]{:S(2)}, u32[]{:S(2)}) collective-permute-start(bf16[320,768]{1,0:T(8,128)(2,1)S(1)} %get-tuple-element.34.two_ref), channel_id=1, source_target_pairs={{0,1},{1,0},{4,8},{5,9},{8,4},{9,5},{12,13},{13,12},{2,3},{3,2},{6... | collective-permute-start | bytes 1474568 | tf_op jit(solution)/shard_map/ppermute | solution.py:391
  25.3 6.8 %copy-start = (s32[4]{0:T(128)S(1)}, s32[4]{0:T(128)}, u32[]{:S(2)}) copy-start(s32[4]{0:T(128)} %offsets.5) | copy-start | bytes 52
  31.4 12.3 %collective-permute-start = (bf16[320,512]{1,0:T(8,128)(2,1)S(1)}, bf16[320,512]{1,0:T(8,128)(2,1)S(1)}, u32[]{:S(2)}, u32[]{:S(2)}) collective-permute-start(bf16[320,512]{1,0:T(8,128)(2,1)S(1)} %get-tuple-element.31.one_ref), channel_id=1, source_target_pairs={{0,4},{1,5},{4,0},{5,1},{8,12},{9,13},{12,8},{13,9},{2,6},{3,7},{6... | collective-permute-start | bytes 983048 | tf_op jit(solution)/shard_map/ppermute | solution.py:391
  31.9 11.8 %collective-permute-start.1 = (bf16[320,512]{1,0:T(8,128)(2,1)S(1)}, bf16[320,512]{1,0:T(8,128)(2,1)S(1)}, u32[]{:S(2)}, u32[]{:S(2)}) collective-permute-start(bf16[320,512]{1,0:T(8,128)(2,1)S(1)} %get-tuple-element.32.two_ref), channel_id=1, source_target_pairs={{0,1},{1,0},{4,8},{5,9},{8,4},{9,5},{12,13},{13,12},{2,3},{3,2},{6... | collective-permute-start | bytes 983048 | tf_op jit(solution)/shard_map/ppermute | solution.py:391
  47.1 1.8 %collective-permute-start.6 = (bf16[4,192,256]{2,1,0:T(8,128)(2,1)S(1)}, bf16[4,192,256]{2,1,0:T(8,128)(2,1)S(1)}, u32[]{:S(2)}, u32[]{:S(2)}) collective-permute-start(bf16[4,192,256]{2,1,0:T(8,128)(2,1)S(1)} %get-tuple-element.39), channel_id=1, source_target_pairs={{0,1},{1,0},{2,3},{3,2},{4,5},{5,4},{6,7},{7,6},{8,9},{9,8},{10,11... | collective-permute-start | bytes 1179656 | tf_op jit(solution)/shard_map/ppermute | solution.py:456
  49.0 6.4 %collective-permute-start.7 = (bf16[4,64,256]{2,1,0:T(8,128)(2,1)S(1)}, bf16[4,64,256]{2,1,0:T(8,128)(2,1)S(1)}, u32[]{:S(2)}, u32[]{:S(2)}) collective-permute-start(bf16[4,64,256]{2,1,0:T(8,128)(2,1)S(1)} %get-tuple-element.41), channel_id=1, source_target_pairs={{0,2},{2,0},{1,3},{3,1},{4,6},{6,4},{5,7},{7,5},{8,10},{10,8},{9,1... | collective-permute-start | bytes 393224 | tf_op jit(solution)/shard_map/ppermute | solution.py:462
  50.7 6.7 %collective-permute-start.8 = (bf16[4,64,256]{2,1,0:T(8,128)(2,1)S(1)}, bf16[4,64,256]{2,1,0:T(8,128)(2,1)S(1)}, u32[]{:S(2)}, u32[]{:S(2)}) collective-permute-start(bf16[4,64,256]{2,1,0:T(8,128)(2,1)S(1)} %get-tuple-element.42), channel_id=1, source_target_pairs={{2,0},{3,1},{0,4},{1,5},{6,2},{7,3},{4,8},{5,9},{10,6},{11,7},{8,1... | collective-permute-start | bytes 393224 | tf_op jit(solution)/shard_map/ppermute | solution.py:464
  53.5 4.0 %collective-permute-start.9 = (bf16[4,64,256]{2,1,0:T(8,128)(2,1)S(1)}, bf16[4,64,256]{2,1,0:T(8,128)(2,1)S(1)}, u32[]{:S(2)}, u32[]{:S(2)}) collective-permute-start(bf16[4,64,256]{2,1,0:T(8,128)(2,1)S(1)} %get-tuple-element.42), channel_id=1, source_target_pairs={{0,1},{1,0},{2,4},{3,5},{4,2},{5,3},{6,8},{7,9},{8,6},{9,7},{10,12... | collective-permute-start | bytes 393224 | tf_op jit(solution)/shard_map/ppermute | solution.py:465

commit v9 on v8

--- a/solution.py
+++ b/solution.py
@@ -17,7 +17,7 @@
 EPSILON = 1e-06
 MIB = 1 << 20
 EXTRA = 16
-LAG_TILES = 4
+LAG_TILES = 1
 GROUPS = (4, 7, 9)
 AHEAD = (5, 8, 9)
 

time: 59.2 us -> 59.1 us (level)
  transfers between devices with their start and end apart: 10 -> 10, of which waited for: 5 -> 5; matrix products, arithmetic and copies ran while one was open for 0% -> 0% of each run, Pallas kernels for 38% -> 37%
where the time goes in v9:
time: 59.1 us; the launch traced here: 58.4 us
  Pallas kernels  36.5 us (62%)
  starting transfers between devices  11.5 us (19%)
  waiting for transfers between devices  9.22 us (16%)
  local copies, waits for them, and re-layouts  0.88 us (1%)
    pallas_call x3, Pallas kernels, whiten(): pl.pallas_call(functools.partial(whiten_kernel, plan, names), out_shape=[...  25.1 us
    pallas_call x3, Pallas kernels, correlate(): pl.pallas_call(functools.partial(correlate_kernel, plan), out_shape=out_s...  11.4 us
    ppermute x6, starting transfers between devices, swap(): return lax.ppermute(block, ('chan', 'freq'), route)  6.97 us
    ppermute x6, waiting for transfers between devices, swap(): return lax.ppermute(block, ('chan', 'freq'), route)  3.53 us
    ppermute x1, starting transfers between devices, shards(): near = lax.ppermute(back, ('chan', 'seg', 'freq'), route_near)  2.71 us
    ppermute x1, waiting for transfers between devices, shards(): near = lax.ppermute(back, ('chan', 'seg', 'freq'), route_near)  2.01 us
    ppermute x1, waiting for transfers between devices, shards(): other = lax.ppermute(other, 'seg', [(0, 1), (1, 0)])  1.98 us
    ppermute x1, starting transfers between devices, shards(): other = lax.ppermute(other, 'seg', [(0, 1), (1, 0)])  1.72 us
  transfers between devices with their start and end apart: 10, of which 5 were waited for; matrix products, arithmetic and copies ran while one was open for 0% of the time, Pallas kernels for 37%

profile of v9, /device:TPU:0, one launch (start us, length us, event | category | flops | bytes accessed | tf_op | source)
XLA Modules:
  0.0 58.4 jit_solution(11765888441505392758)
XLA Ops:
  0.0 11.3 %whiten.3 = (bf16[336,768]{1,0:T(8,128)(2,1)S(1)}, bf16[336,768]{1,0:T(8,128)(2,1)S(1)}, bf16[640,4096]{1,0:T(8,128)(2,1)S(1)}, f32[2,128]{1,0:T(2,128)S(1)}, f3...) custom-call(bf16[2,10,4096,256]{3,2,1,0:T(8,128)(2,1)} %constant.19.clone.refs_0_.table_hbm, ...), custom_call_target="tpu_custom_call" | custom-call | flops 5368709120 | bytes 13631488 | tf_op jit(solution)/shard_map/whiten/pallas_call | solution.py:209
  11.3 3.1 %collective-permute-start.4 = (bf16[336,768]{1,0:T(8,128)(2,1)S(1)}, bf16[336,768]{1,0:T(8,128)(2,1)S(1)}, u32[]{:S(2)}, u32[]{:S(2)}) collective-permute-start(bf16[336,768]{1,0:T(8,128)(2,1)S(1)} %get-tuple-element.35.one_ref), channel_id=1, source_target_pairs={{0,4},{1,5},{4,0},{5,1},{8,12},{9,13},{12,8},{13,9},{2,6},{3,7},{6... | collective-permute-start | bytes 1548296 | tf_op jit(solution)/shard_map/ppermute | solution.py:391
  14.4 7.7 %whiten.4 = (bf16[320,768]{1,0:T(8,128)(2,1)S(1)}, bf16[320,768]{1,0:T(8,128)(2,1)S(1)}, f32[640,256]{1,0:T(8,128)S(1)}, bf16[2,640,128]{2,1,0:T(8,128)(2,1)S(1)}, bf16[1,4096,256]{2,1,0:T(8,128)(2,1)S(1)}) custom-call(bf16[2,10,4096,256]{3,2,1,0:T(8,128)(2,1)} %constant.19.clone.refs_0_.table_hbm, bf16[640,4096]{1,0:T(8,128)(2,1)S(1)} %get-tuple-element.23.refs_1_, ...), custom_call_target="tpu_custom_call" | custom-call | flops 4026531840 | bytes 11534336 | tf_op jit(solution)/shard_map/whiten/pallas_call | solution.py:209
  22.1 3.2 %collective-permute-start.2 = (bf16[320,768]{1,0:T(8,128)(2,1)S(1)}, bf16[320,768]{1,0:T(8,128)(2,1)S(1)}, u32[]{:S(2)}, u32[]{:S(2)}) collective-permute-start(bf16[320,768]{1,0:T(8,128)(2,1)S(1)} %get-tuple-element.33.one_ref), channel_id=1, source_target_pairs={{0,4},{1,5},{4,0},{5,1},{8,12},{9,13},{12,8},{13,9},{2,6},{3,7},{6... | collective-permute-start | bytes 1474568 | tf_op jit(solution)/shard_map/ppermute | solution.py:391
  25.3 6.1 %whiten.5 = (bf16[320,512]{1,0:T(8,128)(2,1)S(1)}, bf16[320,512]{1,0:T(8,128)(2,1)S(1)}) custom-call(bf16[2,10,4096,256]{3,2,1,0:T(8,128)(2,1)} %constant.19.clone.refs_0_.table_hbm, bf16[640,4096]{1,0:T(8,128)(2,1)S(1)} %get-tuple-element.23.refs_1_, f32[2,128]{1,0:T(2,128)S(1)} %get-tuple-element.24.refs_2_.refs_0_, ...), custom_call_target="tpu_custom_call" | custom-call | flops 2684354560 | bytes 9437184 | tf_op jit(solution)/shard_map/whiten/pallas_call | solution.py:209
  31.4 0.5 collective-permute-start
  31.9 0.0 collective-permute-done.4.got_one_ref
  31.9 0.1 collective-permute-start.1
  32.1 0.0 collective-permute-done.5.got_two_ref
  32.1 4.1 %correlate.3 = (f32[512,512]{1,0:T(8,128)S(1)}, f32[4,128,256]{2,1,0:T(8,128)S(1)}) custom-call(s32[4]{0:T(128)S(1)} %copy-done, bf16[336,768]{1,0:T(8,128)(2,1)S(1)} %get-tuple-element.35.one_ref, bf16[336,768]{1,0:T(8,128)(2,1)S(1)} %get-tuple-element.36.two_ref, bf16[336,768]{1,0:T(8,128)(2,1)S(1)} %collective-permute-done.4.got_one_ref, ...), custom_call_target="tpu_custom_call" | custom-call | flops 1409286144 | bytes 1966080 | tf_op jit(solution)/shard_map/correlate/pallas_call | solution.py:362
  36.2 1.3 %collective-permute-done.2.got_one_ref = bf16[320,768]{1,0:T(8,128)(2,1)S(1)} collective-permute-done((bf16[320,768]{1,0:T(8,128)(2,1)S(1)}, bf16[320,768]{1,0:T(8,128)(2,1)S(1)}, u32[]{:S(2)}, u32[]{:S(2)}) %collective-permute-start.2) | collective-permute-done | bytes 491552 | tf_op jit(solution)/shard_map/ppermute | solution.py:391
  37.4 0.0 collective-permute-done.3.got_two_ref
  37.4 4.0 %correlate.4.refs_0_ = f32[512,512]{1,0:T(8,128)S(1)} custom-call(s32[4]{0:T(128)S(1)} %copy-done, bf16[320,768]{1,0:T(8,128)(2,1)S(1)} %get-tuple-element.33.one_ref, bf16[320,768]{1,0:T(8,128)(2,1)S(1)} %get-tuple-element.34.two_ref, bf16[320,768]{1,0:T(8,128)(2,1)S(1)} %collective-permute-done.2.got_one_ref, ...), custom_call_target="tpu_custom_call" | custom-call | flops 1409286144 | bytes 1966080 | tf_op jit(solution)/shard_map/correlate/pallas_call | solution.py:362
  41.5 2.2 %collective-permute-done.got_one_ref = bf16[320,512]{1,0:T(8,128)(2,1)S(1)} collective-permute-done((bf16[320,512]{1,0:T(8,128)(2,1)S(1)}, bf16[320,512]{1,0:T(8,128)(2,1)S(1)}, u32[]{:S(2)}, u32[]{:S(2)}) %collective-permute-start) | collective-permute-done | bytes 327712 | tf_op jit(solution)/shard_map/ppermute | solution.py:391
  43.7 3.3 %correlate.5 = (f32[4,192,256]{2,1,0:T(8,128)S(1)}, bf16[4,192,256]{2,1,0:T(8,128)(2,1)S(1)}) custom-call(s32[4]{0:T(128)S(1)} %copy-done, bf16[320,512]{1,0:T(8,128)(2,1)S(1)} %get-tuple-element.31.one_ref, bf16[320,512]{1,0:T(8,128)(2,1)S(1)} %get-tuple-element.32.two_ref, bf16[320,512]{1,0:T(8,128)(2,1)S(1)} %collective-permute-done.got_one_ref, ...), custom_call_target="tpu_custom_call" | custom-call | flops 939524096 | bytes 1310720 | tf_op jit(solution)/shard_map/correlate/pallas_call | solution.py:362
  47.0 0.1 collective-permute-start.6
  47.1 1.7 %collective-permute-done.6 = bf16[4,192,256]{2,1,0:T(8,128)(2,1)S(1)} collective-permute-done((bf16[4,192,256]{2,1,0:T(8,128)(2,1)S(1)}, bf16[4,192,256]{2,1,0:T(8,128)(2,1)S(1)}, u32[]{:S(2)}, u32[]{:S(2)}) %collective-permute-start.6) | collective-permute-done | bytes 393248 | tf_op jit(solution)/shard_map/ppermute | solution.py:456
  48.8 0.1 convert_add_fusion
  49.0 1.7 %collective-permute-start.7 = (bf16[4,64,256]{2,1,0:T(8,128)(2,1)S(1)}, bf16[4,64,256]{2,1,0:T(8,128)(2,1)S(1)}, u32[]{:S(2)}, u32[]{:S(2)}) collective-permute-start(bf16[4,64,256]{2,1,0:T(8,128)(2,1)S(1)} %get-tuple-element.41), channel_id=1, source_target_pairs={{0,2},{2,0},{1,3},{3,1},{4,6},{6,4},{5,7},{7,5},{8,10},{10,8},{9,1... | collective-permute-start | bytes 393224 | tf_op jit(solution)/shard_map/ppermute | solution.py:462
  50.7 2.7 %collective-permute-start.8 = (bf16[4,64,256]{2,1,0:T(8,128)(2,1)S(1)}, bf16[4,64,256]{2,1,0:T(8,128)(2,1)S(1)}, u32[]{:S(2)}, u32[]{:S(2)}) collective-permute-start(bf16[4,64,256]{2,1,0:T(8,128)(2,1)S(1)} %get-tuple-element.42), channel_id=1, source_target_pairs={{2,0},{3,1},{0,4},{1,5},{6,2},{7,3},{4,8},{5,9},{10,6},{11,7},{8,1... | collective-permute-start | bytes 393224 | tf_op jit(solution)/shard_map/ppermute | solution.py:464
  53.4 2.0 %collective-permute-done.7 = bf16[4,64,256]{2,1,0:T(8,128)(2,1)S(1)} collective-permute-done((bf16[4,64,256]{2,1,0:T(8,128)(2,1)S(1)}, bf16[4,64,256]{2,1,0:T(8,128)(2,1)S(1)}, u32[]{:S(2)}, u32[]{:S(2)}) %collective-permute-start.7) | collective-permute-done | bytes 131104 | tf_op jit(solution)/shard_map/ppermute | solution.py:462
  55.4 2.0 %collective-permute-done.8 = bf16[4,64,256]{2,1,0:T(8,128)(2,1)S(1)} collective-permute-done((bf16[4,64,256]{2,1,0:T(8,128)(2,1)S(1)}, bf16[4,64,256]{2,1,0:T(8,128)(2,1)S(1)}, u32[]{:S(2)}, u32[]{:S(2)}) %collective-permute-start.8) | collective-permute-done | bytes 131104 | tf_op jit(solution)/shard_map/ppermute | solution.py:464
  57.4 0.1 multiply_bitcast_fusion
  57.5 0.9 %copy.6 = f32[64,4,256]{2,1,0:T(4,128)} copy(f32[64,4,256]{2,0,1:T(8,128)S(1)} %multiply_bitcast_fusion) | data formatting | bytes 524288 | tf_op jit(solution)/shard_map/transpose | solution.py:473
  (8 shorter events, 0.1 us)
Async XLA Ops:
  11.3 20.6 %collective-permute-start.4 = (bf16[336,768]{1,0:T(8,128)(2,1)S(1)}, bf16[336,768]{1,0:T(8,128)(2,1)S(1)}, u32[]{:S(2)}, u32[]{:S(2)}) collective-permute-start(bf16[336,768]{1,0:T(8,128)(2,1)S(1)} %get-tuple-element.35.one_ref), channel_id=1, source_target_pairs={{0,4},{1,5},{4,0},{5,1},{8,12},{9,13},{12,8},{13,9},{2,6},{3,7},{6... | collective-permute-start | bytes 1548296 | tf_op jit(solution)/shard_map/ppermute | solution.py:391
  14.4 17.7 %collective-permute-start.5 = (bf16[336,768]{1,0:T(8,128)(2,1)S(1)}, bf16[336,768]{1,0:T(8,128)(2,1)S(1)}, u32[]{:S(2)}, u32[]{:S(2)}) collective-permute-start(bf16[336,768]{1,0:T(8,128)(2,1)S(1)} %get-tuple-element.36.two_ref), channel_id=1, source_target_pairs={{0,1},{1,0},{4,8},{5,9},{8,4},{9,5},{12,13},{13,12},{2,3},{3,2},{6... | collective-permute-start | bytes 1548296 | tf_op jit(solution)/shard_map/ppermute | solution.py:391
  22.1 15.3 %collective-permute-start.2 = (bf16[320,768]{1,0:T(8,128)(2,1)S(1)}, bf16[320,768]{1,0:T(8,128)(2,1)S(1)}, u32[]{:S(2)}, u32[]{:S(2)}) collective-permute-start(bf16[320,768]{1,0:T(8,128)(2,1)S(1)} %get-tuple-element.33.one_ref), channel_id=1, source_target_pairs={{0,4},{1,5},{4,0},{5,1},{8,12},{9,13},{12,8},{13,9},{2,6},{3,7},{6... | collective-permute-start | bytes 1474568 | tf_op jit(solution)/shard_map/ppermute | solution.py:391
  25.3 12.1 %collective-permute-start.3 = (bf16[320,768]{1,0:T(8,128)(2,1)S(1)}, bf16[320,768]{1,0:T(8,128)(2,1)S(1)}, u32[]{:S(2)}, u32[]{:S(2)}) collective-permute-start(bf16[320,768]{1,0:T(8,128)(2,1)S(1)} %get-tuple-element.34.two_ref), channel_id=1, source_target_pairs={{0,1},{1,0},{4,8},{5,9},{8,4},{9,5},{12,13},{13,12},{2,3},{3,2},{6... | collective-permute-start | bytes 1474568 | tf_op jit(solution)/shard_map/ppermute | solution.py:391
  25.3 6.8 %copy-start = (s32[4]{0:T(128)S(1)}, s32[4]{0:T(128)}, u32[]{:S(2)}) copy-start(s32[4]{0:T(128)} %offsets.5) | copy-start | bytes 52
  31.4 12.3 %collective-permute-start = (bf16[320,512]{1,0:T(8,128)(2,1)S(1)}, bf16[320,512]{1,0:T(8,128)(2,1)S(1)}, u32[]{:S(2)}, u32[]{:S(2)}) collective-permute-start(bf16[320,512]{1,0:T(8,128)(2,1)S(1)} %get-tuple-element.31.one_ref), channel_id=1, source_target_pairs={{0,4},{1,5},{4,0},{5,1},{8,12},{9,13},{12,8},{13,9},{2,6},{3,7},{6... | collective-permute-start | bytes 983048 | tf_op jit(solution)/shard_map/ppermute | solution.py:391
  31.9 11.8 %collective-permute-start.1 = (bf16[320,512]{1,0:T(8,128)(2,1)S(1)}, bf16[320,512]{1,0:T(8,128)(2,1)S(1)}, u32[]{:S(2)}, u32[]{:S(2)}) collective-permute-start(bf16[320,512]{1,0:T(8,128)(2,1)S(1)} %get-tuple-element.32.two_ref), channel_id=1, source_target_pairs={{0,1},{1,0},{4,8},{5,9},{8,4},{9,5},{12,13},{13,12},{2,3},{3,2},{6... | collective-permute-start | bytes 983048 | tf_op jit(solution)/shard_map/ppermute | solution.py:391
  47.0 1.8 %collective-permute-start.6 = (bf16[4,192,256]{2,1,0:T(8,128)(2,1)S(1)}, bf16[4,192,256]{2,1,0:T(8,128)(2,1)S(1)}, u32[]{:S(2)}, u32[]{:S(2)}) collective-permute-start(bf16[4,192,256]{2,1,0:T(8,128)(2,1)S(1)} %get-tuple-element.39), channel_id=1, source_target_pairs={{0,1},{1,0},{2,3},{3,2},{4,5},{5,4},{6,7},{7,6},{8,9},{9,8},{10,11... | collective-permute-start | bytes 1179656 | tf_op jit(solution)/shard_map/ppermute | solution.py:456
  49.0 6.4 %collective-permute-start.7 = (bf16[4,64,256]{2,1,0:T(8,128)(2,1)S(1)}, bf16[4,64,256]{2,1,0:T(8,128)(2,1)S(1)}, u32[]{:S(2)}, u32[]{:S(2)}) collective-permute-start(bf16[4,64,256]{2,1,0:T(8,128)(2,1)S(1)} %get-tuple-element.41), channel_id=1, source_target_pairs={{0,2},{2,0},{1,3},{3,1},{4,6},{6,4},{5,7},{7,5},{8,10},{10,8},{9,1... | collective-permute-start | bytes 393224 | tf_op jit(solution)/shard_map/ppermute | solution.py:462
  50.7 6.7 %collective-permute-start.8 = (bf16[4,64,256]{2,1,0:T(8,128)(2,1)S(1)}, bf16[4,64,256]{2,1,0:T(8,128)(2,1)S(1)}, u32[]{:S(2)}, u32[]{:S(2)}) collective-permute-start(bf16[4,64,256]{2,1,0:T(8,128)(2,1)S(1)} %get-tuple-element.42), channel_id=1, source_target_pairs={{2,0},{3,1},{0,4},{1,5},{6,2},{7,3},{4,8},{5,9},{10,6},{11,7},{8,1... | collective-permute-start | bytes 393224 | tf_op jit(solution)/shard_map/ppermute | solution.py:464
  53.4 4.0 %collective-permute-start.9 = (bf16[4,64,256]{2,1,0:T(8,128)(2,1)S(1)}, bf16[4,64,256]{2,1,0:T(8,128)(2,1)S(1)}, u32[]{:S(2)}, u32[]{:S(2)}) collective-permute-start(bf16[4,64,256]{2,1,0:T(8,128)(2,1)S(1)} %get-tuple-element.42), channel_id=1, source_target_pairs={{0,1},{1,0},{2,4},{3,5},{4,2},{5,3},{6,8},{7,9},{8,6},{9,7},{10,12... | collective-permute-start | bytes 393224 | tf_op jit(solution)/shard_map/ppermute | solution.py:465
